TPU v7x, 32 devices: a whole 2x2x4 slice. The times are simulated.
32 devices in a mesh: parts: 2 (over x), step: 16 (over z, y, core).
Axes of the slice: x: 2, y: 2, z: 4, core: 2. Of those that a mesh axis runs over, the one named last changes fastest.
Arguments:
- propagators: float32 [32, 1024, 1024], P(('parts', 'step')), parts along dimension 0, may hold values from -1 to 1
- forcing: float32 [32, 1024], P(('parts', 'step')), parts along dimension 0, may hold values from -3 to 3
- starts: float32 [32, 256], P(('parts', 'step')), parts along dimension 0, may hold values from -6 to 6
- directions: float32 [32, 64, 1024], P(('parts', 'step')), parts along dimension 0, may hold values from -6 to 6
Outputs:
- residual: float32 [32, 256], P(('parts', 'step')), parts along dimension 0
- jacobian_rows: float32 [32, 64, 1024], P(('parts', 'step')), parts along dimension 0
There are 2 independent parts, one for each index of `parts`. A program takes and returns all parts, laid end to end along the dimension named above; each array names one. Nothing has to cross between parts.
All inputs are finite; a program needn't handle non-finite values.
Results may differ from a plain program's by a relative error of at most 0.00012.
Values sent between devices are 32-bit elements; how exact they have to be, the bound alone decides.
No kernel may reach another device: no remote copies, remote signals or barrier semaphores. Data moves between devices by JAX's collectives and lax.ppermute only.
A program may use at most 64 MiB of HBM per device.

v0:
```python
import jax
import jax.numpy as jnp
from jax import lax
from jax.sharding import PartitionSpec as P

WIN = 4


def passed_along(shard, axis, by):
    length = lax.axis_size(axis)
    pairs = [(i, i + by) for i in range(length) if 0 <= i + by < length]
    return lax.ppermute(shard, axis, pairs)


def partner(block, axis, stride):
    count = lax.axis_size(axis)
    route = []
    for low in range(count):
        high = low | 1 << stride
        if high != low and high < count:
            route += [(low, high), (high, low)]
    return lax.ppermute(block, axis, route)


def shifted(shard, axis, by):
    length = lax.axis_size(axis)
    return lax.ppermute(shard, axis, [(i, (i + by) % length) for i in range(length)])


def compose(later_mat, later_vec, earlier_mat, earlier_vec):
    joined_mat = jnp.dot(
        later_mat, earlier_mat, precision=lax.Precision.HIGHEST, preferred_element_type=jnp.float32
    )
    joined_vec = (
        jnp.dot(
            later_mat,
            earlier_vec,
            precision=lax.Precision.HIGHEST,
            preferred_element_type=jnp.float32,
        )
        + later_vec
    )
    return (joined_mat, joined_vec)


def local(propagators, forcing, starts, directions):
    matrix = propagators[0]
    vector = forcing[0]
    position = lax.axis_index("step")
    within = position % WIN
    levels = WIN.bit_length() - 1
    slice_len = starts.shape[1]
    for bit_level in range(levels):
        stride = 1 << bit_level
        got_mat, got_vec = passed_along((matrix, vector), "step", stride)
        active = within % (2 * stride) == 2 * stride - 1
        matrix, vector = lax.cond(
            active, lambda: compose(matrix, vector, got_mat, got_vec), lambda: (matrix, vector)
        )
    for bit_level in reversed(range(levels)):
        stride = 1 << bit_level
        got_mat, got_vec = passed_along((matrix, vector), "step", -stride)
        accept_down = within % (2 * stride) == stride - 1
        matrix = jnp.where(accept_down, got_mat, matrix)
        vector = jnp.where(accept_down, got_vec, vector)
    columns = lax.dynamic_slice_in_dim(matrix, within * slice_len, slice_len, 1)
    summed = jnp.dot(
        columns, starts[0], precision=lax.Precision.HIGHEST, preferred_element_type=jnp.float32
    )
    for bit_level in range(levels):
        summed = summed + partner(summed, "step", bit_level)
    end_state = summed + vector
    own_slice = lax.dynamic_slice_in_dim(end_state, within * slice_len, slice_len, 0)
    images = lax.dot_general(
        directions[0],
        matrix,
        (((1,), (1,)), ((), ())),
        precision=lax.Precision.HIGHEST,
        preferred_element_type=jnp.float32,
    )
    came_end, came_images = shifted((own_slice, images), "step", WIN)
    residual = (came_end - starts[0])[None]
    jacobian_rows = (came_images - directions[0])[None]
    return (residual, jacobian_rows)


def solution(mesh):
    return jax.shard_map(
        local,
        mesh=mesh,
        in_specs=(
            P(("parts", "step"), None, None),
            P(("parts", "step"), None),
            P(("parts", "step"), None),
            P(("parts", "step"), None, None),
        ),
        out_specs=(P(("parts", "step"), None), P(("parts", "step"), None, None)),
        check_vma=False,
    )
```

profile of v0, /device:TPU:0, one launch (start us, length us, event | category | flops | bytes accessed | tf_op | source)
XLA Modules:
  0.0 350.3 jit_solution(5259818254241493761)
XLA Ops:
  0.6 0.7 copy.15
  1.3 4.3 %collective-permute-start = (f32[1024,1024]{1,0:T(8,128)}, f32[1024,1024]{1,0:T(8,128)}, u32[]{:S(2)}, u32[]{:S(2)}) collective-permute-start(f32[1024,1024]{1,0:T(8,128)} %bitcast.31), channel_id=1, source_target_pairs={{0,1},{1,2},{2,3},{3,4},{4,5},{5,6},{6,7},{7,8},{8,9},{9,10},{10,1... | collective-permute-start | bytes 12582920 | tf_op jit(solution)/shard_map/ppermute | solution.py:12
  5.6 2.6 collective-permute-start.1
  8.3 2.2 collective-permute-done.1
  10.4 0.3 collective-permute-done
  10.8 4.8 %conditional.2 = (f32[1024,1024]{1,0:T(8,128)}, f32[1024]{0:T(1024)S(1)}) conditional(s32[]{:T(128)} %convert_element_type.7, (f32[1024,1024]{1,0:T(8,128)}, f32[1024]{0:T(1024)S(1)}) %tuple.31, (f32[1024,1024]{1,0:T(8,128)}, f32[1024,1024]{1,0:T(8,128)}, f32[1024]{0:T(1024)S(1)}, f32[1024]{0:T(1024)S(1)}) %tuple.32), branch_computations={%region_0.1_spmd, %region_1.2_spmd} | conditional | flops 12897485824 | bytes 33574956 | solution.py:57
  10.8 4.8 %copy.6 = f32[1024,1024]{1,0:T(8,128)} copy(f32[1024,1024]{1,0:T(8,128)} %get-tuple-element.42) | data formatting | bytes 8388608 | tf_op jit(solution)/shard_map/cond
  15.5 47.5 %collective-permute-start.2 = (f32[1024,1024]{1,0:T(8,128)}, f32[1024,1024]{1,0:T(8,128)}, u32[]{:S(2)}, u32[]{:S(2)}) collective-permute-start(f32[1024,1024]{1,0:T(8,128)} %get-tuple-element.38), channel_id=1, source_target_pairs={{0,2},{1,3},{2,4},{3,5},{4,6},{5,7},{6,8},{7,9},{8,10},{9,11},{10,... | collective-permute-start | bytes 12582920 | tf_op jit(solution)/shard_map/ppermute | solution.py:12
  63.0 2.4 collective-permute-start.3
  65.4 72.0 %collective-permute-done.3 = f32[1024]{0:T(1024)S(1)} collective-permute-done((f32[1024]{0:T(1024)S(1)}, f32[1024]{0:T(1024)S(1)}, u32[]{:S(2)}, u32[]{:S(2)}) %collective-permute-start.3) | collective-permute-done | bytes 4128 | tf_op jit(solution)/shard_map/ppermute | solution.py:12
  137.5 4.8 %conditional.3 = (f32[1024,1024]{1,0:T(8,128)}, f32[1024]{0:T(1024)S(1)}) conditional(s32[]{:T(128)} %convert_element_type.6, (f32[1024,1024]{1,0:T(8,128)}, f32[1024]{0:T(1024)S(1)}) %conditional.2, (f32[1024,1024]{1,0:T(8,128)}, f32[1024,1024]{1,0:T(8,128)}, f32[1024]{0:T(1024)S(1)}, f32[1024]{0:T(1024)S(1)}) %tuple.23), branch_computations={%region_2.3_spmd, %region_3.4_spmd} | conditional | flops 12897485824 | bytes 16797712 | solution.py:57
  137.5 4.8 %copy.10 = f32[1024,1024]{1,0:T(8,128)} copy(f32[1024,1024]{1,0:T(8,128)} %get-tuple-element.46) | data formatting | bytes 8388608 | tf_op jit(solution)/shard_map/cond
  142.2 1.3 collective-permute-start.4
  143.5 50.7 %collective-permute-done.4 = f32[1024,1024]{1,0:T(8,128)} collective-permute-done((f32[1024,1024]{1,0:T(8,128)}, f32[1024,1024]{1,0:T(8,128)}, u32[]{:S(2)}, u32[]{:S(2)}) %collective-permute-start.4) | collective-permute-done | bytes 4194336 | tf_op jit(solution)/shard_map/ppermute | solution.py:12
  194.2 5.5 %broadcast_select_fusion = f32[1024,1024]{1,0:T(8,128)} fusion(f32[1024,1024]{1,0:T(8,128)} %collective-permute-done.4, f32[1024,1024]{1,0:T(8,128)} %get-tuple-element.40, pred[]{:T(512)S(6)} %eq.19), kind=kLoop, calls=%fused_computation | loop fusion | flops 1048576 | bytes 12582913 | tf_op jit(solution)/shard_map/jit(_where)/select_n | solution.py:64
  199.7 1.3 collective-permute-start.5
  201.1 1.6 collective-permute-start.8
  202.7 82.5 %collective-permute-done.5 = f32[1024,1024]{1,0:T(8,128)} collective-permute-done((f32[1024,1024]{1,0:T(8,128)}, f32[1024,1024]{1,0:T(8,128)}, u32[]{:S(2)}, u32[]{:S(2)}) %collective-permute-start.5) | collective-permute-done | bytes 4194336 | tf_op jit(solution)/shard_map/ppermute | solution.py:12
  285.2 3.1 broadcast_select_fusion.1
  288.3 0.0 copy-start.2
  288.4 4.2 %convolution_bitcast_fusion = f32[64,1024]{1,0:T(8,128)S(1)} fusion(f32[1024,1024]{1,0:T(8,128)S(1)} %broadcast_select_fusion.1, f32[1,64,1024]{2,1,0:T(8,128)S(1)} %copy-done.1), kind=kOutput, calls=%fused_computation.2 | convolution fusion | flops 805306368 | bytes 4718592 | tf_op jit(solution)/shard_map/dot_general | solution.py:74
  292.6 1.0 fusion
  293.6 41.3 %collective-permute-start.6 = (f32[1024]{0:T(1024)S(1)}, f32[1024]{0:T(1024)S(1)}, u32[]{:S(2)}, u32[]{:S(2)}) collective-permute-start(f32[1024]{0:T(1024)S(1)} %bitcast.37), channel_id=1, source_target_pairs={{0,1},{1,0},{2,3},{3,2},{4,5},{5,4},{6,7},{7,6},{8,9},{9,8},{10,11... | collective-permute-start | bytes 12296 | tf_op jit(solution)/shard_map/ppermute | solution.py:22
  334.9 1.9 collective-permute-start.11
  336.7 1.3 collective-permute-start.9
  338.0 3.9 %collective-permute-start.7 = (f32[1024]{0:T(1024)S(1)}, f32[1024]{0:T(1024)S(1)}, u32[]{:S(2)}, u32[]{:S(2)}) collective-permute-start(f32[1024]{0:T(1024)S(1)} %add.35), channel_id=1, source_target_pairs={{0,2},{2,0},{1,3},{3,1},{4,6},{6,4},{5,7},{7,5},{8,10},{10,8},{9,1... | collective-permute-start | bytes 12296 | tf_op jit(solution)/shard_map/ppermute | solution.py:22
  342.0 1.6 collective-permute-done.7
  343.6 0.1 dynamic_slice.7
  343.7 2.9 collective-permute-start.10
  346.5 2.5 collective-permute-done.10
  349.0 0.6 sub.6
  349.6 0.7 fusion.3
  (11 shorter events, 0.0 us)
Async XLA Ops:
  1.3 9.5 %collective-permute-start = (f32[1024,1024]{1,0:T(8,128)}, f32[1024,1024]{1,0:T(8,128)}, u32[]{:S(2)}, u32[]{:S(2)}) collective-permute-start(f32[1024,1024]{1,0:T(8,128)} %bitcast.31), channel_id=1, source_target_pairs={{0,1},{1,2},{2,3},{3,4},{4,5},{5,6},{6,7},{7,8},{8,9},{9,10},{10,1... | collective-permute-start | bytes 12582920 | tf_op jit(solution)/shard_map/ppermute | solution.py:12
  5.6 4.8 %collective-permute-start.1 = (f32[1024]{0:T(1024)S(1)}, f32[1024]{0:T(1024)S(1)}, u32[]{:S(2)}, u32[]{:S(2)}) collective-permute-start(f32[1024]{0:T(1024)S(1)} %bitcast.34), channel_id=1, source_target_pairs={{0,1},{1,2},{2,3},{3,4},{4,5},{5,6},{6,7},{7,8},{8,9},{9,10},{10,1... | collective-permute-start | bytes 12296 | tf_op jit(solution)/shard_map/ppermute | solution.py:12
  15.5 121.9 %collective-permute-start.2 = (f32[1024,1024]{1,0:T(8,128)}, f32[1024,1024]{1,0:T(8,128)}, u32[]{:S(2)}, u32[]{:S(2)}) collective-permute-start(f32[1024,1024]{1,0:T(8,128)} %get-tuple-element.38), channel_id=1, source_target_pairs={{0,2},{1,3},{2,4},{3,5},{4,6},{5,7},{6,8},{7,9},{8,10},{9,11},{10,... | collective-permute-start | bytes 12582920 | tf_op jit(solution)/shard_map/ppermute | solution.py:12
  63.0 74.4 %collective-permute-start.3 = (f32[1024]{0:T(1024)S(1)}, f32[1024]{0:T(1024)S(1)}, u32[]{:S(2)}, u32[]{:S(2)}) collective-permute-start(f32[1024]{0:T(1024)S(1)} %get-tuple-element.39), channel_id=1, source_target_pairs={{0,2},{1,3},{2,4},{3,5},{4,6},{5,7},{6,8},{7,9},{8,10},{9,11},{10,... | collective-permute-start | bytes 12296 | tf_op jit(solution)/shard_map/ppermute | solution.py:12
  142.2 52.0 %collective-permute-start.4 = (f32[1024,1024]{1,0:T(8,128)}, f32[1024,1024]{1,0:T(8,128)}, u32[]{:S(2)}, u32[]{:S(2)}) collective-permute-start(f32[1024,1024]{1,0:T(8,128)} %get-tuple-element.40), channel_id=1, source_target_pairs={{2,0},{3,1},{4,2},{5,3},{6,4},{7,5},{8,6},{9,7},{10,8},{11,9},{12,... | collective-permute-start | bytes 12582920 | tf_op jit(solution)/shard_map/ppermute | solution.py:12
  199.7 85.5 %collective-permute-start.5 = (f32[1024,1024]{1,0:T(8,128)}, f32[1024,1024]{1,0:T(8,128)}, u32[]{:S(2)}, u32[]{:S(2)}) collective-permute-start(f32[1024,1024]{1,0:T(8,128)} %broadcast_select_fusion), channel_id=1, source_target_pairs={{1,0},{2,1},{3,2},{4,3},{5,4},{6,5},{7,6},{8,7},{9,8},{10,9},{11,1... | collective-permute-start | bytes 12582920 | tf_op jit(solution)/shard_map/ppermute | solution.py:12
  201.0 87.3 %copy-start.1 = (f32[1,64,1024]{2,1,0:T(8,128)S(1)}, f32[1,64,1024]{2,1,0:T(8,128)}, u32[]{:S(2)}) copy-start(f32[1,64,1024]{2,1,0:T(8,128)} %param.11) | copy-start | bytes 786436
  201.1 135.7 %collective-permute-start.8 = (f32[1024]{0:T(1024)S(1)}, f32[1024]{0:T(1024)S(1)}, u32[]{:S(2)}, u32[]{:S(2)}) collective-permute-start(f32[1024]{0:T(1024)S(1)} %get-tuple-element.41), channel_id=1, source_target_pairs={{2,0},{3,1},{4,2},{5,3},{6,4},{7,5},{8,6},{9,7},{10,8},{11,9},{12,... | collective-permute-start | bytes 12296 | tf_op jit(solution)/shard_map/ppermute | solution.py:12
  288.3 4.2 %copy-start.2 = (f32[1,256]{1,0:T(1,128)S(1)}, f32[1,256]{1,0:T(1,128)}, u32[]{:S(2)}) copy-start(f32[1,256]{1,0:T(1,128)} %param.10) | copy-start | bytes 3076
  293.6 44.5 %collective-permute-start.6 = (f32[1024]{0:T(1024)S(1)}, f32[1024]{0:T(1024)S(1)}, u32[]{:S(2)}, u32[]{:S(2)}) collective-permute-start(f32[1024]{0:T(1024)S(1)} %bitcast.37), channel_id=1, source_target_pairs={{0,1},{1,0},{2,3},{3,2},{4,5},{5,4},{6,7},{7,6},{8,9},{9,8},{10,11... | collective-permute-start | bytes 12296 | tf_op jit(solution)/shard_map/ppermute | solution.py:22
  334.9 14.7 %collective-permute-start.11 = (f32[64,1024]{1,0:T(8,128)S(1)}, f32[64,1024]{1,0:T(8,128)S(1)}, u32[]{:S(2)}, u32[]{:S(2)}) collective-permute-start(f32[64,1024]{1,0:T(8,128)S(1)} %convolution_bitcast_fusion), channel_id=1, source_target_pairs={{0,4},{1,5},{2,6},{3,7},{4,8},{5,9},{6,10},{7,11},{8,12},{9,13},{1... | collective-permute-start | bytes 786440 | tf_op jit(solution)/shard_map/ppermute | solution.py:27
  336.7 5.3 %collective-permute-start.9 = (f32[1024]{0:T(1024)S(1)}, f32[1024]{0:T(1024)S(1)}, u32[]{:S(2)}, u32[]{:S(2)}) collective-permute-start(f32[1024]{0:T(1024)S(1)} %broadcast_select_fusion.2), channel_id=1, source_target_pairs={{1,0},{2,1},{3,2},{4,3},{5,4},{6,5},{7,6},{8,7},{9,8},{10,9},{11,1... | collective-permute-start | bytes 12296 | tf_op jit(solution)/shard_map/ppermute | solution.py:12
  338.0 5.5 %collective-permute-start.7 = (f32[1024]{0:T(1024)S(1)}, f32[1024]{0:T(1024)S(1)}, u32[]{:S(2)}, u32[]{:S(2)}) collective-permute-start(f32[1024]{0:T(1024)S(1)} %add.35), channel_id=1, source_target_pairs={{0,2},{2,0},{1,3},{3,1},{4,6},{6,4},{5,7},{7,5},{8,10},{10,8},{9,1... | collective-permute-start | bytes 12296 | tf_op jit(solution)/shard_map/ppermute | solution.py:22
  343.7 5.4 %collective-permute-start.10 = (f32[256]{0:T(256)S(1)}, f32[256]{0:T(256)S(1)}, u32[]{:S(2)}, u32[]{:S(2)}) collective-permute-start(f32[256]{0:T(256)S(1)} %dynamic_slice.7), channel_id=1, source_target_pairs={{0,4},{1,5},{2,6},{3,7},{4,8},{5,9},{6,10},{7,11},{8,12},{9,13},{1... | collective-permute-start | bytes 3080 | tf_op jit(solution)/shard_map/ppermute | solution.py:27
where the time goes:
time: 351 us; the launch traced here: 350 us
  waiting for transfers between devices  212 us (60%)
  starting transfers between devices  112 us (32%)
  local copies, waits for them, and re-layouts  10.3 us (3%)
  other arithmetic  9.96 us (3%)
  matrix products  5.19 us (1%)
    ppermute x8, waiting for transfers between devices, passed_along(): return lax.ppermute(shard, axis, pairs)  208 us
    ppermute x8, starting transfers between devices, passed_along(): return lax.ppermute(shard, axis, pairs)  62.2 us
    ppermute x2, starting transfers between devices, partner(): return lax.ppermute(block, axis, route)  45.2 us
    cond x2, local copies, waits for them, and re-layouts  9.51 us
    select_n x2, other arithmetic, local(): matrix = jnp.where(accept_down, got_mat, matrix)  8.64 us
  transfers between devices with their start and end apart: 12, of which 7 were waited for; matrix products, arithmetic and copies ran while one was open for 3% of the time, Pallas kernels for 0%

commit v1 on v0

v1 whole, which is shorter than its diff:
```python
import functools

import jax
import jax.numpy as jnp
from jax import lax
from jax.experimental import pallas as pl
from jax.experimental.pallas import tpu as pltpu
from jax.sharding import PartitionSpec as P

WIN = 4
VMEM = pl.BlockSpec(memory_space=pltpu.VMEM)
PAD = 8


def swapped(block, bit):
    count = lax.axis_size("step")
    return lax.ppermute(block, "step", [(i, i ^ bit) for i in range(count)])


def product_nt(left, right):
    return lax.dot_general(left, right, (((1,), (1,)), ((), ())), preferred_element_type=jnp.float32)


def high_low(value):
    high = value.astype(jnp.bfloat16)
    return high, (value - high.astype(jnp.float32)).astype(jnp.bfloat16)


def times(x, high, low):
    rows = x.shape[0]
    x_high = x.astype(jnp.bfloat16).astype(jnp.float32)
    both = jnp.concatenate([x_high, x - x_high], 0).astype(jnp.bfloat16)
    wide = product_nt(both, high)
    narrow = product_nt(both[: (rows + 15) // 16 * 16], low)
    return wide[:rows] + wide[rows:] + narrow[:rows]


def two_steps(x, maps, sources, state):
    for k in range(2):
        x = times(x, maps[0, k], maps[1, k])
        if state:
            row = lax.broadcasted_iota(jnp.int32, (PAD, x.shape[1]), 0)
            tail = x[-PAD:] + jnp.where(row == 0, sources[k], 0.0)
            x = jnp.concatenate([x[:-PAD], tail], 0)
    return x


def load_sources(own_f, other_f, core):
    own, other = own_f[...], other_f[...]
    return jnp.where(core == 0, own, other), jnp.where(core == 0, other, own)


def first_kernel(rows_ref, own_s, s1, s2, s3, own_f, other_f, own_p, other_p, out, maps):
    place = lax.axis_index("step") % WIN
    core = place % 2
    maps[0, core], maps[1, core] = high_low(own_p[...])
    maps[0, 1 - core], maps[1, 1 - core] = high_low(other_p[...])
    slices = (own_s[...], s1[...], s2[...], s3[...])
    ordered = []
    for j in range(WIN):
        flip = j ^ place
        pick = slices[0]
        for k in range(1, WIN):
            pick = jnp.where(flip == k, slices[k], pick)
        ordered.append(pick)
    x0 = jnp.concatenate(ordered, 1)
    row = lax.broadcasted_iota(jnp.int32, (PAD, x0.shape[1]), 0)
    x = jnp.concatenate([rows_ref[...], jnp.where(row == 0, x0, 0.0)], 0)
    out[...] = two_steps(x, maps, load_sources(own_f, other_f, core), True)


def rows_kernel(rows_ref, maps, out):
    out[...] = two_steps(rows_ref[...], maps, None, False)


def state_kernel(rows_ref, own_f, other_f, maps, out):
    core = lax.axis_index("step") % 2
    out[...] = two_steps(rows_ref[...], maps, load_sources(own_f, other_f, core), True)


def rows_and_state_kernel(rows_ref, state_ref, maps, out):
    count = rows_ref.shape[0]
    out[:count] = two_steps(rows_ref[...], maps, None, False)
    out[count:] = state_ref[count:]


def last_kernel(near, far, starts, directions, residual, jacobian):
    place = lax.axis_index("step") % WIN
    count = directions.shape[0]
    width = starts.shape[1]
    second = place >= WIN // 2
    jacobian[...] = jnp.where(second, near[:count], far[:count]) - directions[...]
    end = jnp.where(second, near[count : count + 1], far[count : count + 1])
    mine = end[:, :width]
    for j in range(1, WIN):
        mine = jnp.where(place == j, end[:, j * width : (j + 1) * width], mine)
    residual[...] = mine - starts[...]


def call(body, out_shape, *args):
    return pl.pallas_call(
        body,
        out_shape=out_shape,
        in_specs=[VMEM] * len(args),
        out_specs=jax.tree.map(lambda _: VMEM, out_shape),
        compiler_params=pltpu.CompilerParams(vmem_limit_bytes=40 << 20),
    )(*args)


def local(propagators, forcing, starts, directions):
    own_p, rows = propagators[0], directions[0]
    order = own_p.shape[0]
    count = rows.shape[0]
    steps = lax.axis_size("step")
    f32 = functools.partial(jax.ShapeDtypeStruct, dtype=jnp.float32)
    other_p = swapped(own_p, 1)
    other_rows = swapped(rows, 2)
    other_f = swapped(forcing, 1)
    s1, s2, s3 = (swapped(starts, k) for k in range(1, WIN))
    x_b, maps = call(
        first_kernel,
        (f32((count + PAD, order)), jax.ShapeDtypeStruct((2, 2, order, order), jnp.bfloat16)),
        other_rows, starts, s1, s2, s3, forcing, other_f, own_p, other_p,
    )
    got_b = swapped(x_b, 2)
    x_a = call(rows_kernel, f32((count, order)), rows, maps)
    got_a = swapped(x_a, 2)
    y_b = call(state_kernel, f32((count + PAD, order)), got_b, forcing, other_f, maps)
    near = lax.ppermute(
        y_b, "step", [(i, (i + WIN) % steps if i % WIN >= WIN // 2 else i ^ 1) for i in range(steps)]
    )
    y_a = call(rows_and_state_kernel, f32((count + PAD, order)), got_a, y_b, maps)
    far = lax.ppermute(
        y_a, "step",
        [(i, (i + WIN - 2) % steps if i % WIN >= WIN // 2 else i + 2) for i in range(steps)],
    )
    residual, jacobian = call(last_kernel, (f32(starts.shape), f32(rows.shape)), near, far, starts, rows)
    return residual, jacobian[None]


def solution(mesh):
    return jax.shard_map(
        local,
        mesh=mesh,
        in_specs=(
            P(("parts", "step"), None, None),
            P(("parts", "step"), None),
            P(("parts", "step"), None),
            P(("parts", "step"), None, None),
        ),
        out_specs=(P(("parts", "step"), None), P(("parts", "step"), None, None)),
        check_vma=False,
    )
```

time: 351 us -> 55.9 us (0.16)
  the two profiles are of different devices: /device:TPU:0 before, /device:TPU:4 now
where the time goes in v1:
time: 55.9 us; the launch traced here: 55.7 us
  waiting for transfers between devices  24.2 us (43%)
  Pallas kernels  14.6 us (26%)
  starting transfers between devices  9.29 us (17%)
  local copies, waits for them, and re-layouts  6.94 us (12%)
  between operations  0.68 us (1%)
    pallas_call x5, Pallas kernels, call(): pl.pallas_call(body, out_shape=out_shape, in_specs=[VMEM] * len(args), ou...  14.6 us
    ppermute x8, waiting for transfers between devices, swapped(): return lax.ppermute(block, 'step', [(i, i ^ bit) for i in range(count)])  11.1 us
    ppermute x1, waiting for transfers between devices, local(): lax.ppermute(y_b, 'step', [(i, (i + WIN) % steps if i % WIN >= WIN // 2 e...  7.18 us
    unnamed x16, local copies, waits for them, and re-layouts  6.94 us
    ppermute x1, waiting for transfers between devices, local(): lax.ppermute(y_a, 'step', [(i, (i + WIN - 2) % steps if i % WIN >= WIN //...  5.9 us
    ppermute x8, starting transfers between devices, swapped(): return lax.ppermute(block, 'step', [(i, i ^ bit) for i in range(count)])  5.03 us
    ppermute x1, starting transfers between devices, local(): lax.ppermute(y_a, 'step', [(i, (i + WIN - 2) % steps if i % WIN >= WIN //...  2.68 us
    ppermute x1, starting transfers between devices, local(): lax.ppermute(y_b, 'step', [(i, (i + WIN) % steps if i % WIN >= WIN // 2 e...  1.57 us
  transfers between devices with their start and end apart: 10, of which 6 were waited for; matrix products, arithmetic and copies ran while one was open for 0% of the time, Pallas kernels for 10%

profile of v1, /device:TPU:4, one launch (start us, length us, event | category | flops | bytes accessed | tf_op | source)
XLA Modules:
  0.0 55.7 jit_solution(4907379881522747449)
XLA Ops:
  0.6 0.1 collective-permute-start.5
  0.7 0.1 collective-permute-start
  0.8 0.4 collective-permute-start.4
  1.2 1.7 %collective-permute-start.3 = (f32[1,256]{1,0:T(1,128)}, f32[1,256]{1,0:T(1,128)S(1)}, u32[]{:S(2)}, u32[]{:S(2)}) collective-permute-start(f32[1,256]{1,0:T(1,128)} %starts.1), channel_id=1, source_target_pairs={{0,3},{1,2},{2,1},{3,0},{4,7},{5,6},{6,5},{7,4},{8,11},{9,10},{10,... | collective-permute-start | bytes 3080 | tf_op jit(solution)/shard_map/ppermute | solution.py:17
  2.9 0.1 collective-permute-start.2
  3.0 6.2 %collective-permute-done.3.s3 = f32[1,256]{1,0:T(1,128)S(1)} collective-permute-done((f32[1,256]{1,0:T(1,128)}, f32[1,256]{1,0:T(1,128)S(1)}, u32[]{:S(2)}, u32[]{:S(2)}) %collective-permute-start.3) | collective-permute-done | bytes 1056 | tf_op jit(solution)/shard_map/ppermute | solution.py:17
  9.2 0.6 %collective-permute-start.1 = (f32[1,256]{1,0:T(1,128)}, f32[1,256]{1,0:T(1,128)S(1)}, u32[]{:S(2)}, u32[]{:S(2)}) collective-permute-start(f32[1,256]{1,0:T(1,128)} %starts.1), channel_id=1, source_target_pairs={{0,1},{1,0},{2,3},{3,2},{4,5},{5,4},{6,7},{7,6},{8,9},{9,8},{10,11... | collective-permute-start | bytes 3080 | tf_op jit(solution)/shard_map/ppermute | solution.py:17
  9.8 0.0 collective-permute-done.2.s2
  9.8 1.0 %collective-permute-done.1.s1 = f32[1,256]{1,0:T(1,128)S(1)} collective-permute-done((f32[1,256]{1,0:T(1,128)}, f32[1,256]{1,0:T(1,128)S(1)}, u32[]{:S(2)}, u32[]{:S(2)}) %collective-permute-start.1) | collective-permute-done | bytes 1056 | tf_op jit(solution)/shard_map/ppermute | solution.py:17
  10.8 0.0 collective-permute-done.4.other_f
  10.8 0.0 collective-permute-done.rows_ref
  10.8 0.0 collective-permute-done.5.other_p
  10.8 0.0 copy-start.2
  10.8 2.2 %copy-done.2 = f32[1,1024,1024]{2,1,0:T(8,128)S(1)} copy-done((f32[1,1024,1024]{2,1,0:T(8,128)S(1)}, f32[1,1024,1024]{2,1,0:T(8,128)}, u32[]{:S(2)}) %copy-start.2) | copy-done | bytes 4194328
  13.0 0.7 %copy-done.4 = f32[1,1024]{1,0:T(1,128)S(1)} copy-done((f32[1,1024]{1,0:T(1,128)S(1)}, f32[1,1024]{1,0:T(1,128)}, u32[]{:S(2)}) %copy-start.4) | copy-done | bytes 4120
  13.7 0.7 %copy-done.6 = f32[1,256]{1,0:T(1,128)S(1)} copy-done((f32[1,256]{1,0:T(1,128)S(1)}, f32[1,256]{1,0:T(1,128)}, u32[]{:S(2)}) %copy-start.6) | copy-done | bytes 1048
  14.4 5.6 %shard_map.59 = (f32[72,1024]{1,0:T(8,128)S(1)}, bf16[2,2,1024,1024]{3,2,1,0:T(8,128)(2,1)}) custom-call(f32[64,1024]{1,0:T(8,128)S(1)} %collective-permute-done.rows_ref, f32[1,256]{1,0:T(1,128)S(1)} %copy-done.6, f32[1,256]{1,0:T(1,128)S(1)} %collective-permute-done.1.s1, f32[1,256]{1,0:T(1,128)S(1)} %collective-permute-done.2.s2, ...), custom_call_target="tpu_custom_call" | custom-call | tf_op jit(solution)/shard_map/pallas_call | solution.py:101
  20.0 0.3 collective-permute-start.6
  20.3 3.4 %copy-done = bf16[2,2,1024,1024]{3,2,1,0:T(8,128)(2,1)S(1)} copy-done((bf16[2,2,1024,1024]{3,2,1,0:T(8,128)(2,1)S(1)}, bf16[2,2,1024,1024]{3,2,1,0:T(8,128)(2,1)}, u32[]{:S(2)}) %copy-start) | copy-done | bytes 8388632
  23.7 2.7 %shard_map.61 = f32[64,1024]{1,0:T(8,128)S(1)} custom-call(f32[64,1024]{1,0:T(8,128)S(1)} %bitcast.6, bf16[2,2,1024,1024]{3,2,1,0:T(8,128)(2,1)S(1)} %copy-done), custom_call_target="tpu_custom_call" | custom-call | tf_op jit(solution)/shard_map/pallas_call | solution.py:101
  26.4 1.8 %collective-permute-start.8 = (f32[64,1024]{1,0:T(8,128)S(1)}, f32[64,1024]{1,0:T(8,128)S(1)}, u32[]{:S(2)}, u32[]{:S(2)}) collective-permute-start(f32[64,1024]{1,0:T(8,128)S(1)} %shard_map.61), channel_id=1, source_target_pairs={{0,2},{1,3},{2,0},{3,1},{4,6},{5,7},{6,4},{7,5},{8,10},{9,11},{10,... | collective-permute-start | bytes 786440 | tf_op jit(solution)/shard_map/ppermute | solution.py:17
  28.2 1.1 %collective-permute-done.6.rows_ref = f32[72,1024]{1,0:T(8,128)S(1)} collective-permute-done((f32[72,1024]{1,0:T(8,128)S(1)}, f32[72,1024]{1,0:T(8,128)S(1)}, u32[]{:S(2)}, u32[]{:S(2)}) %collective-permute-start.6) | collective-permute-done | bytes 294944 | tf_op jit(solution)/shard_map/ppermute | solution.py:17
  29.3 0.0 copy-done.1
  29.3 2.8 %shard_map.60.state_ref = f32[72,1024]{1,0:T(8,128)S(1)} custom-call(f32[72,1024]{1,0:T(8,128)S(1)} %collective-permute-done.6.rows_ref, f32[1,1024]{1,0:T(1,128)S(1)} %copy-done.5, f32[1,1024]{1,0:T(1,128)S(1)} %collective-permute-done.4.other_f, bf16[2,2,1024,1024]{3,2,1,0:T(8,128)(2,1)S(1)} %copy-done.1), custom_call_target="tpu_custom_call" | custom-call | tf_op jit(solution)/shard_map/pallas_call | solution.py:101
  32.1 0.0 copy-start.7
  32.1 2.8 %collective-permute-done.8.rows_ref = f32[64,1024]{1,0:T(8,128)S(1)} collective-permute-done((f32[64,1024]{1,0:T(8,128)S(1)}, f32[64,1024]{1,0:T(8,128)S(1)}, u32[]{:S(2)}, u32[]{:S(2)}) %collective-permute-start.8) | collective-permute-done | bytes 262176 | tf_op jit(solution)/shard_map/ppermute | solution.py:17
  34.9 2.7 %shard_map.62 = f32[72,1024]{1,0:T(8,128)S(1)} custom-call(f32[64,1024]{1,0:T(8,128)S(1)} %collective-permute-done.8.rows_ref, f32[72,1024]{1,0:T(8,128)S(1)} %shard_map.60.state_ref, bf16[2,2,1024,1024]{3,2,1,0:T(8,128)(2,1)S(1)} %copy-done.1), custom_call_target="tpu_custom_call" | custom-call | tf_op jit(solution)/shard_map/pallas_call | solution.py:101
  37.6 2.7 %collective-permute-start.9 = (f32[72,1024]{1,0:T(8,128)S(1)}, f32[72,1024]{1,0:T(8,128)S(1)}, u32[]{:S(2)}, u32[]{:S(2)}) collective-permute-start(f32[72,1024]{1,0:T(8,128)S(1)} %shard_map.62), channel_id=1, source_target_pairs={{0,2},{1,3},{2,4},{3,5},{4,6},{5,7},{6,8},{7,9},{8,10},{9,11},{10,... | collective-permute-start | bytes 884744 | tf_op jit(solution)/shard_map/ppermute | solution.py:133
  40.3 1.6 %collective-permute-start.7 = (f32[72,1024]{1,0:T(8,128)S(1)}, f32[72,1024]{1,0:T(8,128)S(1)}, u32[]{:S(2)}, u32[]{:S(2)}) collective-permute-start(f32[72,1024]{1,0:T(8,128)S(1)} %shard_map.60.state_ref), channel_id=1, source_target_pairs={{0,1},{1,0},{2,6},{3,7},{4,5},{5,4},{6,10},{7,11},{8,9},{9,8},{10,... | collective-permute-start | bytes 884744 | tf_op jit(solution)/shard_map/ppermute | solution.py:129
  41.9 5.9 %collective-permute-done.9.far = f32[72,1024]{1,0:T(8,128)S(1)} collective-permute-done((f32[72,1024]{1,0:T(8,128)S(1)}, f32[72,1024]{1,0:T(8,128)S(1)}, u32[]{:S(2)}, u32[]{:S(2)}) %collective-permute-start.9) | collective-permute-done | bytes 294944 | tf_op jit(solution)/shard_map/ppermute | solution.py:133
  47.8 7.2 %collective-permute-done.7.near = f32[72,1024]{1,0:T(8,128)S(1)} collective-permute-done((f32[72,1024]{1,0:T(8,128)S(1)}, f32[72,1024]{1,0:T(8,128)S(1)}, u32[]{:S(2)}, u32[]{:S(2)}) %collective-permute-start.7) | collective-permute-done | bytes 294944 | tf_op jit(solution)/shard_map/ppermute | solution.py:129
  54.9 0.7 %shard_map.63 = (f32[1,256]{1,0:T(1,128)}, f32[64,1024]{1,0:T(8,128)}) custom-call(f32[72,1024]{1,0:T(8,128)S(1)} %collective-permute-done.7.near, f32[72,1024]{1,0:T(8,128)S(1)} %collective-permute-done.9.far, f32[1,256]{1,0:T(1,128)S(1)} %copy-done.7, f32[64,1024]{1,0:T(8,128)S(1)} %bitcast.7), custom_call_target="tpu_custom_call" | custom-call | tf_op jit(solution)/shard_map/pallas_call | solution.py:101
  (9 shorter events, 0.0 us)
Async XLA Ops:
  0.6 10.2 %collective-permute-start.5 = (f32[1024,1024]{1,0:T(8,128)}, f32[1024,1024]{1,0:T(8,128)S(1)}, u32[]{:S(2)}, u32[]{:S(2)}) collective-permute-start(f32[1024,1024]{1,0:T(8,128)} %bitcast.3), channel_id=1, source_target_pairs={{0,1},{1,0},{2,3},{3,2},{4,5},{5,4},{6,7},{7,6},{8,9},{9,8},{10,11... | collective-permute-start | bytes 12582920 | tf_op jit(solution)/shard_map/ppermute | solution.py:17
  0.7 10.1 %collective-permute-start = (f32[64,1024]{1,0:T(8,128)}, f32[64,1024]{1,0:T(8,128)S(1)}, u32[]{:S(2)}, u32[]{:S(2)}) collective-permute-start(f32[64,1024]{1,0:T(8,128)} %bitcast.5), channel_id=1, source_target_pairs={{0,2},{1,3},{2,0},{3,1},{4,6},{5,7},{6,4},{7,5},{8,10},{9,11},{10,... | collective-permute-start | bytes 786440 | tf_op jit(solution)/shard_map/ppermute | solution.py:17
  0.8 10.0 %collective-permute-start.4 = (f32[1,1024]{1,0:T(1,128)}, f32[1,1024]{1,0:T(1,128)S(1)}, u32[]{:S(2)}, u32[]{:S(2)}) collective-permute-start(f32[1,1024]{1,0:T(1,128)} %own_f.3), channel_id=1, source_target_pairs={{0,1},{1,0},{2,3},{3,2},{4,5},{5,4},{6,7},{7,6},{8,9},{9,8},{10,11... | collective-permute-start | bytes 12296 | tf_op jit(solution)/shard_map/ppermute | solution.py:17
  1.2 8.0 %collective-permute-start.3 = (f32[1,256]{1,0:T(1,128)}, f32[1,256]{1,0:T(1,128)S(1)}, u32[]{:S(2)}, u32[]{:S(2)}) collective-permute-start(f32[1,256]{1,0:T(1,128)} %starts.1), channel_id=1, source_target_pairs={{0,3},{1,2},{2,1},{3,0},{4,7},{5,6},{6,5},{7,4},{8,11},{9,10},{10,... | collective-permute-start | bytes 3080 | tf_op jit(solution)/shard_map/ppermute | solution.py:17
  2.9 6.9 %collective-permute-start.2 = (f32[1,256]{1,0:T(1,128)}, f32[1,256]{1,0:T(1,128)S(1)}, u32[]{:S(2)}, u32[]{:S(2)}) collective-permute-start(f32[1,256]{1,0:T(1,128)} %starts.1), channel_id=1, source_target_pairs={{0,2},{1,3},{2,0},{3,1},{4,6},{5,7},{6,4},{7,5},{8,10},{9,11},{10,... | collective-permute-start | bytes 3080 | tf_op jit(solution)/shard_map/ppermute | solution.py:17
  9.2 1.6 %collective-permute-start.1 = (f32[1,256]{1,0:T(1,128)}, f32[1,256]{1,0:T(1,128)S(1)}, u32[]{:S(2)}, u32[]{:S(2)}) collective-permute-start(f32[1,256]{1,0:T(1,128)} %starts.1), channel_id=1, source_target_pairs={{0,1},{1,0},{2,3},{3,2},{4,5},{5,4},{6,7},{7,6},{8,9},{9,8},{10,11... | collective-permute-start | bytes 3080 | tf_op jit(solution)/shard_map/ppermute | solution.py:17
  10.8 2.2 %copy-start.2 = (f32[1,1024,1024]{2,1,0:T(8,128)S(1)}, f32[1,1024,1024]{2,1,0:T(8,128)}, u32[]{:S(2)}) copy-start(f32[1,1024,1024]{2,1,0:T(8,128)} %param.4) | copy-start | bytes 12582916
  13.0 0.7 %copy-start.4 = (f32[1,1024]{1,0:T(1,128)S(1)}, f32[1,1024]{1,0:T(1,128)}, u32[]{:S(2)}) copy-start(f32[1,1024]{1,0:T(1,128)} %own_f.3) | copy-start | bytes 12292
  13.7 0.7 %copy-start.6 = (f32[1,256]{1,0:T(1,128)S(1)}, f32[1,256]{1,0:T(1,128)}, u32[]{:S(2)}) copy-start(f32[1,256]{1,0:T(1,128)} %starts.1) | copy-start | bytes 3076
  14.4 5.9 %copy-start.3 = (f32[1,64,1024]{2,1,0:T(8,128)S(1)}, f32[1,64,1024]{2,1,0:T(8,128)}, u32[]{:S(2)}) copy-start(f32[1,64,1024]{2,1,0:T(8,128)} %param.7) | copy-start | bytes 786436
  20.0 9.3 %collective-permute-start.6 = (f32[72,1024]{1,0:T(8,128)S(1)}, f32[72,1024]{1,0:T(8,128)S(1)}, u32[]{:S(2)}, u32[]{:S(2)}) collective-permute-start(f32[72,1024]{1,0:T(8,128)S(1)} %get-tuple-element.6), channel_id=1, source_target_pairs={{0,2},{1,3},{2,0},{3,1},{4,6},{5,7},{6,4},{7,5},{8,10},{9,11},{10,... | collective-permute-start | bytes 884744 | tf_op jit(solution)/shard_map/ppermute | solution.py:17
  20.3 3.4 %copy-start = (bf16[2,2,1024,1024]{3,2,1,0:T(8,128)(2,1)S(1)}, bf16[2,2,1024,1024]{3,2,1,0:T(8,128)(2,1)}, u32[]{:S(2)}) copy-start(bf16[2,2,1024,1024]{3,2,1,0:T(8,128)(2,1)} %get-tuple-element.7.maps) | copy-start | bytes 25165828
  23.7 5.6 %copy-start.1 = (bf16[2,2,1024,1024]{3,2,1,0:T(8,128)(2,1)S(1)}, bf16[2,2,1024,1024]{3,2,1,0:T(8,128)(2,1)}, u32[]{:S(2)}) copy-start(bf16[2,2,1024,1024]{3,2,1,0:T(8,128)(2,1)} %get-tuple-element.7.maps) | copy-start | bytes 25165828
  23.7 5.6 %copy-start.5 = (f32[1,1024]{1,0:T(1,128)S(1)}, f32[1,1024]{1,0:T(1,128)}, u32[]{:S(2)}) copy-start(f32[1,1024]{1,0:T(1,128)} %own_f.3) | copy-start | bytes 12292
  26.4 8.5 %collective-permute-start.8 = (f32[64,1024]{1,0:T(8,128)S(1)}, f32[64,1024]{1,0:T(8,128)S(1)}, u32[]{:S(2)}, u32[]{:S(2)}) collective-permute-start(f32[64,1024]{1,0:T(8,128)S(1)} %shard_map.61), channel_id=1, source_target_pairs={{0,2},{1,3},{2,0},{3,1},{4,6},{5,7},{6,4},{7,5},{8,10},{9,11},{10,... | collective-permute-start | bytes 786440 | tf_op jit(solution)/shard_map/ppermute | solution.py:17
  32.1 22.9 %copy-start.7 = (f32[1,256]{1,0:T(1,128)S(1)}, f32[1,256]{1,0:T(1,128)}, u32[]{:S(2)}) copy-start(f32[1,256]{1,0:T(1,128)} %starts.1) | copy-start | bytes 3076
  37.6 10.2 %collective-permute-start.9 = (f32[72,1024]{1,0:T(8,128)S(1)}, f32[72,1024]{1,0:T(8,128)S(1)}, u32[]{:S(2)}, u32[]{:S(2)}) collective-permute-start(f32[72,1024]{1,0:T(8,128)S(1)} %shard_map.62), channel_id=1, source_target_pairs={{0,2},{1,3},{2,4},{3,5},{4,6},{5,7},{6,8},{7,9},{8,10},{9,11},{10,... | collective-permute-start | bytes 884744 | tf_op jit(solution)/shard_map/ppermute | solution.py:133
  40.3 14.6 %collective-permute-start.7 = (f32[72,1024]{1,0:T(8,128)S(1)}, f32[72,1024]{1,0:T(8,128)S(1)}, u32[]{:S(2)}, u32[]{:S(2)}) collective-permute-start(f32[72,1024]{1,0:T(8,128)S(1)} %shard_map.60.state_ref), channel_id=1, source_target_pairs={{0,1},{1,0},{2,6},{3,7},{4,5},{5,4},{6,10},{7,11},{8,9},{9,8},{10,... | collective-permute-start | bytes 884744 | tf_op jit(solution)/shard_map/ppermute | solution.py:129

commit v2 on v1

v2 whole, which is shorter than its diff:
```python
import functools

import jax
import jax.numpy as jnp
from jax import lax
from jax.experimental import pallas as pl
from jax.experimental.pallas import tpu as pltpu
from jax.sharding import PartitionSpec as P

WIN = 4
HALF = WIN // 2
PAD = 8
PIECES = 4
VMEM = pl.BlockSpec(memory_space=pltpu.VMEM)
ANY = pl.BlockSpec(memory_space=pl.ANY)


def swapped(block, bit):
    count = lax.axis_size("step")
    return lax.ppermute(block, "step", [(i, i ^ bit) for i in range(count)])


def product_nt(left, right):
    return lax.dot_general(left, right, (((1,), (1,)), ((), ())), preferred_element_type=jnp.float32)


def high_low(value):
    high = value.astype(jnp.bfloat16)
    return high, (value - high.astype(jnp.float32)).astype(jnp.bfloat16)


def stacked(x):
    high = x.astype(jnp.bfloat16).astype(jnp.float32)
    return jnp.concatenate([high, x - high], 0).astype(jnp.bfloat16)


def times(both, high, low):
    rows = both.shape[0] // 2
    wide = product_nt(both, high)
    narrow = product_nt(both[: (rows + 15) // 16 * 16], low)
    return wide[:rows] + wide[rows:] + narrow[:rows]


def one_row(at, value):
    row = lax.broadcasted_iota(jnp.int32, (PAD, value.shape[1]), 0)
    return jnp.where(row == at, value, 0.0)


def by_core(body):
    core = lax.axis_index("step") % 2
    for k in range(2):
        pl.when(core == k)(functools.partial(body, k))


def own_kernel(own_p, maps):
    maps[0], maps[1] = high_low(own_p[...])


def first_kernel(mirror_v, own_v, v0, v1, v2, v3, own, other_p, out_b, out_a, other, forces):
    place = lax.axis_index("step") % WIN
    rows = out_a.shape[0]
    order = other_p.shape[0]
    part = order // PIECES

    def split_times(both):
        columns = []
        for k in range(PIECES):
            at = pl.ds(k * part, part)
            high, low = high_low(other_p[at])
            other[0, at] = high
            other[1, at] = low
            columns.append(times(both, high, low))
        return jnp.concatenate(columns, 1)

    vectors = (v0[...], v1[...], v2[...], v3[...])
    width = vectors[0].shape[1] - order
    slices = []
    for j in range(WIN):
        pick = vectors[0][:, :width]
        for flip in range(1, WIN):
            pick = jnp.where(j ^ place == flip, vectors[flip][:, :width], pick)
        slices.append(pick)
    x0 = jnp.concatenate(slices, 1)
    even = place % 2 == 0
    own_f, other_f = vectors[0][:, width:], vectors[1][:, width:]
    forces[0] = one_row(0, jnp.where(even, own_f, other_f))
    forces[1] = one_row(0, jnp.where(even, other_f, own_f))

    def body(k):
        x = jnp.concatenate([mirror_v[...], own_v[...], one_row(0, x0)], 0)
        for step in range(2):
            both = stacked(x)
            y = times(both, own[0], own[1]) if step == k else split_times(both)
            x = jnp.concatenate([y[:-PAD], y[-PAD:] + forces[step]], 0)
        out_b[:rows] = x[:rows]
        out_b[rows:] = x[2 * rows :]
        out_a[...] = x[rows : 2 * rows]

    by_core(body)


def state_kernel(got, forces, own, other, out):
    def body(k):
        maps = (own, other) if k == 0 else (other, own)
        x = got[...]
        for step in range(2):
            y = times(stacked(x), maps[step][0], maps[step][1])
            x = jnp.concatenate([y[:-PAD], y[-PAD:] + forces[step]], 0)
        out[...] = x

    by_core(body)


def rows_kernel(got, with_state, own, other, out):
    def body(k):
        maps = (own, other) if k == 0 else (other, own)
        x = got[...]
        for step in range(2):
            x = times(stacked(x), maps[step][0], maps[step][1])
        out[: x.shape[0]] = x
        out[x.shape[0] :] = with_state[x.shape[0] :]

    by_core(body)


def near_kernel(near, starts, directions, residual, jacobian):
    place = lax.axis_index("step") % WIN
    later = place >= HALF
    rows = directions.shape[0]
    width = starts.shape[1]
    jacobian[...] = jnp.where(later, near[:rows], 0.0) - directions[...]
    mine = slice_of(near[rows : rows + 1], place, width)
    residual[...] = jnp.where(later, mine, 0.0) - starts[...]


def slice_of(end, place, width):
    mine = end[:, :width]
    for j in range(1, WIN):
        mine = jnp.where(place == j, end[:, j * width : (j + 1) * width], mine)
    return mine


def far_kernel(far, near_residual, near_jacobian, residual, jacobian):
    place = lax.axis_index("step") % WIN
    first = place < HALF
    rows = near_jacobian.shape[0]
    jacobian[...] = jnp.where(first, far[:rows], 0.0) + near_jacobian[...]
    mine = slice_of(far[rows : rows + 1], place, residual.shape[1])
    residual[...] = jnp.where(first, mine, 0.0) + near_residual[...]


def call(body, micros, out_shape, *args, specs=None, scratch=(), after=()):
    count, extra = len(args), len(after)

    def run(*refs):
        body(*refs[:count], *refs[count + extra :])

    return pl.pallas_call(
        run,
        out_shape=out_shape,
        in_specs=(specs or [VMEM] * count) + [ANY] * extra,
        out_specs=jax.tree.map(lambda _: VMEM, out_shape),
        scratch_shapes=scratch,
        compiler_params=pltpu.CompilerParams(vmem_limit_bytes=20 << 20),
        cost_estimate=pl.CostEstimate(flops=int(micros * 1e9), bytes_accessed=1, transcendentals=0),
    )(*args, *after)


def local(propagators, forcing, starts, directions):
    own_p, own_v = propagators[0], directions[0]
    order = own_p.shape[0]
    rows = own_v.shape[0]
    steps = lax.axis_size("step")
    f32 = functools.partial(jax.ShapeDtypeStruct, dtype=jnp.float32)
    split = jax.ShapeDtypeStruct((2, order, order), jnp.bfloat16)
    tall = f32((rows + PAD, order))
    other_p = swapped(own_p, 1)
    mirror_v = swapped(own_v, 2)
    vector = jnp.concatenate([starts, forcing], 1)
    vectors = [vector] + [swapped(vector, k) for k in range(1, WIN)]
    own = call(own_kernel, 1, split, own_p)
    x_b, x_a, other, forces = call(
        first_kernel, 3, (tall, f32((rows, order)), split, f32((2, PAD, order))), mirror_v, own_v, *vectors, own, other_p
    )
    got_b = swapped(x_b, 2)
    got_a = swapped(x_a, 2)
    y_b = call(state_kernel, 3, tall, got_b, forces, own, other)
    near = lax.ppermute(
        y_b, "step", [(i, (i + WIN) % steps if i % WIN >= HALF else i ^ 1) for i in range(steps)]
    )
    y_a = call(rows_kernel, 3, tall, got_a, y_b, own, other)
    far = lax.ppermute(
        y_a, "step", [(i, (i + WIN - HALF) % steps if i % WIN >= HALF else i + HALF) for i in range(steps)]
    )
    results = f32(starts.shape), f32(own_v.shape)
    near_results = call(near_kernel, 1, results, near, starts, own_v)
    residual, jacobian = call(far_kernel, 1, results, far, *near_results)
    return residual, jacobian[None]


def solution(mesh):
    return jax.shard_map(
        local,
        mesh=mesh,
        in_specs=(
            P(("parts", "step"), None, None),
            P(("parts", "step"), None),
            P(("parts", "step"), None),
            P(("parts", "step"), None, None),
        ),
        out_specs=(P(("parts", "step"), None), P(("parts", "step"), None, None)),
        check_vma=False,
    )
```

time: 55.9 us -> 44.1 us (0.79)
  the two profiles are of different devices: /device:TPU:4 before, /device:TPU:0 now
where the time goes in v2:
time: 44.1 us; the launch traced here: 43.9 us
  waiting for transfers between devices  20.8 us (47%)
  Pallas kernels  9.85 us (22%)
  starting transfers between devices  8.92 us (20%)
  local copies, waits for them, and re-layouts  3.57 us (8%)
  between operations  0.69 us (2%)
    ppermute x7, waiting for transfers between devices, swapped(): return lax.ppermute(block, 'step', [(i, i ^ bit) for i in range(count)])  10.8 us
    ppermute x1, waiting for transfers between devices, local(): lax.ppermute(y_a, 'step', [(i, (i + WIN - HALF) % steps if i % WIN >= HAL...  10 us
    pallas_call x6, Pallas kernels, call(): pl.pallas_call(run, out_shape=out_shape, in_specs=(specs or [VMEM] * coun...  9.85 us
    ppermute x7, starting transfers between devices, swapped(): return lax.ppermute(block, 'step', [(i, i ^ bit) for i in range(count)])  7.06 us
    unnamed x7, local copies, waits for them, and re-layouts  2.88 us
    ppermute x1, starting transfers between devices, local(): lax.ppermute(y_a, 'step', [(i, (i + WIN - HALF) % steps if i % WIN >= HAL...  1.8 us
  transfers between devices with their start and end apart: 9, of which 5 were waited for; matrix products, arithmetic and copies ran while one was open for 3% of the time, Pallas kernels for 14%

profile of v2, /device:TPU:0, one launch (start us, length us, event | category | flops | bytes accessed | tf_op | source)
XLA Modules:
  0.0 43.9 jit_solution(10798081234653229689)
XLA Ops:
  0.6 0.5 %collective-permute-start.4 = (f32[1024,1024]{1,0:T(8,128)}, f32[1024,1024]{1,0:T(8,128)S(1)}, u32[]{:S(2)}, u32[]{:S(2)}) collective-permute-start(f32[1024,1024]{1,0:T(8,128)} %bitcast.3), channel_id=1, source_target_pairs={{0,1},{1,0},{2,3},{3,2},{4,5},{5,4},{6,7},{7,6},{8,9},{9,8},{10,11... | collective-permute-start | bytes 12582920 | tf_op jit(solution)/shard_map/ppermute | solution.py:20
  1.1 2.6 %collective-permute-start = (f32[64,1024]{1,0:T(8,128)}, f32[64,1024]{1,0:T(8,128)S(1)}, u32[]{:S(2)}, u32[]{:S(2)}) collective-permute-start(f32[64,1024]{1,0:T(8,128)} %bitcast.5), channel_id=1, source_target_pairs={{0,2},{1,3},{2,0},{3,1},{4,6},{5,7},{6,4},{7,5},{8,10},{9,11},{10,... | collective-permute-start | bytes 786440 | tf_op jit(solution)/shard_map/ppermute | solution.py:20
  3.7 0.7 %constant_dynamic-update-slice_fusion.1 = f32[1,1280]{1,0:T(1,128)S(1)} fusion(f32[1,256]{1,0:T(1,128)} %refs_1_.1), kind=kLoop, calls=%fused_computation.1 | loop fusion | bytes 2048
  4.4 0.7 %constant_dynamic-update-slice_fusion.refs_2_ = f32[1,1280]{1,0:T(1,128)S(1)} fusion(f32[1,1280]{1,0:T(1,128)S(1)} %constant_dynamic-update-slice_fusion.1, f32[1,1024]{1,0:T(1,128)} %param.5), kind=kLoop, calls=%fused_computation | loop fusion | bytes 8192 | tf_op jit(solution)/shard_map/concatenate | solution.py:179
  5.1 0.1 collective-permute-start.3
  5.2 1.7 %collective-permute-start.2 = (f32[1,1280]{1,0:T(1,128)S(1)}, f32[1,1280]{1,0:T(1,128)S(1)}, u32[]{:S(2)}, u32[]{:S(2)}) collective-permute-start(f32[1,1280]{1,0:T(1,128)S(1)} %constant_dynamic-update-slice_fusion.refs_2_), channel_id=1, source_target_pairs={{0,2},{1,3},{2,0},{3,1},{4,6},{5,7},{6,4},{7,5},{8,10},{9,11},{10,... | collective-permute-start | bytes 15368 | tf_op jit(solution)/shard_map/ppermute | solution.py:20
  6.9 0.1 collective-permute-start.1
  7.0 0.0 copy-start
  7.0 2.2 %copy-done = f32[1,1024,1024]{2,1,0:T(8,128)S(1)} copy-done((f32[1,1024,1024]{2,1,0:T(8,128)S(1)}, f32[1,1024,1024]{2,1,0:T(8,128)}, u32[]{:S(2)}) %copy-start) | copy-done | bytes 4194328
  9.2 0.0 copy-start.2
  9.2 0.7 %shard_map.59.refs_6_.refs_2_ = bf16[2,1024,1024]{2,1,0:T(8,128)(2,1)S(1)} custom-call(f32[1024,1024]{1,0:T(8,128)S(1)} %bitcast.4), custom_call_target="tpu_custom_call" | custom-call | flops 1000000000 | bytes 1 | tf_op jit(solution)/shard_map/pallas_call | solution.py:158
  9.9 0.8 %collective-permute-done.3.refs_5_ = f32[1,1280]{1,0:T(1,128)S(1)} collective-permute-done((f32[1,1280]{1,0:T(1,128)S(1)}, f32[1,1280]{1,0:T(1,128)S(1)}, u32[]{:S(2)}, u32[]{:S(2)}) %collective-permute-start.3) | collective-permute-done | bytes 5152 | tf_op jit(solution)/shard_map/ppermute | solution.py:20
  10.7 0.4 collective-permute-done.2.refs_4_
  11.1 0.0 collective-permute-done.1.refs_3_
  11.1 0.0 collective-permute-done.refs_0_
  11.1 0.0 collective-permute-done.4.refs_7_
  11.1 0.0 copy-done.2
  11.1 2.9 %shard_map.60 = (f32[72,1024]{1,0:T(8,128)S(1)}, f32[64,1024]{1,0:T(8,128)S(1)}, bf16[2,1024,1024]{2,1,0:T(8,128)(2,1)S(1)}, f32[2,8,1024]{2,1,0:T(8,128)S(1)}) custom-call(f32[64,1024]{1,0:T(8,128)S(1)} %collective-permute-done.refs_0_, f32[64,1024]{1,0:T(8,128)S(1)} %bitcast.6, f32[1,1280]{1,0:T(1,128)S(1)} %constant_dynamic-update-slice_fusion.refs_2_, ...), custom_call_target="tpu_custom_call" | custom-call | flops 3000000000 | bytes 1 | tf_op jit(solution)/shard_map/pallas_call | solution.py:158
  14.0 1.8 %collective-permute-start.6 = (f32[72,1024]{1,0:T(8,128)S(1)}, f32[72,1024]{1,0:T(8,128)S(1)}, u32[]{:S(2)}, u32[]{:S(2)}) collective-permute-start(f32[72,1024]{1,0:T(8,128)S(1)} %get-tuple-element.11), channel_id=1, source_target_pairs={{0,2},{1,3},{2,0},{3,1},{4,6},{5,7},{6,4},{7,5},{8,10},{9,11},{10,... | collective-permute-start | bytes 884744 | tf_op jit(solution)/shard_map/ppermute | solution.py:20
  15.8 0.3 collective-permute-start.5
  16.0 7.8 %collective-permute-done.6.refs_0_ = f32[72,1024]{1,0:T(8,128)S(1)} collective-permute-done((f32[72,1024]{1,0:T(8,128)S(1)}, f32[72,1024]{1,0:T(8,128)S(1)}, u32[]{:S(2)}, u32[]{:S(2)}) %collective-permute-start.6) | collective-permute-done | bytes 294944 | tf_op jit(solution)/shard_map/ppermute | solution.py:20
  23.9 2.8 %shard_map.61.refs_1_ = f32[72,1024]{1,0:T(8,128)S(1)} custom-call(f32[72,1024]{1,0:T(8,128)S(1)} %collective-permute-done.6.refs_0_, f32[2,8,1024]{2,1,0:T(8,128)S(1)} %get-tuple-element.12.refs_1_, bf16[2,1024,1024]{2,1,0:T(8,128)(2,1)S(1)} %shard_map.59.refs_6_.refs_2_, bf16[2,1024,1024]{2,1,0:T(8,128)(2,1)S(1)} %get-tuple-element.13.refs_3_), custom_call_target="tpu_custom_call" | custom-call | flops 3000000000 | bytes 1 | tf_op jit(solution)/shard_map/pallas_call | solution.py:158
  26.7 0.0 copy-start.1
  26.7 0.1 collective-permute-start.8
  26.7 1.8 %collective-permute-done.5.refs_0_ = f32[64,1024]{1,0:T(8,128)S(1)} collective-permute-done((f32[64,1024]{1,0:T(8,128)S(1)}, f32[64,1024]{1,0:T(8,128)S(1)}, u32[]{:S(2)}, u32[]{:S(2)}) %collective-permute-start.5) | collective-permute-done | bytes 262176 | tf_op jit(solution)/shard_map/ppermute | solution.py:20
  28.5 2.7 %shard_map.62 = f32[72,1024]{1,0:T(8,128)S(1)} custom-call(f32[64,1024]{1,0:T(8,128)S(1)} %collective-permute-done.5.refs_0_, f32[72,1024]{1,0:T(8,128)S(1)} %shard_map.61.refs_1_, bf16[2,1024,1024]{2,1,0:T(8,128)(2,1)S(1)} %shard_map.59.refs_6_.refs_2_, bf16[2,1024,1024]{2,1,0:T(8,128)(2,1)S(1)} %get-tuple-element.13.refs_3_), custom_call_target="tpu_custom_call" | custom-call | flops 3000000000 | bytes 1 | tf_op jit(solution)/shard_map/pallas_call | solution.py:158
  31.3 1.8 %collective-permute-start.7 = (f32[72,1024]{1,0:T(8,128)S(1)}, f32[72,1024]{1,0:T(8,128)S(1)}, u32[]{:S(2)}, u32[]{:S(2)}) collective-permute-start(f32[72,1024]{1,0:T(8,128)S(1)} %shard_map.62), channel_id=1, source_target_pairs={{0,2},{1,3},{2,4},{3,5},{4,6},{5,7},{6,8},{7,9},{8,10},{9,11},{10,... | collective-permute-start | bytes 884744 | tf_op jit(solution)/shard_map/ppermute | solution.py:192
  33.1 0.0 collective-permute-done.8.refs_0_
  33.1 0.0 copy-done.1
  33.1 10.0 %collective-permute-done.7.refs_0_ = f32[72,1024]{1,0:T(8,128)S(1)} collective-permute-done((f32[72,1024]{1,0:T(8,128)S(1)}, f32[72,1024]{1,0:T(8,128)S(1)}, u32[]{:S(2)}, u32[]{:S(2)}) %collective-permute-start.7) | collective-permute-done | bytes 294944 | tf_op jit(solution)/shard_map/ppermute | solution.py:192
  43.1 0.7 %shard_map.64 = (f32[1,256]{1,0:T(1,128)}, f32[64,1024]{1,0:T(8,128)}) custom-call(f32[72,1024]{1,0:T(8,128)S(1)} %collective-permute-done.7.refs_0_, f32[1,256]{1,0:T(1,128)S(1)} %get-tuple-element.14.refs_1_, f32[64,1024]{1,0:T(8,128)S(1)} %get-tuple-element.15.refs_2_), custom_call_target="tpu_custom_call" | custom-call | flops 1000000000 | bytes 1 | tf_op jit(solution)/shard_map/pallas_call | solution.py:158
  (1 shorter events, 0.0 us)
Async XLA Ops:
  0.6 10.4 %collective-permute-start.4 = (f32[1024,1024]{1,0:T(8,128)}, f32[1024,1024]{1,0:T(8,128)S(1)}, u32[]{:S(2)}, u32[]{:S(2)}) collective-permute-start(f32[1024,1024]{1,0:T(8,128)} %bitcast.3), channel_id=1, source_target_pairs={{0,1},{1,0},{2,3},{3,2},{4,5},{5,4},{6,7},{7,6},{8,9},{9,8},{10,11... | collective-permute-start | bytes 12582920 | tf_op jit(solution)/shard_map/ppermute | solution.py:20
  1.1 9.9 %collective-permute-start = (f32[64,1024]{1,0:T(8,128)}, f32[64,1024]{1,0:T(8,128)S(1)}, u32[]{:S(2)}, u32[]{:S(2)}) collective-permute-start(f32[64,1024]{1,0:T(8,128)} %bitcast.5), channel_id=1, source_target_pairs={{0,2},{1,3},{2,0},{3,1},{4,6},{5,7},{6,4},{7,5},{8,10},{9,11},{10,... | collective-permute-start | bytes 786440 | tf_op jit(solution)/shard_map/ppermute | solution.py:20
  5.1 5.6 %collective-permute-start.3 = (f32[1,1280]{1,0:T(1,128)S(1)}, f32[1,1280]{1,0:T(1,128)S(1)}, u32[]{:S(2)}, u32[]{:S(2)}) collective-permute-start(f32[1,1280]{1,0:T(1,128)S(1)} %constant_dynamic-update-slice_fusion.refs_2_), channel_id=1, source_target_pairs={{0,3},{1,2},{2,1},{3,0},{4,7},{5,6},{6,5},{7,4},{8,11},{9,10},{10,... | collective-permute-start | bytes 15368 | tf_op jit(solution)/shard_map/ppermute | solution.py:20
  5.2 5.9 %collective-permute-start.2 = (f32[1,1280]{1,0:T(1,128)S(1)}, f32[1,1280]{1,0:T(1,128)S(1)}, u32[]{:S(2)}, u32[]{:S(2)}) collective-permute-start(f32[1,1280]{1,0:T(1,128)S(1)} %constant_dynamic-update-slice_fusion.refs_2_), channel_id=1, source_target_pairs={{0,2},{1,3},{2,0},{3,1},{4,6},{5,7},{6,4},{7,5},{8,10},{9,11},{10,... | collective-permute-start | bytes 15368 | tf_op jit(solution)/shard_map/ppermute | solution.py:20
  6.9 4.2 %collective-permute-start.1 = (f32[1,1280]{1,0:T(1,128)S(1)}, f32[1,1280]{1,0:T(1,128)S(1)}, u32[]{:S(2)}, u32[]{:S(2)}) collective-permute-start(f32[1,1280]{1,0:T(1,128)S(1)} %constant_dynamic-update-slice_fusion.refs_2_), channel_id=1, source_target_pairs={{0,1},{1,0},{2,3},{3,2},{4,5},{5,4},{6,7},{7,6},{8,9},{9,8},{10,11... | collective-permute-start | bytes 15368 | tf_op jit(solution)/shard_map/ppermute | solution.py:20
  7.0 2.2 %copy-start = (f32[1,1024,1024]{2,1,0:T(8,128)S(1)}, f32[1,1024,1024]{2,1,0:T(8,128)}, u32[]{:S(2)}) copy-start(f32[1,1024,1024]{2,1,0:T(8,128)} %param.4) | copy-start | bytes 12582916
  9.2 1.9 %copy-start.2 = (f32[1,64,1024]{2,1,0:T(8,128)S(1)}, f32[1,64,1024]{2,1,0:T(8,128)}, u32[]{:S(2)}) copy-start(f32[1,64,1024]{2,1,0:T(8,128)} %param.7) | copy-start | bytes 786436
  14.0 9.9 %collective-permute-start.6 = (f32[72,1024]{1,0:T(8,128)S(1)}, f32[72,1024]{1,0:T(8,128)S(1)}, u32[]{:S(2)}, u32[]{:S(2)}) collective-permute-start(f32[72,1024]{1,0:T(8,128)S(1)} %get-tuple-element.11), channel_id=1, source_target_pairs={{0,2},{1,3},{2,0},{3,1},{4,6},{5,7},{6,4},{7,5},{8,10},{9,11},{10,... | collective-permute-start | bytes 884744 | tf_op jit(solution)/shard_map/ppermute | solution.py:20
  15.8 12.8 %collective-permute-start.5 = (f32[64,1024]{1,0:T(8,128)S(1)}, f32[64,1024]{1,0:T(8,128)S(1)}, u32[]{:S(2)}, u32[]{:S(2)}) collective-permute-start(f32[64,1024]{1,0:T(8,128)S(1)} %get-tuple-element.10), channel_id=1, source_target_pairs={{0,2},{1,3},{2,0},{3,1},{4,6},{5,7},{6,4},{7,5},{8,10},{9,11},{10,... | collective-permute-start | bytes 786440 | tf_op jit(solution)/shard_map/ppermute | solution.py:20
  26.7 6.4 %copy-start.1 = (f32[1,256]{1,0:T(1,128)S(1)}, f32[1,256]{1,0:T(1,128)}, u32[]{:S(2)}) copy-start(f32[1,256]{1,0:T(1,128)} %refs_1_.1) | copy-start | bytes 3076
  26.7 6.4 %collective-permute-start.8 = (f32[72,1024]{1,0:T(8,128)S(1)}, f32[72,1024]{1,0:T(8,128)S(1)}, u32[]{:S(2)}, u32[]{:S(2)}) collective-permute-start(f32[72,1024]{1,0:T(8,128)S(1)} %shard_map.61.refs_1_), channel_id=1, source_target_pairs={{0,1},{1,0},{2,6},{3,7},{4,5},{5,4},{6,10},{7,11},{8,9},{9,8},{10,... | collective-permute-start | bytes 884744 | tf_op jit(solution)/shard_map/ppermute | solution.py:188
  31.3 11.9 %collective-permute-start.7 = (f32[72,1024]{1,0:T(8,128)S(1)}, f32[72,1024]{1,0:T(8,128)S(1)}, u32[]{:S(2)}, u32[]{:S(2)}) collective-permute-start(f32[72,1024]{1,0:T(8,128)S(1)} %shard_map.62), channel_id=1, source_target_pairs={{0,2},{1,3},{2,4},{3,5},{4,6},{5,7},{6,8},{7,9},{8,10},{9,11},{10,... | collective-permute-start | bytes 884744 | tf_op jit(solution)/shard_map/ppermute | solution.py:192

commit v3 on v2

v3 whole, which is shorter than its diff:
```python
import functools

import jax
import jax.numpy as jnp
from jax import lax
from jax.experimental import pallas as pl
from jax.experimental.pallas import tpu as pltpu
from jax.sharding import PartitionSpec as P

WIN = 4
HALF = WIN // 2
PAD = 8
PIECES = 4
VMEM = pl.BlockSpec(memory_space=pltpu.VMEM)
ANY = pl.BlockSpec(memory_space=pl.ANY)


def swapped(block, bit):
    count = lax.axis_size("step")
    return lax.ppermute(block, "step", [(i, i ^ bit) for i in range(count)])


def product_nt(left, right):
    return lax.dot_general(left, right, (((1,), (1,)), ((), ())), preferred_element_type=jnp.float32)


def high_low(value):
    high = value.astype(jnp.bfloat16)
    return high, (value - high.astype(jnp.float32)).astype(jnp.bfloat16)


def stacked(x):
    high = x.astype(jnp.bfloat16).astype(jnp.float32)
    return jnp.concatenate([high, x - high], 0).astype(jnp.bfloat16)


def times(both, high, low):
    rows = both.shape[0] // 2
    wide = product_nt(both, high)
    narrow = product_nt(both[: (rows + 15) // 16 * 16], low)
    return wide[:rows] + wide[rows:] + narrow[:rows]


def one_row(at, value):
    row = lax.broadcasted_iota(jnp.int32, (PAD, value.shape[1]), 0)
    return jnp.where(row == at, value, 0.0)


def own_kernel(own_p, maps):
    maps[0], maps[1] = high_low(own_p[...])


def whole_start(vectors, width):
    place = lax.axis_index("step") % WIN
    ordered = []
    for j in range(WIN):
        pick = vectors[0][:, :width]
        for flip in range(1, WIN):
            pick = jnp.where(j ^ place == flip, vectors[flip][:, :width], pick)
        ordered.append(pick)
    return jnp.concatenate(ordered, 1)


def on_second_chip():
    return lax.axis_index("step") % WIN >= HALF


def by_place(body):
    place = lax.axis_index("step") % WIN
    for k in range(WIN):
        pl.when(place == k)(functools.partial(body, k // 2, k % 2))


def product_rows(later, earlier_high, earlier_low):
    rows = later.shape[0]
    both = stacked(later)
    dot = functools.partial(jnp.dot, preferred_element_type=jnp.float32)
    wide = dot(both, earlier_high)
    return wide[:rows] + wide[rows:] + dot(both[:rows], earlier_low)


def joint_rows(joint, low, later, earlier):
    order = later.shape[0]
    part = order // PIECES
    for at in range(0, joint.shape[1], part):
        block = later[low + at : low + at + part]
        joint[0, at : at + part], joint[1, at : at + part] = high_low(product_rows(block, earlier[0], earlier[1]))


def other_kernel(own, own_p, other_p, other, joint):
    other[0], other[1] = high_low(other_p[...])

    def body(chip, core):
        if chip == 1:
            joint_rows(joint, 0, (other_p, own_p)[core], (own, other)[core])

    by_place(body)


def first_kernel(mirror_v, own_v, v0, v1, v2, v3, own, other, own_p, other_p, out_b, out_a, state, joint):
    order = other_p.shape[0]
    rows = out_b.shape[0]
    vectors = (v0[...], v1[...], v2[...], v3[...])
    width = v0.shape[1] - order

    def body(chip, core):
        if chip == 0:
            x = jnp.concatenate([one_row(0, whole_start(vectors, width)), mirror_v[...], own_v[...]], 0)
            for step in range(2):
                maps = (own, other)[step ^ core]
                y = times(stacked(x), maps[0], maps[1])
                x = jnp.concatenate([y[:PAD] + one_row(0, vectors[step ^ core][:, width:]), y[PAD:]], 0)
            state[...] = x[:1]
            out_b[...] = x[PAD : PAD + rows]
            out_a[...] = x[PAD + rows :]
        else:
            joint_rows(joint, joint.shape[1], (other_p, own_p)[core], (own, other)[core])

    by_place(body)


def joint_kernel(v0, v1, own, other, own_p, other_p, joint, joint_f):
    order = own_p.shape[0]
    width = v0.shape[1] - order
    lanes = 128

    def body(chip, core):
        if chip == 0:
            return
        later = (other_p, own_p)[core]
        joint_rows(joint, order - joint.shape[1], later, (own, other)[core])
        first_f, second_f = [(v0, v1)[k ^ core][:, width:] for k in range(2)]
        part = order // PIECES
        for at in range(0, order, part):
            pushed = later[at : at + part] * first_f
            total = pushed[:, :lanes]
            for k in range(lanes, order, lanes):
                total = total + pushed[:, k : k + lanes]
            joint_f[:, at : at + part] = (
                jnp.sum(total.T, axis=0, keepdims=True) + second_f[:, at : at + part]
            )

    by_place(body)


def joint_times(x, parts):
    both = stacked(x)
    return jnp.concatenate([times(both, part[0], part[1]) for part in parts], 1)


def state_rows_kernel(got, state, joint_f, part_0, part_1, part_2, out):
    @pl.when(on_second_chip())
    def _():
        x = jnp.concatenate([one_row(0, state[...]), got[...]], 0)
        y = joint_times(x, (part_0, part_1, part_2))
        out[:PAD] = y[:PAD] + one_row(0, joint_f[...])
        out[PAD:] = y[PAD:]


def rows_kernel(got, part_0, part_1, part_2, out):
    @pl.when(on_second_chip())
    def _():
        out[...] = joint_times(got[...], (part_0, part_1, part_2))


def slice_of(end, place, width):
    mine = end[:, :width]
    for j in range(1, WIN):
        mine = jnp.where(place == j, end[:, j * width : (j + 1) * width], mine)
    return mine


def near_kernel(came, starts, directions, residual, jacobian, end):
    place = lax.axis_index("step") % WIN
    mine = place >= HALF
    end[...] = came[:1]
    jacobian[...] = jnp.where(mine, came[PAD:], 0.0) - directions[...]
    residual[...] = jnp.where(mine, slice_of(came[:1], place, starts.shape[1]), 0.0) - starts[...]


def far_kernel(came, end, residual_in, jacobian_in, residual, jacobian):
    place = lax.axis_index("step") % WIN
    mine = place < HALF
    jacobian[...] = jnp.where(mine, came[...], 0.0) + jacobian_in[...]
    residual[...] = jnp.where(mine, slice_of(end[...], place, residual.shape[1]), 0.0) + residual_in[...]


def call(body, micros, out_shape, *args, specs=None, scratch=(), after=()):
    count, extra = len(args), len(after)

    def run(*refs):
        body(*refs[:count], *refs[count + extra :])

    return pl.pallas_call(
        run,
        out_shape=out_shape,
        in_specs=(specs or [VMEM] * count) + [ANY] * extra,
        out_specs=jax.tree.map(lambda _: VMEM, out_shape),
        scratch_shapes=scratch,
        compiler_params=pltpu.CompilerParams(vmem_limit_bytes=20 << 20),
        cost_estimate=pl.CostEstimate(flops=int(micros * 1e9), bytes_accessed=1, transcendentals=0),
    )(*args, *after)


def local(propagators, forcing, starts, directions):
    own_p, own_v = propagators[0], directions[0]
    order = own_p.shape[0]
    rows = own_v.shape[0]
    steps = lax.axis_size("step")
    block = jax.ShapeDtypeStruct((rows, order), jnp.float32)
    row = jax.ShapeDtypeStruct((1, order), jnp.float32)

    def split(height):
        return jax.ShapeDtypeStruct((2, height, order), jnp.bfloat16)

    other_p = swapped(own_p, 1)
    mirror_v = swapped(own_v, 2)
    vector = jnp.concatenate([starts, forcing], 1)
    vectors = [vector] + [swapped(vector, k) for k in range(1, WIN)]
    own = call(own_kernel, 0.01, split(order), own_p)
    other, part_0 = call(other_kernel, 0.01, [split(order), split(order // 4)], own, own_p, other_p)
    x_b, x_a, state, part_1 = call(
        first_kernel, 3, [block, block, row, split(order // 4)], mirror_v, own_v, *vectors, own, other, own_p, other_p
    )
    got_b, got_a, got_state = swapped(x_b, 2), swapped(x_a, 2), swapped(state, 2)
    part_2, joint_f = call(
        joint_kernel, 1, [split(order // 2), row], *vectors[:2], own, other, own_p, other_p, after=(x_b,)
    )
    joint = part_0, part_1, part_2
    y_b = call(state_rows_kernel, 2, jax.ShapeDtypeStruct((PAD + rows, order), jnp.float32), got_b, got_state, joint_f, *joint)
    to_near = [(i, (i + WIN) % steps if i % WIN >= HALF else i ^ 1) for i in range(steps)]
    to_far = [(i, (i + WIN - HALF) % steps if i % WIN >= HALF else i + HALF) for i in range(steps)]
    near = lax.ppermute(y_b, "step", to_near)
    y_a = call(rows_kernel, 2, block, got_a, *joint, after=(y_b,))
    far = lax.ppermute(y_a, "step", to_far)
    results = [jax.ShapeDtypeStruct(starts.shape, jnp.float32), block]
    *sums, end = call(near_kernel, 1, results + [row], near, starts, own_v)
    residual, jacobian = call(far_kernel, 1, results, far, swapped(end, 2), *sums)
    return residual, jacobian[None]


def solution(mesh):
    return jax.shard_map(
        local,
        mesh=mesh,
        in_specs=(
            P(("parts", "step"), None, None),
            P(("parts", "step"), None),
            P(("parts", "step"), None),
            P(("parts", "step"), None, None),
        ),
        out_specs=(P(("parts", "step"), None), P(("parts", "step"), None, None)),
        check_vma=False,
    )
```

time: 44.1 us -> 41.5 us (0.941)
  starting transfers between devices: 8.92 us -> 16.9 us
  waiting for transfers between devices: 20.8 us -> 15.2 us
  Pallas kernels: 9.85 us -> 4.96 us
    ppermute x7 -> x9, starting transfers between devices: 7.06 us -> 13.8 us  [swapped(): return lax.ppermute(block, 'step', [(i, i ^ bit) for i in range(count)])]
    ppermute x2, waiting for transfers between devices: 10 us -> 4.33 us  [the longest x1 4.32 us: local(): far = lax.ppermute(y_a, 'step', to_far)]
    pallas_call x6 -> x8, Pallas kernels: 9.85 us -> 4.96 us  [call(): pl.pallas_call(run, out_shape=out_shape, in_specs=(specs or [VMEM] * coun...]
    ppermute x2, starting transfers between devices: 1.85 us -> 3.03 us  [the longest x1 3.03 us: local(): far = lax.ppermute(y_a, 'step', to_far)]
    ppermute x7 -> x9, waiting for transfers between devices: 10.8 us -> 10.9 us  [swapped(): return lax.ppermute(block, 'step', [(i, i ^ bit) for i in range(count)])]
  transfers between devices with their start and end apart: 9 -> 11, of which waited for: 5 -> 5; matrix products, arithmetic and copies ran while one was open for 3% -> 3% of each run, Pallas kernels for 14% -> 4%
where the time goes in v3:
time: 41.5 us; the launch traced here: 41.3 us
  starting transfers between devices  16.9 us (41%)
  waiting for transfers between devices  15.2 us (37%)
  Pallas kernels  4.96 us (12%)
  local copies, waits for them, and re-layouts  3.57 us (9%)
  between operations  0.7 us (2%)
    ppermute x9, starting transfers between devices, swapped(): return lax.ppermute(block, 'step', [(i, i ^ bit) for i in range(count)])  13.8 us
    ppermute x9, waiting for transfers between devices, swapped(): return lax.ppermute(block, 'step', [(i, i ^ bit) for i in range(count)])  10.9 us
    pallas_call x8, Pallas kernels, call(): pl.pallas_call(run, out_shape=out_shape, in_specs=(specs or [VMEM] * coun...  4.96 us
    ppermute x1, waiting for transfers between devices, local(): far = lax.ppermute(y_a, 'step', to_far)  4.32 us
    ppermute x1, starting transfers between devices, local(): far = lax.ppermute(y_a, 'step', to_far)  3.03 us
    unnamed x7, local copies, waits for them, and re-layouts  2.88 us
  transfers between devices with their start and end apart: 11, of which 5 were waited for; matrix products, arithmetic and copies ran while one was open for 3% of the time, Pallas kernels for 4%

profile of v3, /device:TPU:0, one launch (start us, length us, event | category | flops | bytes accessed | tf_op | source)
XLA Modules:
  0.0 41.3 jit_solution(16701493082689425000)
XLA Ops:
  0.6 0.5 %collective-permute-start.4 = (f32[1024,1024]{1,0:T(8,128)}, f32[1024,1024]{1,0:T(8,128)S(1)}, u32[]{:S(2)}, u32[]{:S(2)}) collective-permute-start(f32[1024,1024]{1,0:T(8,128)} %bitcast.3), channel_id=1, source_target_pairs={{0,1},{1,0},{2,3},{3,2},{4,5},{5,4},{6,7},{7,6},{8,9},{9,8},{10,11... | collective-permute-start | bytes 12582920 | tf_op jit(solution)/shard_map/ppermute | solution.py:20
  1.1 2.6 %collective-permute-start = (f32[64,1024]{1,0:T(8,128)}, f32[64,1024]{1,0:T(8,128)S(1)}, u32[]{:S(2)}, u32[]{:S(2)}) collective-permute-start(f32[64,1024]{1,0:T(8,128)} %bitcast.8), channel_id=1, source_target_pairs={{0,2},{1,3},{2,0},{3,1},{4,6},{5,7},{6,4},{7,5},{8,10},{9,11},{10,... | collective-permute-start | bytes 786440 | tf_op jit(solution)/shard_map/ppermute | solution.py:20
  3.7 0.7 %constant_dynamic-update-slice_fusion.1 = f32[1,1280]{1,0:T(1,128)S(1)} fusion(f32[1,256]{1,0:T(1,128)} %refs_1_.1), kind=kLoop, calls=%fused_computation.1 | loop fusion | bytes 2048
  4.4 0.7 %constant_dynamic-update-slice_fusion.refs_2_.refs_0_ = f32[1,1280]{1,0:T(1,128)S(1)} fusion(f32[1,1280]{1,0:T(1,128)S(1)} %constant_dynamic-update-slice_fusion.1, f32[1,1024]{1,0:T(1,128)} %param.5), kind=kLoop, calls=%fused_computation | loop fusion | bytes 8192 | tf_op jit(solution)/shard_map/concatenate | solution.py:218
  5.1 0.1 collective-permute-start.3
  5.2 1.7 %collective-permute-start.2 = (f32[1,1280]{1,0:T(1,128)S(1)}, f32[1,1280]{1,0:T(1,128)S(1)}, u32[]{:S(2)}, u32[]{:S(2)}) collective-permute-start(f32[1,1280]{1,0:T(1,128)S(1)} %constant_dynamic-update-slice_fusion.refs_2_.refs_0_), channel_id=1, source_target_pairs={{0,2},{1,3},{2,0},{3,1},{4,6},{5,7},{6,4},{7,5},{8,10},{9,11},{10,... | collective-permute-start | bytes 15368 | tf_op jit(solution)/shard_map/ppermute | solution.py:20
  6.9 0.1 collective-permute-start.1
  7.0 2.2 %copy-done = f32[1,1024,1024]{2,1,0:T(8,128)S(1)} copy-done((f32[1,1024,1024]{2,1,0:T(8,128)S(1)}, f32[1,1024,1024]{2,1,0:T(8,128)}, u32[]{:S(2)}) %copy-start) | copy-done | bytes 4194328
  9.2 0.7 %shard_map.59.refs_0_.refs_6_.refs_2_ = bf16[2,1024,1024]{2,1,0:T(8,128)(2,1)S(1)} custom-call(f32[1024,1024]{1,0:T(8,128)S(1)} %bitcast.4), custom_call_target="tpu_custom_call" | custom-call | flops 10000000 | bytes 1 | tf_op jit(solution)/shard_map/pallas_call | solution.py:194
  9.9 0.0 copy-start.1
  9.9 0.0 collective-permute-done.4.refs_2_.refs_9_.refs_5_
  9.9 0.7 %shard_map.60 = (bf16[2,1024,1024]{2,1,0:T(8,128)(2,1)S(1)}, bf16[2,256,1024]{2,1,0:T(8,128)(2,1)S(1)}) custom-call(bf16[2,1024,1024]{2,1,0:T(8,128)(2,1)S(1)} %shard_map.59.refs_0_.refs_6_.refs_2_, f32[1024,1024]{1,0:T(8,128)S(1)} %bitcast.5, f32[1024,1024]{1,0:T(8,128)S(1)} %collective-permute-done.4.refs_2_.refs_9_.refs_5_), custom_call_target="tpu_custom_call" | custom-call | flops 10000000 | bytes 1 | tf_op jit(solution)/shard_map/pallas_call | solution.py:194
  10.6 0.1 collective-permute-done.3.refs_5_
  10.7 0.4 collective-permute-done.2.refs_4_
  11.1 0.0 collective-permute-done.1.refs_3_.refs_1_
  11.1 0.0 collective-permute-done.refs_0_
  11.1 0.0 copy-done.1
  11.1 2.8 %shard_map.61 = (f32[64,1024]{1,0:T(8,128)S(1)}, f32[64,1024]{1,0:T(8,128)S(1)}, f32[1,1024]{1,0:T(1,128)S(1)}, bf16[2,256,1024]{2,1,0:T(8,128)(2,1)S(1)}) custom-call(f32[64,1024]{1,0:T(8,128)S(1)} %collective-permute-done.refs_0_, f32[64,1024]{1,0:T(8,128)S(1)} %bitcast.9, f32[1,1280]{1,0:T(1,128)S(1)} %constant_dynamic-update-slice_fusion.refs_2_.refs_0_, ...), custom_call_target="tpu_custom_call" | custom-call | flops 3000000000 | bytes 1 | tf_op jit(solution)/shard_map/pallas_call | solution.py:194
  13.8 1.7 %collective-permute-start.6 = (f32[64,1024]{1,0:T(8,128)S(1)}, f32[64,1024]{1,0:T(8,128)S(1)}, u32[]{:S(2)}, u32[]{:S(2)}) collective-permute-start(f32[64,1024]{1,0:T(8,128)S(1)} %get-tuple-element.19.refs_6_), channel_id=1, source_target_pairs={{0,2},{1,3},{2,0},{3,1},{4,6},{5,7},{6,4},{7,5},{8,10},{9,11},{10,... | collective-permute-start | bytes 786440 | tf_op jit(solution)/shard_map/ppermute | solution.py:20
  15.6 0.4 collective-permute-start.7
  15.9 1.6 %collective-permute-start.5 = (f32[64,1024]{1,0:T(8,128)S(1)}, f32[64,1024]{1,0:T(8,128)S(1)}, u32[]{:S(2)}, u32[]{:S(2)}) collective-permute-start(f32[64,1024]{1,0:T(8,128)S(1)} %get-tuple-element.16), channel_id=1, source_target_pairs={{0,2},{1,3},{2,0},{3,1},{4,6},{5,7},{6,4},{7,5},{8,10},{9,11},{10,... | collective-permute-start | bytes 786440 | tf_op jit(solution)/shard_map/ppermute | solution.py:20
  17.6 5.6 %collective-permute-done.7.refs_1_ = f32[1,1024]{1,0:T(1,128)S(1)} collective-permute-done((f32[1,1024]{1,0:T(1,128)S(1)}, f32[1,1024]{1,0:T(1,128)S(1)}, u32[]{:S(2)}, u32[]{:S(2)}) %collective-permute-start.7) | collective-permute-done | bytes 4128 | tf_op jit(solution)/shard_map/ppermute | solution.py:20
  23.1 0.0 collective-permute-done.6.refs_0_
  23.2 0.0 collective-permute-start.9
  23.2 4.8 %collective-permute-done.5.refs_0_ = f32[64,1024]{1,0:T(8,128)S(1)} collective-permute-done((f32[64,1024]{1,0:T(8,128)S(1)}, f32[64,1024]{1,0:T(8,128)S(1)}, u32[]{:S(2)}, u32[]{:S(2)}) %collective-permute-start.5) | collective-permute-done | bytes 262176 | tf_op jit(solution)/shard_map/ppermute | solution.py:20
  28.0 3.0 %collective-permute-start.8 = (f32[64,1024]{1,0:T(8,128)S(1)}, f32[64,1024]{1,0:T(8,128)S(1)}, u32[]{:S(2)}, u32[]{:S(2)}) collective-permute-start(f32[64,1024]{1,0:T(8,128)S(1)} %shard_map.64), channel_id=1, source_target_pairs={{0,2},{1,3},{2,4},{3,5},{4,6},{5,7},{6,8},{7,9},{8,10},{9,11},{10,... | collective-permute-start | bytes 786440 | tf_op jit(solution)/shard_map/ppermute | solution.py:235
  31.0 0.0 collective-permute-done.9.refs_0_
  31.0 0.0 copy-done.2
  31.1 5.1 %collective-permute-start.10 = (f32[1,1024]{1,0:T(1,128)S(1)}, f32[1,1024]{1,0:T(1,128)S(1)}, u32[]{:S(2)}, u32[]{:S(2)}) collective-permute-start(f32[1,1024]{1,0:T(1,128)S(1)} %get-tuple-element.23), channel_id=1, source_target_pairs={{0,2},{1,3},{2,0},{3,1},{4,6},{5,7},{6,4},{7,5},{8,10},{9,11},{10,... | collective-permute-start | bytes 12296 | tf_op jit(solution)/shard_map/ppermute | solution.py:20
  36.2 4.3 %collective-permute-done.8.refs_0_ = f32[64,1024]{1,0:T(8,128)S(1)} collective-permute-done((f32[64,1024]{1,0:T(8,128)S(1)}, f32[64,1024]{1,0:T(8,128)S(1)}, u32[]{:S(2)}, u32[]{:S(2)}) %collective-permute-start.8) | collective-permute-done | bytes 262176 | tf_op jit(solution)/shard_map/ppermute | solution.py:235
  40.5 0.0 collective-permute-done.10.refs_1_
  40.5 0.7 %shard_map.66 = (f32[1,256]{1,0:T(1,128)}, f32[64,1024]{1,0:T(8,128)}) custom-call(f32[64,1024]{1,0:T(8,128)S(1)} %collective-permute-done.8.refs_0_, f32[1,1024]{1,0:T(1,128)S(1)} %collective-permute-done.10.refs_1_, f32[1,256]{1,0:T(1,128)S(1)} %get-tuple-element.24.refs_2_, f32[64,1024]{1,0:T(8,128)S(1)} %get-tuple-element.25.refs_3_), custom_call_target="tpu_custom_call" | custom-call | flops 1000000000 | bytes 1 | tf_op jit(solution)/shard_map/pallas_call | solution.py:194
  (6 shorter events, 0.0 us)
Async XLA Ops:
  0.6 9.3 %collective-permute-start.4 = (f32[1024,1024]{1,0:T(8,128)}, f32[1024,1024]{1,0:T(8,128)S(1)}, u32[]{:S(2)}, u32[]{:S(2)}) collective-permute-start(f32[1024,1024]{1,0:T(8,128)} %bitcast.3), channel_id=1, source_target_pairs={{0,1},{1,0},{2,3},{3,2},{4,5},{5,4},{6,7},{7,6},{8,9},{9,8},{10,11... | collective-permute-start | bytes 12582920 | tf_op jit(solution)/shard_map/ppermute | solution.py:20
  1.1 9.9 %collective-permute-start = (f32[64,1024]{1,0:T(8,128)}, f32[64,1024]{1,0:T(8,128)S(1)}, u32[]{:S(2)}, u32[]{:S(2)}) collective-permute-start(f32[64,1024]{1,0:T(8,128)} %bitcast.8), channel_id=1, source_target_pairs={{0,2},{1,3},{2,0},{3,1},{4,6},{5,7},{6,4},{7,5},{8,10},{9,11},{10,... | collective-permute-start | bytes 786440 | tf_op jit(solution)/shard_map/ppermute | solution.py:20
  5.1 5.6 %collective-permute-start.3 = (f32[1,1280]{1,0:T(1,128)S(1)}, f32[1,1280]{1,0:T(1,128)S(1)}, u32[]{:S(2)}, u32[]{:S(2)}) collective-permute-start(f32[1,1280]{1,0:T(1,128)S(1)} %constant_dynamic-update-slice_fusion.refs_2_.refs_0_), channel_id=1, source_target_pairs={{0,3},{1,2},{2,1},{3,0},{4,7},{5,6},{6,5},{7,4},{8,11},{9,10},{10,... | collective-permute-start | bytes 15368 | tf_op jit(solution)/shard_map/ppermute | solution.py:20
  5.2 5.9 %collective-permute-start.2 = (f32[1,1280]{1,0:T(1,128)S(1)}, f32[1,1280]{1,0:T(1,128)S(1)}, u32[]{:S(2)}, u32[]{:S(2)}) collective-permute-start(f32[1,1280]{1,0:T(1,128)S(1)} %constant_dynamic-update-slice_fusion.refs_2_.refs_0_), channel_id=1, source_target_pairs={{0,2},{1,3},{2,0},{3,1},{4,6},{5,7},{6,4},{7,5},{8,10},{9,11},{10,... | collective-permute-start | bytes 15368 | tf_op jit(solution)/shard_map/ppermute | solution.py:20
  6.9 4.2 %collective-permute-start.1 = (f32[1,1280]{1,0:T(1,128)S(1)}, f32[1,1280]{1,0:T(1,128)S(1)}, u32[]{:S(2)}, u32[]{:S(2)}) collective-permute-start(f32[1,1280]{1,0:T(1,128)S(1)} %constant_dynamic-update-slice_fusion.refs_2_.refs_0_), channel_id=1, source_target_pairs={{0,1},{1,0},{2,3},{3,2},{4,5},{5,4},{6,7},{7,6},{8,9},{9,8},{10,11... | collective-permute-start | bytes 15368 | tf_op jit(solution)/shard_map/ppermute | solution.py:20
  7.0 2.2 %copy-start = (f32[1,1024,1024]{2,1,0:T(8,128)S(1)}, f32[1,1024,1024]{2,1,0:T(8,128)}, u32[]{:S(2)}) copy-start(f32[1,1024,1024]{2,1,0:T(8,128)} %param.4) | copy-start | bytes 12582916
  9.9 1.2 %copy-start.1 = (f32[1,64,1024]{2,1,0:T(8,128)S(1)}, f32[1,64,1024]{2,1,0:T(8,128)}, u32[]{:S(2)}) copy-start(f32[1,64,1024]{2,1,0:T(8,128)} %param.7) | copy-start | bytes 786436
  13.8 9.3 %collective-permute-start.6 = (f32[64,1024]{1,0:T(8,128)S(1)}, f32[64,1024]{1,0:T(8,128)S(1)}, u32[]{:S(2)}, u32[]{:S(2)}) collective-permute-start(f32[64,1024]{1,0:T(8,128)S(1)} %get-tuple-element.19.refs_6_), channel_id=1, source_target_pairs={{0,2},{1,3},{2,0},{3,1},{4,6},{5,7},{6,4},{7,5},{8,10},{9,11},{10,... | collective-permute-start | bytes 786440 | tf_op jit(solution)/shard_map/ppermute | solution.py:20
  15.6 7.6 %collective-permute-start.7 = (f32[1,1024]{1,0:T(1,128)S(1)}, f32[1,1024]{1,0:T(1,128)S(1)}, u32[]{:S(2)}, u32[]{:S(2)}) collective-permute-start(f32[1,1024]{1,0:T(1,128)S(1)} %get-tuple-element.21), channel_id=1, source_target_pairs={{0,2},{1,3},{2,0},{3,1},{4,6},{5,7},{6,4},{7,5},{8,10},{9,11},{10,... | collective-permute-start | bytes 12296 | tf_op jit(solution)/shard_map/ppermute | solution.py:20
  15.9 12.1 %collective-permute-start.5 = (f32[64,1024]{1,0:T(8,128)S(1)}, f32[64,1024]{1,0:T(8,128)S(1)}, u32[]{:S(2)}, u32[]{:S(2)}) collective-permute-start(f32[64,1024]{1,0:T(8,128)S(1)} %get-tuple-element.16), channel_id=1, source_target_pairs={{0,2},{1,3},{2,0},{3,1},{4,6},{5,7},{6,4},{7,5},{8,10},{9,11},{10,... | collective-permute-start | bytes 786440 | tf_op jit(solution)/shard_map/ppermute | solution.py:20
  23.1 7.9 %copy-start.2 = (f32[1,256]{1,0:T(1,128)S(1)}, f32[1,256]{1,0:T(1,128)}, u32[]{:S(2)}) copy-start(f32[1,256]{1,0:T(1,128)} %refs_1_.1) | copy-start | bytes 3076
  23.2 7.9 %collective-permute-start.9 = (f32[72,1024]{1,0:T(8,128)S(1)}, f32[72,1024]{1,0:T(8,128)S(1)}, u32[]{:S(2)}, u32[]{:S(2)}) collective-permute-start(f32[72,1024]{1,0:T(8,128)S(1)} %shard_map.63.refs_4_), channel_id=1, source_target_pairs={{0,1},{1,0},{2,6},{3,7},{4,5},{5,4},{6,10},{7,11},{8,9},{9,8},{10,... | collective-permute-start | bytes 884744 | tf_op jit(solution)/shard_map/ppermute | solution.py:233
  28.0 12.5 %collective-permute-start.8 = (f32[64,1024]{1,0:T(8,128)S(1)}, f32[64,1024]{1,0:T(8,128)S(1)}, u32[]{:S(2)}, u32[]{:S(2)}) collective-permute-start(f32[64,1024]{1,0:T(8,128)S(1)} %shard_map.64), channel_id=1, source_target_pairs={{0,2},{1,3},{2,4},{3,5},{4,6},{5,7},{6,8},{7,9},{8,10},{9,11},{10,... | collective-permute-start | bytes 786440 | tf_op jit(solution)/shard_map/ppermute | solution.py:235
  31.1 9.4 %collective-permute-start.10 = (f32[1,1024]{1,0:T(1,128)S(1)}, f32[1,1024]{1,0:T(1,128)S(1)}, u32[]{:S(2)}, u32[]{:S(2)}) collective-permute-start(f32[1,1024]{1,0:T(1,128)S(1)} %get-tuple-element.23), channel_id=1, source_target_pairs={{0,2},{1,3},{2,0},{3,1},{4,6},{5,7},{6,4},{7,5},{8,10},{9,11},{10,... | collective-permute-start | bytes 12296 | tf_op jit(solution)/shard_map/ppermute | solution.py:20

commit v4 on v3

--- a/solution.py
+++ b/solution.py
@@ -11,6 +11,8 @@
 HALF = WIN // 2
 PAD = 8
 PIECES = 4
+NEAR_PIECES = 2
+FAR_PIECES = 2
 VMEM = pl.BlockSpec(memory_space=pltpu.VMEM)
 ANY = pl.BlockSpec(memory_space=pl.ANY)
 
@@ -47,7 +49,9 @@
 
 
 def own_kernel(own_p, maps):
-    maps[0], maps[1] = high_low(own_p[...])
+    @pl.when(on_second_chip())
+    def _():
+        maps[0], maps[1] = high_low(own_p[...])
 
 
 def whole_start(vectors, width):
@@ -71,6 +75,13 @@
         pl.when(place == k)(functools.partial(body, k // 2, k % 2))
 
 
+def split_times(x, matrix):
+    order = matrix.shape[0]
+    part = order // PIECES
+    both = stacked(x)
+    return jnp.concatenate([times(both, *high_low(matrix[k * part : (k + 1) * part])) for k in range(PIECES)], 1)
+
+
 def product_rows(later, earlier_high, earlier_low):
     rows = later.shape[0]
     both = stacked(later)
@@ -79,27 +90,23 @@
     return wide[:rows] + wide[rows:] + dot(both[:rows], earlier_low)
 
 
-def joint_rows(joint, low, later, earlier):
-    order = later.shape[0]
-    part = order // PIECES
-    for at in range(0, joint.shape[1], part):
-        block = later[low + at : low + at + part]
-        joint[0, at : at + part], joint[1, at : at + part] = high_low(product_rows(block, earlier[0], earlier[1]))
-
-
-def other_kernel(own, own_p, other_p, other, joint):
-    other[0], other[1] = high_low(other_p[...])
+def other_kernel(own, own_p, other_p, half, other):
+    rows = half.shape[0]
+    part = rows // 2
 
     def body(chip, core):
         if chip == 1:
-            joint_rows(joint, 0, (other_p, own_p)[core], (own, other)[core])
+            other[0], other[1] = high_low(other_p[...])
+            earlier, later = (own, other)[core], (other_p, own_p)[core]
+            for at in range(0, rows, part):
+                block = later[rows * core + at : rows * core + at + part]
+                half[at : at + part] = product_rows(block, earlier[0], earlier[1])
 
     by_place(body)
 
 
-def first_kernel(mirror_v, own_v, v0, v1, v2, v3, own, other, own_p, other_p, out_b, out_a, state, joint):
-    order = other_p.shape[0]
-    rows = out_b.shape[0]
+def first_kernel(mirror_v, own_v, v0, v1, v2, v3, own_p, other_p, state, *outs):
+    order = mirror_v.shape[1]
     vectors = (v0[...], v1[...], v2[...], v3[...])
     width = v0.shape[1] - order
 
@@ -107,28 +114,30 @@
         if chip == 0:
             x = jnp.concatenate([one_row(0, whole_start(vectors, width)), mirror_v[...], own_v[...]], 0)
             for step in range(2):
-                maps = (own, other)[step ^ core]
-                y = times(stacked(x), maps[0], maps[1])
+                y = split_times(x, (own_p, other_p)[step ^ core])
                 x = jnp.concatenate([y[:PAD] + one_row(0, vectors[step ^ core][:, width:]), y[PAD:]], 0)
             state[...] = x[:1]
-            out_b[...] = x[PAD : PAD + rows]
-            out_a[...] = x[PAD + rows :]
-        else:
-            joint_rows(joint, joint.shape[1], (other_p, own_p)[core], (own, other)[core])
+            at = PAD
+            for out in outs:
+                out[...] = x[at : at + out.shape[0]]
+                at += out.shape[0]
 
     by_place(body)
 
 
-def joint_kernel(v0, v1, own, other, own_p, other_p, joint, joint_f):
+def joint_kernel(v0, v1, own_p, other_p, own_half, other_half, joint, joint_f):
     order = own_p.shape[0]
+    rows = own_half.shape[0]
     width = v0.shape[1] - order
     lanes = 128
 
     def body(chip, core):
         if chip == 0:
             return
+        for k, part in enumerate((own_half, other_half)):
+            at = rows * (k ^ core)
+            joint[0, at : at + rows], joint[1, at : at + rows] = high_low(part[...])
         later = (other_p, own_p)[core]
-        joint_rows(joint, order - joint.shape[1], later, (own, other)[core])
         first_f, second_f = [(v0, v1)[k ^ core][:, width:] for k in range(2)]
         part = order // PIECES
         for at in range(0, order, part):
@@ -143,24 +152,19 @@
     by_place(body)
 
 
-def joint_times(x, parts):
-    both = stacked(x)
-    return jnp.concatenate([times(both, part[0], part[1]) for part in parts], 1)
-
-
-def state_rows_kernel(got, state, joint_f, part_0, part_1, part_2, out):
+def state_rows_kernel(got, state, joint, joint_f, out):
     @pl.when(on_second_chip())
     def _():
         x = jnp.concatenate([one_row(0, state[...]), got[...]], 0)
-        y = joint_times(x, (part_0, part_1, part_2))
+        y = times(stacked(x), joint[0], joint[1])
         out[:PAD] = y[:PAD] + one_row(0, joint_f[...])
         out[PAD:] = y[PAD:]
 
 
-def rows_kernel(got, part_0, part_1, part_2, out):
+def rows_kernel(got, joint, out):
     @pl.when(on_second_chip())
     def _():
-        out[...] = joint_times(got[...], (part_0, part_1, part_2))
+        out[...] = times(stacked(got[...]), joint[0], joint[1])
 
 
 def slice_of(end, place, width):
@@ -170,18 +174,22 @@
     return mine
 
 
-def near_kernel(came, starts, directions, residual, jacobian, end):
+def near_kernel(*refs):
+    *came, starts, directions, residual, jacobian, end = refs
     place = lax.axis_index("step") % WIN
     mine = place >= HALF
-    end[...] = came[:1]
-    jacobian[...] = jnp.where(mine, came[PAD:], 0.0) - directions[...]
-    residual[...] = jnp.where(mine, slice_of(came[:1], place, starts.shape[1]), 0.0) - starts[...]
-
-
-def far_kernel(came, end, residual_in, jacobian_in, residual, jacobian):
+    end[...] = came[0][:1]
+    whole = jnp.concatenate([came[0][PAD:]] + [piece[...] for piece in came[1:]], 0)
+    jacobian[...] = jnp.where(mine, whole, 0.0) - directions[...]
+    residual[...] = jnp.where(mine, slice_of(came[0][:1], place, starts.shape[1]), 0.0) - starts[...]
+
+
+def far_kernel(*refs):
+    *came, end, residual_in, jacobian_in, residual, jacobian = refs
     place = lax.axis_index("step") % WIN
     mine = place < HALF
-    jacobian[...] = jnp.where(mine, came[...], 0.0) + jacobian_in[...]
+    whole = jnp.concatenate([piece[...] for piece in came], 0)
+    jacobian[...] = jnp.where(mine, whole, 0.0) + jacobian_in[...]
     residual[...] = jnp.where(mine, slice_of(end[...], place, residual.shape[1]), 0.0) + residual_in[...]
 
 
@@ -218,24 +226,33 @@
     vector = jnp.concatenate([starts, forcing], 1)
     vectors = [vector] + [swapped(vector, k) for k in range(1, WIN)]
     own = call(own_kernel, 0.01, split(order), own_p)
-    other, part_0 = call(other_kernel, 0.01, [split(order), split(order // 4)], own, own_p, other_p)
-    x_b, x_a, state, part_1 = call(
-        first_kernel, 3, [block, block, row, split(order // 4)], mirror_v, own_v, *vectors, own, other, own_p, other_p
+    half_rows = jax.ShapeDtypeStruct((order // 2, order), jnp.float32)
+    own_half = call(
+        other_kernel, 0.01, half_rows, own, own_p, other_p, scratch=[pltpu.VMEM((2, order, order), jnp.bfloat16)]
     )
-    got_b, got_a, got_state = swapped(x_b, 2), swapped(x_a, 2), swapped(state, 2)
-    part_2, joint_f = call(
-        joint_kernel, 1, [split(order // 2), row], *vectors[:2], own, other, own_p, other_p, after=(x_b,)
+    other_half = swapped(own_half, 1)
+    heights = [rows // NEAR_PIECES] * NEAR_PIECES + [rows // FAR_PIECES] * FAR_PIECES
+    pieces = [jax.ShapeDtypeStruct((height, order), jnp.float32) for height in heights]
+    state, *xs = call(first_kernel, 60, [row, *pieces], mirror_v, own_v, *vectors, own_p, other_p)
+    got_state = swapped(state, 2)
+    got = [swapped(x, 2) for x in xs]
+    joint, joint_f = call(
+        joint_kernel, 1, [split(order), row], *vectors[:2], own_p, other_p, own_half, other_half, after=(xs[0],)
     )
-    joint = part_0, part_1, part_2
-    y_b = call(state_rows_kernel, 2, jax.ShapeDtypeStruct((PAD + rows, order), jnp.float32), got_b, got_state, joint_f, *joint)
     to_near = [(i, (i + WIN) % steps if i % WIN >= HALF else i ^ 1) for i in range(steps)]
     to_far = [(i, (i + WIN - HALF) % steps if i % WIN >= HALF else i + HALF) for i in range(steps)]
-    near = lax.ppermute(y_b, "step", to_near)
-    y_a = call(rows_kernel, 2, block, got_a, *joint, after=(y_b,))
-    far = lax.ppermute(y_a, "step", to_far)
+    done = []
+    for k, x in enumerate(got):
+        if k == 0:
+            tall = jax.ShapeDtypeStruct((PAD + heights[0], order), jnp.float32)
+            done.append(call(state_rows_kernel, 2, tall, x, got_state, joint, joint_f))
+        else:
+            done.append(call(rows_kernel, 2, pieces[k], x, joint, after=done[-1:]))
+    near = [lax.ppermute(y, "step", to_near) for y in done[:NEAR_PIECES]]
+    far = [lax.ppermute(y, "step", to_far) for y in done[NEAR_PIECES:]]
     results = [jax.ShapeDtypeStruct(starts.shape, jnp.float32), block]
-    *sums, end = call(near_kernel, 1, results + [row], near, starts, own_v)
-    residual, jacobian = call(far_kernel, 1, results, far, swapped(end, 2), *sums)
+    *sums, end = call(near_kernel, 5, results + [row], *near, starts, own_v)
+    residual, jacobian = call(far_kernel, 1, results, *far, swapped(end, 2), *sums)
     return residual, jacobian[None]
 
 

time: 41.5 us -> 40 us (0.964)
  waiting for transfers between devices: 15.2 us -> 11.7 us
  starting transfers between devices: 16.9 us -> 19.9 us
  Pallas kernels: 4.96 us -> 3.64 us
    ppermute x9 -> x12, waiting for transfers between devices: 10.9 us -> 7.41 us  [swapped(): return lax.ppermute(block, 'step', [(i, i ^ bit) for i in range(count)])]
    ppermute x2 -> x4, starting transfers between devices: 3.03 us -> 5.57 us  [the longest x2 5.56 us: local(): far = [lax.ppermute(y, 'step', to_far) for y in done[NEAR_PIECES:]]]
    pallas_call x8 -> x10, Pallas kernels: 4.96 us -> 3.64 us  [call(): pl.pallas_call(run, out_shape=out_shape, in_specs=(specs or [VMEM] * coun...]
    ppermute x9 -> x12, starting transfers between devices: 13.8 us -> 14.3 us  [swapped(): return lax.ppermute(block, 'step', [(i, i ^ bit) for i in range(count)])]
    unnamed x7 -> x9, local copies, waits for them, and re-layouts: 2.88 us -> 3.23 us
    ppermute x2 -> x4, waiting for transfers between devices: 4.33 us -> 4.25 us  [the longest x2 4.24 us: local(): far = [lax.ppermute(y, 'step', to_far) for y in done[NEAR_PIECES:]]]
  transfers between devices with their start and end apart: 11 -> 16, of which waited for: 5 -> 5; matrix products, arithmetic and copies ran while one was open for 3% -> 3% of each run, Pallas kernels for 4% -> 7%
where the time goes in v4:
time: 40 us; the launch traced here: 39.8 us
  starting transfers between devices  19.9 us (50%)
  waiting for transfers between devices  11.7 us (29%)
  local copies, waits for them, and re-layouts  3.92 us (10%)
  Pallas kernels  3.64 us (9%)
  between operations  0.68 us (2%)
    ppermute x12, starting transfers between devices, swapped(): return lax.ppermute(block, 'step', [(i, i ^ bit) for i in range(count)])  14.3 us
    ppermute x12, waiting for transfers between devices, swapped(): return lax.ppermute(block, 'step', [(i, i ^ bit) for i in range(count)])  7.41 us
    ppermute x2, starting transfers between devices, local(): far = [lax.ppermute(y, 'step', to_far) for y in done[NEAR_PIECES:]]  5.56 us
    ppermute x2, waiting for transfers between devices, local(): far = [lax.ppermute(y, 'step', to_far) for y in done[NEAR_PIECES:]]  4.24 us
    pallas_call x10, Pallas kernels, call(): pl.pallas_call(run, out_shape=out_shape, in_specs=(specs or [VMEM] * coun...  3.64 us
    unnamed x9, local copies, waits for them, and re-layouts  3.23 us
  transfers between devices with their start and end apart: 16, of which 5 were waited for; matrix products, arithmetic and copies ran while one was open for 3% of the time, Pallas kernels for 7%

profile of v4, /device:TPU:0, one launch (start us, length us, event | category | flops | bytes accessed | tf_op | source)
XLA Modules:
  0.0 39.8 jit_solution(9418077242117593267)
XLA Ops:
  0.6 0.5 %collective-permute-start.4 = (f32[1024,1024]{1,0:T(8,128)}, f32[1024,1024]{1,0:T(8,128)S(1)}, u32[]{:S(2)}, u32[]{:S(2)}) collective-permute-start(f32[1024,1024]{1,0:T(8,128)} %bitcast.3), channel_id=1, source_target_pairs={{0,1},{1,0},{2,3},{3,2},{4,5},{5,4},{6,7},{7,6},{8,9},{9,8},{10,11... | collective-permute-start | bytes 12582920 | tf_op jit(solution)/shard_map/ppermute | solution.py:22
  1.1 2.6 %collective-permute-start = (f32[64,1024]{1,0:T(8,128)}, f32[64,1024]{1,0:T(8,128)S(1)}, u32[]{:S(2)}, u32[]{:S(2)}) collective-permute-start(f32[64,1024]{1,0:T(8,128)} %bitcast.8), channel_id=1, source_target_pairs={{0,2},{1,3},{2,0},{3,1},{4,6},{5,7},{6,4},{7,5},{8,10},{9,11},{10,... | collective-permute-start | bytes 786440 | tf_op jit(solution)/shard_map/ppermute | solution.py:22
  3.7 0.7 %constant_dynamic-update-slice_fusion.1 = f32[1,1280]{1,0:T(1,128)S(1)} fusion(f32[1,256]{1,0:T(1,128)} %refs_2_.1), kind=kLoop, calls=%fused_computation.1 | loop fusion | bytes 2048
  4.4 0.7 %constant_dynamic-update-slice_fusion.refs_2_.refs_0_ = f32[1,1280]{1,0:T(1,128)S(1)} fusion(f32[1,1280]{1,0:T(1,128)S(1)} %constant_dynamic-update-slice_fusion.1, f32[1,1024]{1,0:T(1,128)} %param.5), kind=kLoop, calls=%fused_computation | loop fusion | bytes 8192 | tf_op jit(solution)/shard_map/concatenate | solution.py:226
  5.1 0.2 collective-permute-start.1
  5.3 0.3 collective-permute-start.2
  5.5 1.4 %collective-permute-start.3 = (f32[1,1280]{1,0:T(1,128)S(1)}, f32[1,1280]{1,0:T(1,128)S(1)}, u32[]{:S(2)}, u32[]{:S(2)}) collective-permute-start(f32[1,1280]{1,0:T(1,128)S(1)} %constant_dynamic-update-slice_fusion.refs_2_.refs_0_), channel_id=1, source_target_pairs={{0,3},{1,2},{2,1},{3,0},{4,7},{5,6},{6,5},{7,4},{8,11},{9,10},{10,... | collective-permute-start | bytes 15368 | tf_op jit(solution)/shard_map/ppermute | solution.py:22
  7.0 2.2 %copy-done = f32[1,1024,1024]{2,1,0:T(8,128)S(1)} copy-done((f32[1,1024,1024]{2,1,0:T(8,128)S(1)}, f32[1,1024,1024]{2,1,0:T(8,128)}, u32[]{:S(2)}) %copy-start) | copy-done | bytes 4194328
  9.2 0.5 %collective-permute-start.6 = (f32[512,1024]{1,0:T(8,128)S(1)}, f32[512,1024]{1,0:T(8,128)S(1)}, u32[]{:S(2)}, u32[]{:S(2)}) collective-permute-start(f32[512,1024]{1,0:T(8,128)S(1)} %shard_map.61.refs_4_), channel_id=1, source_target_pairs={{0,1},{1,0},{2,3},{3,2},{4,5},{5,4},{6,7},{7,6},{8,9},{9,8},{10,11... | collective-permute-start | bytes 6291464 | tf_op jit(solution)/shard_map/ppermute | solution.py:22
  9.7 1.3 %collective-permute-done.2.refs_4_ = f32[1,1280]{1,0:T(1,128)S(1)} collective-permute-done((f32[1,1280]{1,0:T(1,128)S(1)}, f32[1,1280]{1,0:T(1,128)S(1)}, u32[]{:S(2)}, u32[]{:S(2)}) %collective-permute-start.2) | collective-permute-done | bytes 5152 | tf_op jit(solution)/shard_map/ppermute | solution.py:22
  11.0 0.0 collective-permute-done.3.refs_5_
  11.0 0.0 collective-permute-done.refs_0_
  11.0 0.3 copy-done.1
  11.4 0.0 copy-done.3
  11.4 2.8 %shard_map.59 = (f32[1,1024]{1,0:T(1,128)S(1)}, f32[32,1024]{1,0:T(8,128)S(1)}, f32[32,1024]{1,0:T(8,128)S(1)}, f32[32,1024]{1,0:T(8,128)S(1)}, f32[32,1024]{1,0:T(8,128)S(1)}) custom-call(f32[64,1024]{1,0:T(8,128)S(1)} %collective-permute-done.refs_0_, f32[64,1024]{1,0:T(8,128)S(1)} %bitcast.9, ...), custom_call_target="tpu_custom_call" | custom-call | flops 60000002048 | bytes 1 | tf_op jit(solution)/shard_map/pallas_call | solution.py:202
  14.2 1.9 %collective-permute-start.8 = (f32[32,1024]{1,0:T(8,128)S(1)}, f32[32,1024]{1,0:T(8,128)S(1)}, u32[]{:S(2)}, u32[]{:S(2)}) collective-permute-start(f32[32,1024]{1,0:T(8,128)S(1)} %get-tuple-element.15.refs_6_), channel_id=1, source_target_pairs={{0,2},{1,3},{2,0},{3,1},{4,6},{5,7},{6,4},{7,5},{8,10},{9,11},{10,... | collective-permute-start | bytes 393224 | tf_op jit(solution)/shard_map/ppermute | solution.py:22
  16.1 0.2 collective-permute-start.9
  16.3 1.8 %collective-permute-start.7 = (f32[32,1024]{1,0:T(8,128)S(1)}, f32[32,1024]{1,0:T(8,128)S(1)}, u32[]{:S(2)}, u32[]{:S(2)}) collective-permute-start(f32[32,1024]{1,0:T(8,128)S(1)} %get-tuple-element.17), channel_id=1, source_target_pairs={{0,2},{1,3},{2,0},{3,1},{4,6},{5,7},{6,4},{7,5},{8,10},{9,11},{10,... | collective-permute-start | bytes 393224 | tf_op jit(solution)/shard_map/ppermute | solution.py:22
  18.1 0.2 collective-permute-start.5
  18.3 0.0 collective-permute-done.6.refs_5_
  18.3 1.8 %collective-permute-start.11 = (f32[32,1024]{1,0:T(8,128)S(1)}, f32[32,1024]{1,0:T(8,128)S(1)}, u32[]{:S(2)}, u32[]{:S(2)}) collective-permute-start(f32[32,1024]{1,0:T(8,128)S(1)} %get-tuple-element.20), channel_id=1, source_target_pairs={{0,2},{1,3},{2,0},{3,1},{4,6},{5,7},{6,4},{7,5},{8,10},{9,11},{10,... | collective-permute-start | bytes 393224 | tf_op jit(solution)/shard_map/ppermute | solution.py:22
  20.1 0.5 %collective-permute-done.9.refs_1_ = f32[1,1024]{1,0:T(1,128)S(1)} collective-permute-done((f32[1,1024]{1,0:T(1,128)S(1)}, f32[1,1024]{1,0:T(1,128)S(1)}, u32[]{:S(2)}, u32[]{:S(2)}) %collective-permute-start.9) | collective-permute-done | bytes 4128 | tf_op jit(solution)/shard_map/ppermute | solution.py:22
  20.6 0.0 collective-permute-done.8.refs_0_
  20.7 2.8 %collective-permute-done.7.refs_0_ = f32[32,1024]{1,0:T(8,128)S(1)} collective-permute-done((f32[32,1024]{1,0:T(8,128)S(1)}, f32[32,1024]{1,0:T(8,128)S(1)}, u32[]{:S(2)}, u32[]{:S(2)}) %collective-permute-start.7) | collective-permute-done | bytes 131104 | tf_op jit(solution)/shard_map/ppermute | solution.py:22
  23.5 0.0 collective-permute-start.14
  23.5 2.8 %collective-permute-done.5.refs_0_ = f32[32,1024]{1,0:T(8,128)S(1)} collective-permute-done((f32[32,1024]{1,0:T(8,128)S(1)}, f32[32,1024]{1,0:T(8,128)S(1)}, u32[]{:S(2)}, u32[]{:S(2)}) %collective-permute-start.5) | collective-permute-done | bytes 131104 | tf_op jit(solution)/shard_map/ppermute | solution.py:22
  26.3 3.6 %collective-permute-start.10 = (f32[32,1024]{1,0:T(8,128)S(1)}, f32[32,1024]{1,0:T(8,128)S(1)}, u32[]{:S(2)}, u32[]{:S(2)}) collective-permute-start(f32[32,1024]{1,0:T(8,128)S(1)} %shard_map.65.refs_2_), channel_id=1, source_target_pairs={{0,2},{1,3},{2,4},{3,5},{4,6},{5,7},{6,8},{7,9},{8,10},{9,11},{10,... | collective-permute-start | bytes 393224 | tf_op jit(solution)/shard_map/ppermute | solution.py:252
  29.8 2.0 %collective-permute-start.12 = (f32[32,1024]{1,0:T(8,128)S(1)}, f32[32,1024]{1,0:T(8,128)S(1)}, u32[]{:S(2)}, u32[]{:S(2)}) collective-permute-start(f32[32,1024]{1,0:T(8,128)S(1)} %shard_map.66), channel_id=1, source_target_pairs={{0,2},{1,3},{2,4},{3,5},{4,6},{5,7},{6,8},{7,9},{8,10},{9,11},{10,... | collective-permute-start | bytes 393224 | tf_op jit(solution)/shard_map/ppermute | solution.py:252
  31.9 0.1 shard_map.67
  31.9 2.9 %collective-permute-start.15 = (f32[1,1024]{1,0:T(1,128)S(1)}, f32[1,1024]{1,0:T(1,128)S(1)}, u32[]{:S(2)}, u32[]{:S(2)}) collective-permute-start(f32[1,1024]{1,0:T(1,128)S(1)} %get-tuple-element.21), channel_id=1, source_target_pairs={{0,2},{1,3},{2,0},{3,1},{4,6},{5,7},{6,4},{7,5},{8,10},{9,11},{10,... | collective-permute-start | bytes 12296 | tf_op jit(solution)/shard_map/ppermute | solution.py:22
  34.8 4.2 %collective-permute-done.12.refs_1_ = f32[32,1024]{1,0:T(8,128)S(1)} collective-permute-done((f32[32,1024]{1,0:T(8,128)S(1)}, f32[32,1024]{1,0:T(8,128)S(1)}, u32[]{:S(2)}, u32[]{:S(2)}) %collective-permute-start.12) | collective-permute-done | bytes 131104 | tf_op jit(solution)/shard_map/ppermute | solution.py:252
  39.1 0.7 %shard_map.68 = (f32[1,256]{1,0:T(1,128)}, f32[64,1024]{1,0:T(8,128)}) custom-call(f32[32,1024]{1,0:T(8,128)S(1)} %collective-permute-done.10.refs_0_, f32[32,1024]{1,0:T(8,128)S(1)} %collective-permute-done.12.refs_1_, f32[1,1024]{1,0:T(1,128)S(1)} %collective-permute-done.15.refs_2_, f32[1,256]{1,0:T(1,128)S(1)} %get-tuple-element.22.refs_3_, ...), custom_call_target="tpu_custom_call" | custom-call | flops 1000000000 | bytes 1 | tf_op jit(solution)/shard_map/pallas_call | solution.py:202
  (20 shorter events, 0.1 us)
Async XLA Ops:
  0.6 8.5 %collective-permute-start.4 = (f32[1024,1024]{1,0:T(8,128)}, f32[1024,1024]{1,0:T(8,128)S(1)}, u32[]{:S(2)}, u32[]{:S(2)}) collective-permute-start(f32[1024,1024]{1,0:T(8,128)} %bitcast.3), channel_id=1, source_target_pairs={{0,1},{1,0},{2,3},{3,2},{4,5},{5,4},{6,7},{7,6},{8,9},{9,8},{10,11... | collective-permute-start | bytes 12582920 | tf_op jit(solution)/shard_map/ppermute | solution.py:22
  1.1 9.9 %collective-permute-start = (f32[64,1024]{1,0:T(8,128)}, f32[64,1024]{1,0:T(8,128)S(1)}, u32[]{:S(2)}, u32[]{:S(2)}) collective-permute-start(f32[64,1024]{1,0:T(8,128)} %bitcast.8), channel_id=1, source_target_pairs={{0,2},{1,3},{2,0},{3,1},{4,6},{5,7},{6,4},{7,5},{8,10},{9,11},{10,... | collective-permute-start | bytes 786440 | tf_op jit(solution)/shard_map/ppermute | solution.py:22
  5.1 4.6 %collective-permute-start.1 = (f32[1,1280]{1,0:T(1,128)S(1)}, f32[1,1280]{1,0:T(1,128)S(1)}, u32[]{:S(2)}, u32[]{:S(2)}) collective-permute-start(f32[1,1280]{1,0:T(1,128)S(1)} %constant_dynamic-update-slice_fusion.refs_2_.refs_0_), channel_id=1, source_target_pairs={{0,1},{1,0},{2,3},{3,2},{4,5},{5,4},{6,7},{7,6},{8,9},{9,8},{10,11... | collective-permute-start | bytes 15368 | tf_op jit(solution)/shard_map/ppermute | solution.py:22
  5.3 5.7 %collective-permute-start.2 = (f32[1,1280]{1,0:T(1,128)S(1)}, f32[1,1280]{1,0:T(1,128)S(1)}, u32[]{:S(2)}, u32[]{:S(2)}) collective-permute-start(f32[1,1280]{1,0:T(1,128)S(1)} %constant_dynamic-update-slice_fusion.refs_2_.refs_0_), channel_id=1, source_target_pairs={{0,2},{1,3},{2,0},{3,1},{4,6},{5,7},{6,4},{7,5},{8,10},{9,11},{10,... | collective-permute-start | bytes 15368 | tf_op jit(solution)/shard_map/ppermute | solution.py:22
  5.5 5.5 %collective-permute-start.3 = (f32[1,1280]{1,0:T(1,128)S(1)}, f32[1,1280]{1,0:T(1,128)S(1)}, u32[]{:S(2)}, u32[]{:S(2)}) collective-permute-start(f32[1,1280]{1,0:T(1,128)S(1)} %constant_dynamic-update-slice_fusion.refs_2_.refs_0_), channel_id=1, source_target_pairs={{0,3},{1,2},{2,1},{3,0},{4,7},{5,6},{6,5},{7,4},{8,11},{9,10},{10,... | collective-permute-start | bytes 15368 | tf_op jit(solution)/shard_map/ppermute | solution.py:22
  7.0 2.2 %copy-start = (f32[1,1024,1024]{2,1,0:T(8,128)S(1)}, f32[1,1024,1024]{2,1,0:T(8,128)}, u32[]{:S(2)}) copy-start(f32[1,1024,1024]{2,1,0:T(8,128)} %param.4) | copy-start | bytes 12582916
  9.2 2.2 %copy-start.1 = (f32[1,1024,1024]{2,1,0:T(8,128)S(1)}, f32[1,1024,1024]{2,1,0:T(8,128)}, u32[]{:S(2)}) copy-start(f32[1,1024,1024]{2,1,0:T(8,128)} %param.4) | copy-start | bytes 12582916
  9.2 2.2 %copy-start.3 = (f32[1,64,1024]{2,1,0:T(8,128)S(1)}, f32[1,64,1024]{2,1,0:T(8,128)}, u32[]{:S(2)}) copy-start(f32[1,64,1024]{2,1,0:T(8,128)} %param.7) | copy-start | bytes 786436
  9.2 9.1 %collective-permute-start.6 = (f32[512,1024]{1,0:T(8,128)S(1)}, f32[512,1024]{1,0:T(8,128)S(1)}, u32[]{:S(2)}, u32[]{:S(2)}) collective-permute-start(f32[512,1024]{1,0:T(8,128)S(1)} %shard_map.61.refs_4_), channel_id=1, source_target_pairs={{0,1},{1,0},{2,3},{3,2},{4,5},{5,4},{6,7},{7,6},{8,9},{9,8},{10,11... | collective-permute-start | bytes 6291464 | tf_op jit(solution)/shard_map/ppermute | solution.py:22
  14.2 6.4 %collective-permute-start.8 = (f32[32,1024]{1,0:T(8,128)S(1)}, f32[32,1024]{1,0:T(8,128)S(1)}, u32[]{:S(2)}, u32[]{:S(2)}) collective-permute-start(f32[32,1024]{1,0:T(8,128)S(1)} %get-tuple-element.15.refs_6_), channel_id=1, source_target_pairs={{0,2},{1,3},{2,0},{3,1},{4,6},{5,7},{6,4},{7,5},{8,10},{9,11},{10,... | collective-permute-start | bytes 393224 | tf_op jit(solution)/shard_map/ppermute | solution.py:22
  16.1 4.6 %collective-permute-start.9 = (f32[1,1024]{1,0:T(1,128)S(1)}, f32[1,1024]{1,0:T(1,128)S(1)}, u32[]{:S(2)}, u32[]{:S(2)}) collective-permute-start(f32[1,1024]{1,0:T(1,128)S(1)} %get-tuple-element.18), channel_id=1, source_target_pairs={{0,2},{1,3},{2,0},{3,1},{4,6},{5,7},{6,4},{7,5},{8,10},{9,11},{10,... | collective-permute-start | bytes 12296 | tf_op jit(solution)/shard_map/ppermute | solution.py:22
  16.3 7.2 %collective-permute-start.7 = (f32[32,1024]{1,0:T(8,128)S(1)}, f32[32,1024]{1,0:T(8,128)S(1)}, u32[]{:S(2)}, u32[]{:S(2)}) collective-permute-start(f32[32,1024]{1,0:T(8,128)S(1)} %get-tuple-element.17), channel_id=1, source_target_pairs={{0,2},{1,3},{2,0},{3,1},{4,6},{5,7},{6,4},{7,5},{8,10},{9,11},{10,... | collective-permute-start | bytes 393224 | tf_op jit(solution)/shard_map/ppermute | solution.py:22
  18.1 8.2 %collective-permute-start.5 = (f32[32,1024]{1,0:T(8,128)S(1)}, f32[32,1024]{1,0:T(8,128)S(1)}, u32[]{:S(2)}, u32[]{:S(2)}) collective-permute-start(f32[32,1024]{1,0:T(8,128)S(1)} %get-tuple-element.14), channel_id=1, source_target_pairs={{0,2},{1,3},{2,0},{3,1},{4,6},{5,7},{6,4},{7,5},{8,10},{9,11},{10,... | collective-permute-start | bytes 393224 | tf_op jit(solution)/shard_map/ppermute | solution.py:22
  18.3 11.5 %collective-permute-start.11 = (f32[32,1024]{1,0:T(8,128)S(1)}, f32[32,1024]{1,0:T(8,128)S(1)}, u32[]{:S(2)}, u32[]{:S(2)}) collective-permute-start(f32[32,1024]{1,0:T(8,128)S(1)} %get-tuple-element.20), channel_id=1, source_target_pairs={{0,2},{1,3},{2,0},{3,1},{4,6},{5,7},{6,4},{7,5},{8,10},{9,11},{10,... | collective-permute-start | bytes 393224 | tf_op jit(solution)/shard_map/ppermute | solution.py:22
  20.7 11.2 %collective-permute-start.13 = (f32[40,1024]{1,0:T(8,128)S(1)}, f32[40,1024]{1,0:T(8,128)S(1)}, u32[]{:S(2)}, u32[]{:S(2)}) collective-permute-start(f32[40,1024]{1,0:T(8,128)S(1)} %shard_map.63.refs_2_), channel_id=1, source_target_pairs={{0,1},{1,0},{2,6},{3,7},{4,5},{5,4},{6,10},{7,11},{8,9},{9,8},{10,... | collective-permute-start | bytes 491528 | tf_op jit(solution)/shard_map/ppermute | solution.py:251
  23.5 8.4 %collective-permute-start.14 = (f32[32,1024]{1,0:T(8,128)S(1)}, f32[32,1024]{1,0:T(8,128)S(1)}, u32[]{:S(2)}, u32[]{:S(2)}) collective-permute-start(f32[32,1024]{1,0:T(8,128)S(1)} %shard_map.64.refs_2_), channel_id=1, source_target_pairs={{0,1},{1,0},{2,6},{3,7},{4,5},{5,4},{6,10},{7,11},{8,9},{9,8},{10,... | collective-permute-start | bytes 393224 | tf_op jit(solution)/shard_map/ppermute | solution.py:251
  26.3 5.6 %copy-start.2 = (f32[1,256]{1,0:T(1,128)S(1)}, f32[1,256]{1,0:T(1,128)}, u32[]{:S(2)}) copy-start(f32[1,256]{1,0:T(1,128)} %refs_2_.1) | copy-start | bytes 3076
  26.3 12.8 %collective-permute-start.10 = (f32[32,1024]{1,0:T(8,128)S(1)}, f32[32,1024]{1,0:T(8,128)S(1)}, u32[]{:S(2)}, u32[]{:S(2)}) collective-permute-start(f32[32,1024]{1,0:T(8,128)S(1)} %shard_map.65.refs_2_), channel_id=1, source_target_pairs={{0,2},{1,3},{2,4},{3,5},{4,6},{5,7},{6,8},{7,9},{8,10},{9,11},{10,... | collective-permute-start | bytes 393224 | tf_op jit(solution)/shard_map/ppermute | solution.py:252
  29.8 9.2 %collective-permute-start.12 = (f32[32,1024]{1,0:T(8,128)S(1)}, f32[32,1024]{1,0:T(8,128)S(1)}, u32[]{:S(2)}, u32[]{:S(2)}) collective-permute-start(f32[32,1024]{1,0:T(8,128)S(1)} %shard_map.66), channel_id=1, source_target_pairs={{0,2},{1,3},{2,4},{3,5},{4,6},{5,7},{6,8},{7,9},{8,10},{9,11},{10,... | collective-permute-start | bytes 393224 | tf_op jit(solution)/shard_map/ppermute | solution.py:252
  31.9 7.2 %collective-permute-start.15 = (f32[1,1024]{1,0:T(1,128)S(1)}, f32[1,1024]{1,0:T(1,128)S(1)}, u32[]{:S(2)}, u32[]{:S(2)}) collective-permute-start(f32[1,1024]{1,0:T(1,128)S(1)} %get-tuple-element.21), channel_id=1, source_target_pairs={{0,2},{1,3},{2,0},{3,1},{4,6},{5,7},{6,4},{7,5},{8,10},{9,11},{10,... | collective-permute-start | bytes 12296 | tf_op jit(solution)/shard_map/ppermute | solution.py:22

commit v5 on v4

--- a/solution.py
+++ b/solution.py
@@ -82,25 +82,26 @@
     return jnp.concatenate([times(both, *high_low(matrix[k * part : (k + 1) * part])) for k in range(PIECES)], 1)
 
 
-def product_rows(later, earlier_high, earlier_low):
-    rows = later.shape[0]
-    both = stacked(later)
+def product_rows(both, earlier_high, earlier_low):
+    rows = both.shape[0] // 2
     dot = functools.partial(jnp.dot, preferred_element_type=jnp.float32)
     wide = dot(both, earlier_high)
     return wide[:rows] + wide[rows:] + dot(both[:rows], earlier_low)
 
 
-def other_kernel(own, own_p, other_p, half, other):
-    rows = half.shape[0]
-    part = rows // 2
+def half_kernel(own, own_p, other_p, half):
+    rows, order = half.shape
+    part = order // PIECES
 
     def body(chip, core):
-        if chip == 1:
-            other[0], other[1] = high_low(other_p[...])
-            earlier, later = (own, other)[core], (other_p, own_p)[core]
+        if chip == 1 and core == 0:
             for at in range(0, rows, part):
-                block = later[rows * core + at : rows * core + at + part]
-                half[at : at + part] = product_rows(block, earlier[0], earlier[1])
+                half[at : at + part] = product_rows(stacked(other_p[at : at + part]), own[0], own[1])
+        elif chip == 1:
+            both = stacked(own_p[rows:])
+            for at in range(0, order, part):
+                here = slice(at, at + part)
+                half[:, here] = product_rows(both, *high_low(other_p[:, here]))
 
     by_place(body)
 
@@ -227,9 +228,7 @@
     vectors = [vector] + [swapped(vector, k) for k in range(1, WIN)]
     own = call(own_kernel, 0.01, split(order), own_p)
     half_rows = jax.ShapeDtypeStruct((order // 2, order), jnp.float32)
-    own_half = call(
-        other_kernel, 0.01, half_rows, own, own_p, other_p, scratch=[pltpu.VMEM((2, order, order), jnp.bfloat16)]
-    )
+    own_half = call(half_kernel, 0.01, half_rows, own, own_p, other_p)
     other_half = swapped(own_half, 1)
     heights = [rows // NEAR_PIECES] * NEAR_PIECES + [rows // FAR_PIECES] * FAR_PIECES
     pieces = [jax.ShapeDtypeStruct((height, order), jnp.float32) for height in heights]

time: 40 us -> 39.2 us (0.980)
  starting transfers between devices: 19.9 us -> 18.7 us
  waiting for transfers between devices: 11.7 us -> 12.2 us
    ppermute x2, starting transfers between devices: 5.56 us -> 4.4 us  [local(): far = [lax.ppermute(y, 'step', to_far) for y in done[NEAR_PIECES:]]]
    ppermute x12, waiting for transfers between devices: 7.41 us -> 8.42 us  [swapped(): return lax.ppermute(block, 'step', [(i, i ^ bit) for i in range(count)])]
    ppermute x2, waiting for transfers between devices: 4.24 us -> 3.73 us  [local(): far = [lax.ppermute(y, 'step', to_far) for y in done[NEAR_PIECES:]]]
  transfers between devices with their start and end apart: 16 -> 16, of which waited for: 5 -> 5; matrix products, arithmetic and copies ran while one was open for 3% -> 4% of each run, Pallas kernels for 7% -> 7%
where the time goes in v5:
time: 39.2 us; the launch traced here: 39 us
  starting transfers between devices  18.7 us (48%)
  waiting for transfers between devices  12.2 us (31%)
  local copies, waits for them, and re-layouts  3.92 us (10%)
  Pallas kernels  3.46 us (9%)
  between operations  0.68 us (2%)
    ppermute x12, starting transfers between devices, swapped(): return lax.ppermute(block, 'step', [(i, i ^ bit) for i in range(count)])  14.3 us
    ppermute x12, waiting for transfers between devices, swapped(): return lax.ppermute(block, 'step', [(i, i ^ bit) for i in range(count)])  8.42 us
    ppermute x2, starting transfers between devices, local(): far = [lax.ppermute(y, 'step', to_far) for y in done[NEAR_PIECES:]]  4.4 us
    ppermute x2, waiting for transfers between devices, local(): far = [lax.ppermute(y, 'step', to_far) for y in done[NEAR_PIECES:]]  3.73 us
    pallas_call x10, Pallas kernels, call(): pl.pallas_call(run, out_shape=out_shape, in_specs=(specs or [VMEM] * coun...  3.46 us
    unnamed x9, local copies, waits for them, and re-layouts  3.23 us
  transfers between devices with their start and end apart: 16, of which 5 were waited for; matrix products, arithmetic and copies ran while one was open for 4% of the time, Pallas kernels for 7%

profile of v5, /device:TPU:0, one launch (start us, length us, event | category | flops | bytes accessed | tf_op | source)
XLA Modules:
  0.0 39.0 jit_solution(6929409663968968875)
XLA Ops:
  0.6 0.5 %collective-permute-start.4 = (f32[1024,1024]{1,0:T(8,128)}, f32[1024,1024]{1,0:T(8,128)S(1)}, u32[]{:S(2)}, u32[]{:S(2)}) collective-permute-start(f32[1024,1024]{1,0:T(8,128)} %bitcast.3), channel_id=1, source_target_pairs={{0,1},{1,0},{2,3},{3,2},{4,5},{5,4},{6,7},{7,6},{8,9},{9,8},{10,11... | collective-permute-start | bytes 12582920 | tf_op jit(solution)/shard_map/ppermute | solution.py:22
  1.1 2.6 %collective-permute-start = (f32[64,1024]{1,0:T(8,128)}, f32[64,1024]{1,0:T(8,128)S(1)}, u32[]{:S(2)}, u32[]{:S(2)}) collective-permute-start(f32[64,1024]{1,0:T(8,128)} %bitcast.8), channel_id=1, source_target_pairs={{0,2},{1,3},{2,0},{3,1},{4,6},{5,7},{6,4},{7,5},{8,10},{9,11},{10,... | collective-permute-start | bytes 786440 | tf_op jit(solution)/shard_map/ppermute | solution.py:22
  3.7 0.7 %constant_dynamic-update-slice_fusion.1 = f32[1,1280]{1,0:T(1,128)S(1)} fusion(f32[1,256]{1,0:T(1,128)} %refs_2_.1), kind=kLoop, calls=%fused_computation.1 | loop fusion | bytes 2048
  4.4 0.7 %constant_dynamic-update-slice_fusion.refs_2_.refs_0_ = f32[1,1280]{1,0:T(1,128)S(1)} fusion(f32[1,1280]{1,0:T(1,128)S(1)} %constant_dynamic-update-slice_fusion.1, f32[1,1024]{1,0:T(1,128)} %param.5), kind=kLoop, calls=%fused_computation | loop fusion | bytes 8192 | tf_op jit(solution)/shard_map/concatenate | solution.py:227
  5.1 0.2 collective-permute-start.1
  5.3 0.3 collective-permute-start.2
  5.5 1.4 %collective-permute-start.3 = (f32[1,1280]{1,0:T(1,128)S(1)}, f32[1,1280]{1,0:T(1,128)S(1)}, u32[]{:S(2)}, u32[]{:S(2)}) collective-permute-start(f32[1,1280]{1,0:T(1,128)S(1)} %constant_dynamic-update-slice_fusion.refs_2_.refs_0_), channel_id=1, source_target_pairs={{0,3},{1,2},{2,1},{3,0},{4,7},{5,6},{6,5},{7,4},{8,11},{9,10},{10,... | collective-permute-start | bytes 15368 | tf_op jit(solution)/shard_map/ppermute | solution.py:22
  7.0 2.2 %copy-done = f32[1,1024,1024]{2,1,0:T(8,128)S(1)} copy-done((f32[1,1024,1024]{2,1,0:T(8,128)S(1)}, f32[1,1024,1024]{2,1,0:T(8,128)}, u32[]{:S(2)}) %copy-start) | copy-done | bytes 4194328
  9.2 0.5 %collective-permute-start.6 = (f32[512,1024]{1,0:T(8,128)S(1)}, f32[512,1024]{1,0:T(8,128)S(1)}, u32[]{:S(2)}, u32[]{:S(2)}) collective-permute-start(f32[512,1024]{1,0:T(8,128)S(1)} %shard_map.61.refs_4_), channel_id=1, source_target_pairs={{0,1},{1,0},{2,3},{3,2},{4,5},{5,4},{6,7},{7,6},{8,9},{9,8},{10,11... | collective-permute-start | bytes 6291464 | tf_op jit(solution)/shard_map/ppermute | solution.py:22
  9.7 1.3 %collective-permute-done.2.refs_4_ = f32[1,1280]{1,0:T(1,128)S(1)} collective-permute-done((f32[1,1280]{1,0:T(1,128)S(1)}, f32[1,1280]{1,0:T(1,128)S(1)}, u32[]{:S(2)}, u32[]{:S(2)}) %collective-permute-start.2) | collective-permute-done | bytes 5152 | tf_op jit(solution)/shard_map/ppermute | solution.py:22
  11.0 0.0 collective-permute-done.3.refs_5_
  11.0 0.0 collective-permute-done.refs_0_
  11.0 0.3 copy-done.1
  11.4 0.0 copy-done.3
  11.4 2.6 %shard_map.59 = (f32[1,1024]{1,0:T(1,128)S(1)}, f32[32,1024]{1,0:T(8,128)S(1)}, f32[32,1024]{1,0:T(8,128)S(1)}, f32[32,1024]{1,0:T(8,128)S(1)}, f32[32,1024]{1,0:T(8,128)S(1)}) custom-call(f32[64,1024]{1,0:T(8,128)S(1)} %collective-permute-done.refs_0_, f32[64,1024]{1,0:T(8,128)S(1)} %bitcast.9, ...), custom_call_target="tpu_custom_call" | custom-call | flops 60000002048 | bytes 1 | tf_op jit(solution)/shard_map/pallas_call | solution.py:203
  14.0 0.9 %collective-permute-start.8 = (f32[32,1024]{1,0:T(8,128)S(1)}, f32[32,1024]{1,0:T(8,128)S(1)}, u32[]{:S(2)}, u32[]{:S(2)}) collective-permute-start(f32[32,1024]{1,0:T(8,128)S(1)} %get-tuple-element.15.refs_6_), channel_id=1, source_target_pairs={{0,2},{1,3},{2,0},{3,1},{4,6},{5,7},{6,4},{7,5},{8,10},{9,11},{10,... | collective-permute-start | bytes 393224 | tf_op jit(solution)/shard_map/ppermute | solution.py:22
  14.9 1.2 %collective-permute-start.9 = (f32[1,1024]{1,0:T(1,128)S(1)}, f32[1,1024]{1,0:T(1,128)S(1)}, u32[]{:S(2)}, u32[]{:S(2)}) collective-permute-start(f32[1,1024]{1,0:T(1,128)S(1)} %get-tuple-element.18), channel_id=1, source_target_pairs={{0,2},{1,3},{2,0},{3,1},{4,6},{5,7},{6,4},{7,5},{8,10},{9,11},{10,... | collective-permute-start | bytes 12296 | tf_op jit(solution)/shard_map/ppermute | solution.py:22
  16.1 0.8 %collective-permute-start.7 = (f32[32,1024]{1,0:T(8,128)S(1)}, f32[32,1024]{1,0:T(8,128)S(1)}, u32[]{:S(2)}, u32[]{:S(2)}) collective-permute-start(f32[32,1024]{1,0:T(8,128)S(1)} %get-tuple-element.17), channel_id=1, source_target_pairs={{0,2},{1,3},{2,0},{3,1},{4,6},{5,7},{6,4},{7,5},{8,10},{9,11},{10,... | collective-permute-start | bytes 393224 | tf_op jit(solution)/shard_map/ppermute | solution.py:22
  16.9 1.2 %collective-permute-start.5 = (f32[32,1024]{1,0:T(8,128)S(1)}, f32[32,1024]{1,0:T(8,128)S(1)}, u32[]{:S(2)}, u32[]{:S(2)}) collective-permute-start(f32[32,1024]{1,0:T(8,128)S(1)} %get-tuple-element.14), channel_id=1, source_target_pairs={{0,2},{1,3},{2,0},{3,1},{4,6},{5,7},{6,4},{7,5},{8,10},{9,11},{10,... | collective-permute-start | bytes 393224 | tf_op jit(solution)/shard_map/ppermute | solution.py:22
  18.1 0.0 collective-permute-done.6.refs_5_
  18.2 0.8 %collective-permute-start.11 = (f32[32,1024]{1,0:T(8,128)S(1)}, f32[32,1024]{1,0:T(8,128)S(1)}, u32[]{:S(2)}, u32[]{:S(2)}) collective-permute-start(f32[32,1024]{1,0:T(8,128)S(1)} %get-tuple-element.20), channel_id=1, source_target_pairs={{0,2},{1,3},{2,0},{3,1},{4,6},{5,7},{6,4},{7,5},{8,10},{9,11},{10,... | collective-permute-start | bytes 393224 | tf_op jit(solution)/shard_map/ppermute | solution.py:22
  19.0 1.5 %collective-permute-done.9.refs_1_ = f32[1,1024]{1,0:T(1,128)S(1)} collective-permute-done((f32[1,1024]{1,0:T(1,128)S(1)}, f32[1,1024]{1,0:T(1,128)S(1)}, u32[]{:S(2)}, u32[]{:S(2)}) %collective-permute-start.9) | collective-permute-done | bytes 4128 | tf_op jit(solution)/shard_map/ppermute | solution.py:22
  20.5 0.0 collective-permute-start.13
  20.5 2.8 %collective-permute-done.7.refs_0_ = f32[32,1024]{1,0:T(8,128)S(1)} collective-permute-done((f32[32,1024]{1,0:T(8,128)S(1)}, f32[32,1024]{1,0:T(8,128)S(1)}, u32[]{:S(2)}, u32[]{:S(2)}) %collective-permute-start.7) | collective-permute-done | bytes 131104 | tf_op jit(solution)/shard_map/ppermute | solution.py:22
  23.3 2.8 %collective-permute-done.5.refs_0_ = f32[32,1024]{1,0:T(8,128)S(1)} collective-permute-done((f32[32,1024]{1,0:T(8,128)S(1)}, f32[32,1024]{1,0:T(8,128)S(1)}, u32[]{:S(2)}, u32[]{:S(2)}) %collective-permute-start.5) | collective-permute-done | bytes 131104 | tf_op jit(solution)/shard_map/ppermute | solution.py:22
  26.1 3.0 %collective-permute-start.10 = (f32[32,1024]{1,0:T(8,128)S(1)}, f32[32,1024]{1,0:T(8,128)S(1)}, u32[]{:S(2)}, u32[]{:S(2)}) collective-permute-start(f32[32,1024]{1,0:T(8,128)S(1)} %shard_map.65.refs_2_), channel_id=1, source_target_pairs={{0,2},{1,3},{2,4},{3,5},{4,6},{5,7},{6,8},{7,9},{8,10},{9,11},{10,... | collective-permute-start | bytes 393224 | tf_op jit(solution)/shard_map/ppermute | solution.py:251
  29.1 0.0 collective-permute-done.11.refs_0_
  29.1 1.4 %collective-permute-start.12 = (f32[32,1024]{1,0:T(8,128)S(1)}, f32[32,1024]{1,0:T(8,128)S(1)}, u32[]{:S(2)}, u32[]{:S(2)}) collective-permute-start(f32[32,1024]{1,0:T(8,128)S(1)} %shard_map.66), channel_id=1, source_target_pairs={{0,2},{1,3},{2,4},{3,5},{4,6},{5,7},{6,8},{7,9},{8,10},{9,11},{10,... | collective-permute-start | bytes 393224 | tf_op jit(solution)/shard_map/ppermute | solution.py:251
  30.5 0.1 shard_map.67
  30.6 3.9 %collective-permute-start.15 = (f32[1,1024]{1,0:T(1,128)S(1)}, f32[1,1024]{1,0:T(1,128)S(1)}, u32[]{:S(2)}, u32[]{:S(2)}) collective-permute-start(f32[1,1024]{1,0:T(1,128)S(1)} %get-tuple-element.21), channel_id=1, source_target_pairs={{0,2},{1,3},{2,0},{3,1},{4,6},{5,7},{6,4},{7,5},{8,10},{9,11},{10,... | collective-permute-start | bytes 12296 | tf_op jit(solution)/shard_map/ppermute | solution.py:22
  34.5 3.7 %collective-permute-done.12.refs_1_ = f32[32,1024]{1,0:T(8,128)S(1)} collective-permute-done((f32[32,1024]{1,0:T(8,128)S(1)}, f32[32,1024]{1,0:T(8,128)S(1)}, u32[]{:S(2)}, u32[]{:S(2)}) %collective-permute-start.12) | collective-permute-done | bytes 131104 | tf_op jit(solution)/shard_map/ppermute | solution.py:251
  38.2 0.7 %shard_map.68 = (f32[1,256]{1,0:T(1,128)}, f32[64,1024]{1,0:T(8,128)}) custom-call(f32[32,1024]{1,0:T(8,128)S(1)} %collective-permute-done.10.refs_0_, f32[32,1024]{1,0:T(8,128)S(1)} %collective-permute-done.12.refs_1_, f32[1,1024]{1,0:T(1,128)S(1)} %collective-permute-done.15.refs_2_, f32[1,256]{1,0:T(1,128)S(1)} %get-tuple-element.22.refs_3_, ...), custom_call_target="tpu_custom_call" | custom-call | flops 1000000000 | bytes 1 | tf_op jit(solution)/shard_map/pallas_call | solution.py:203
  (20 shorter events, 0.1 us)
Async XLA Ops:
  0.6 8.5 %collective-permute-start.4 = (f32[1024,1024]{1,0:T(8,128)}, f32[1024,1024]{1,0:T(8,128)S(1)}, u32[]{:S(2)}, u32[]{:S(2)}) collective-permute-start(f32[1024,1024]{1,0:T(8,128)} %bitcast.3), channel_id=1, source_target_pairs={{0,1},{1,0},{2,3},{3,2},{4,5},{5,4},{6,7},{7,6},{8,9},{9,8},{10,11... | collective-permute-start | bytes 12582920 | tf_op jit(solution)/shard_map/ppermute | solution.py:22
  1.1 9.9 %collective-permute-start = (f32[64,1024]{1,0:T(8,128)}, f32[64,1024]{1,0:T(8,128)S(1)}, u32[]{:S(2)}, u32[]{:S(2)}) collective-permute-start(f32[64,1024]{1,0:T(8,128)} %bitcast.8), channel_id=1, source_target_pairs={{0,2},{1,3},{2,0},{3,1},{4,6},{5,7},{6,4},{7,5},{8,10},{9,11},{10,... | collective-permute-start | bytes 786440 | tf_op jit(solution)/shard_map/ppermute | solution.py:22
  5.1 4.6 %collective-permute-start.1 = (f32[1,1280]{1,0:T(1,128)S(1)}, f32[1,1280]{1,0:T(1,128)S(1)}, u32[]{:S(2)}, u32[]{:S(2)}) collective-permute-start(f32[1,1280]{1,0:T(1,128)S(1)} %constant_dynamic-update-slice_fusion.refs_2_.refs_0_), channel_id=1, source_target_pairs={{0,1},{1,0},{2,3},{3,2},{4,5},{5,4},{6,7},{7,6},{8,9},{9,8},{10,11... | collective-permute-start | bytes 15368 | tf_op jit(solution)/shard_map/ppermute | solution.py:22
  5.3 5.7 %collective-permute-start.2 = (f32[1,1280]{1,0:T(1,128)S(1)}, f32[1,1280]{1,0:T(1,128)S(1)}, u32[]{:S(2)}, u32[]{:S(2)}) collective-permute-start(f32[1,1280]{1,0:T(1,128)S(1)} %constant_dynamic-update-slice_fusion.refs_2_.refs_0_), channel_id=1, source_target_pairs={{0,2},{1,3},{2,0},{3,1},{4,6},{5,7},{6,4},{7,5},{8,10},{9,11},{10,... | collective-permute-start | bytes 15368 | tf_op jit(solution)/shard_map/ppermute | solution.py:22
  5.5 5.5 %collective-permute-start.3 = (f32[1,1280]{1,0:T(1,128)S(1)}, f32[1,1280]{1,0:T(1,128)S(1)}, u32[]{:S(2)}, u32[]{:S(2)}) collective-permute-start(f32[1,1280]{1,0:T(1,128)S(1)} %constant_dynamic-update-slice_fusion.refs_2_.refs_0_), channel_id=1, source_target_pairs={{0,3},{1,2},{2,1},{3,0},{4,7},{5,6},{6,5},{7,4},{8,11},{9,10},{10,... | collective-permute-start | bytes 15368 | tf_op jit(solution)/shard_map/ppermute | solution.py:22
  7.0 2.2 %copy-start = (f32[1,1024,1024]{2,1,0:T(8,128)S(1)}, f32[1,1024,1024]{2,1,0:T(8,128)}, u32[]{:S(2)}) copy-start(f32[1,1024,1024]{2,1,0:T(8,128)} %param.4) | copy-start | bytes 12582916
  9.2 2.2 %copy-start.1 = (f32[1,1024,1024]{2,1,0:T(8,128)S(1)}, f32[1,1024,1024]{2,1,0:T(8,128)}, u32[]{:S(2)}) copy-start(f32[1,1024,1024]{2,1,0:T(8,128)} %param.4) | copy-start | bytes 12582916
  9.2 2.2 %copy-start.3 = (f32[1,64,1024]{2,1,0:T(8,128)S(1)}, f32[1,64,1024]{2,1,0:T(8,128)}, u32[]{:S(2)}) copy-start(f32[1,64,1024]{2,1,0:T(8,128)} %param.7) | copy-start | bytes 786436
  9.2 8.9 %collective-permute-start.6 = (f32[512,1024]{1,0:T(8,128)S(1)}, f32[512,1024]{1,0:T(8,128)S(1)}, u32[]{:S(2)}, u32[]{:S(2)}) collective-permute-start(f32[512,1024]{1,0:T(8,128)S(1)} %shard_map.61.refs_4_), channel_id=1, source_target_pairs={{0,1},{1,0},{2,3},{3,2},{4,5},{5,4},{6,7},{7,6},{8,9},{9,8},{10,11... | collective-permute-start | bytes 6291464 | tf_op jit(solution)/shard_map/ppermute | solution.py:22
  14.0 6.5 %collective-permute-start.8 = (f32[32,1024]{1,0:T(8,128)S(1)}, f32[32,1024]{1,0:T(8,128)S(1)}, u32[]{:S(2)}, u32[]{:S(2)}) collective-permute-start(f32[32,1024]{1,0:T(8,128)S(1)} %get-tuple-element.15.refs_6_), channel_id=1, source_target_pairs={{0,2},{1,3},{2,0},{3,1},{4,6},{5,7},{6,4},{7,5},{8,10},{9,11},{10,... | collective-permute-start | bytes 393224 | tf_op jit(solution)/shard_map/ppermute | solution.py:22
  14.9 5.6 %collective-permute-start.9 = (f32[1,1024]{1,0:T(1,128)S(1)}, f32[1,1024]{1,0:T(1,128)S(1)}, u32[]{:S(2)}, u32[]{:S(2)}) collective-permute-start(f32[1,1024]{1,0:T(1,128)S(1)} %get-tuple-element.18), channel_id=1, source_target_pairs={{0,2},{1,3},{2,0},{3,1},{4,6},{5,7},{6,4},{7,5},{8,10},{9,11},{10,... | collective-permute-start | bytes 12296 | tf_op jit(solution)/shard_map/ppermute | solution.py:22
  16.1 7.2 %collective-permute-start.7 = (f32[32,1024]{1,0:T(8,128)S(1)}, f32[32,1024]{1,0:T(8,128)S(1)}, u32[]{:S(2)}, u32[]{:S(2)}) collective-permute-start(f32[32,1024]{1,0:T(8,128)S(1)} %get-tuple-element.17), channel_id=1, source_target_pairs={{0,2},{1,3},{2,0},{3,1},{4,6},{5,7},{6,4},{7,5},{8,10},{9,11},{10,... | collective-permute-start | bytes 393224 | tf_op jit(solution)/shard_map/ppermute | solution.py:22
  16.9 9.2 %collective-permute-start.5 = (f32[32,1024]{1,0:T(8,128)S(1)}, f32[32,1024]{1,0:T(8,128)S(1)}, u32[]{:S(2)}, u32[]{:S(2)}) collective-permute-start(f32[32,1024]{1,0:T(8,128)S(1)} %get-tuple-element.14), channel_id=1, source_target_pairs={{0,2},{1,3},{2,0},{3,1},{4,6},{5,7},{6,4},{7,5},{8,10},{9,11},{10,... | collective-permute-start | bytes 393224 | tf_op jit(solution)/shard_map/ppermute | solution.py:22
  18.2 11.0 %collective-permute-start.11 = (f32[32,1024]{1,0:T(8,128)S(1)}, f32[32,1024]{1,0:T(8,128)S(1)}, u32[]{:S(2)}, u32[]{:S(2)}) collective-permute-start(f32[32,1024]{1,0:T(8,128)S(1)} %get-tuple-element.20), channel_id=1, source_target_pairs={{0,2},{1,3},{2,0},{3,1},{4,6},{5,7},{6,4},{7,5},{8,10},{9,11},{10,... | collective-permute-start | bytes 393224 | tf_op jit(solution)/shard_map/ppermute | solution.py:22
  20.5 10.0 %collective-permute-start.13 = (f32[40,1024]{1,0:T(8,128)S(1)}, f32[40,1024]{1,0:T(8,128)S(1)}, u32[]{:S(2)}, u32[]{:S(2)}) collective-permute-start(f32[40,1024]{1,0:T(8,128)S(1)} %shard_map.63.refs_2_), channel_id=1, source_target_pairs={{0,1},{1,0},{2,6},{3,7},{4,5},{5,4},{6,10},{7,11},{8,9},{9,8},{10,... | collective-permute-start | bytes 491528 | tf_op jit(solution)/shard_map/ppermute | solution.py:250
  23.3 7.2 %collective-permute-start.14 = (f32[32,1024]{1,0:T(8,128)S(1)}, f32[32,1024]{1,0:T(8,128)S(1)}, u32[]{:S(2)}, u32[]{:S(2)}) collective-permute-start(f32[32,1024]{1,0:T(8,128)S(1)} %shard_map.64.refs_2_), channel_id=1, source_target_pairs={{0,1},{1,0},{2,6},{3,7},{4,5},{5,4},{6,10},{7,11},{8,9},{9,8},{10,... | collective-permute-start | bytes 393224 | tf_op jit(solution)/shard_map/ppermute | solution.py:250
  26.1 4.4 %copy-start.2 = (f32[1,256]{1,0:T(1,128)S(1)}, f32[1,256]{1,0:T(1,128)}, u32[]{:S(2)}) copy-start(f32[1,256]{1,0:T(1,128)} %refs_2_.1) | copy-start | bytes 3076
  26.1 12.1 %collective-permute-start.10 = (f32[32,1024]{1,0:T(8,128)S(1)}, f32[32,1024]{1,0:T(8,128)S(1)}, u32[]{:S(2)}, u32[]{:S(2)}) collective-permute-start(f32[32,1024]{1,0:T(8,128)S(1)} %shard_map.65.refs_2_), channel_id=1, source_target_pairs={{0,2},{1,3},{2,4},{3,5},{4,6},{5,7},{6,8},{7,9},{8,10},{9,11},{10,... | collective-permute-start | bytes 393224 | tf_op jit(solution)/shard_map/ppermute | solution.py:251
  29.1 9.1 %collective-permute-start.12 = (f32[32,1024]{1,0:T(8,128)S(1)}, f32[32,1024]{1,0:T(8,128)S(1)}, u32[]{:S(2)}, u32[]{:S(2)}) collective-permute-start(f32[32,1024]{1,0:T(8,128)S(1)} %shard_map.66), channel_id=1, source_target_pairs={{0,2},{1,3},{2,4},{3,5},{4,6},{5,7},{6,8},{7,9},{8,10},{9,11},{10,... | collective-permute-start | bytes 393224 | tf_op jit(solution)/shard_map/ppermute | solution.py:251
  30.6 7.6 %collective-permute-start.15 = (f32[1,1024]{1,0:T(1,128)S(1)}, f32[1,1024]{1,0:T(1,128)S(1)}, u32[]{:S(2)}, u32[]{:S(2)}) collective-permute-start(f32[1,1024]{1,0:T(1,128)S(1)} %get-tuple-element.21), channel_id=1, source_target_pairs={{0,2},{1,3},{2,0},{3,1},{4,6},{5,7},{6,4},{7,5},{8,10},{9,11},{10,... | collective-permute-start | bytes 12296 | tf_op jit(solution)/shard_map/ppermute | solution.py:22

commit v6 on v5

--- a/solution.py
+++ b/solution.py
@@ -11,6 +11,7 @@
 HALF = WIN // 2
 PAD = 8
 PIECES = 4
+LANES = 128
 NEAR_PIECES = 2
 FAR_PIECES = 2
 VMEM = pl.BlockSpec(memory_space=pltpu.VMEM)
@@ -41,6 +42,30 @@
     wide = product_nt(both, high)
     narrow = product_nt(both[: (rows + 15) // 16 * 16], low)
     return wide[:rows] + wide[rows:] + narrow[:rows]
+
+
+def put_flat(out, rows, state):
+    count = rows.shape[0]
+    for k in range(rows.shape[1] // LANES):
+        here = slice(k * LANES, (k + 1) * LANES)
+        out[k * count : (k + 1) * count] = rows[:, here]
+    groups = rows.shape[1] // LANES
+    at = groups * count
+    out[at : at + groups] = sum(
+        jnp.where(
+            lax.broadcasted_iota(jnp.int32, (groups, LANES), 0) == k, state[:, k * LANES : (k + 1) * LANES], 0.0
+        )
+        for k in range(groups)
+    )
+
+
+def take_flat(flat, order):
+    groups = order // LANES
+    count = flat.shape[0] // groups - 1
+    at = groups * count
+    rows = jnp.concatenate([flat[k * count : (k + 1) * count] for k in range(groups)], 1)
+    state = jnp.concatenate([flat[at + k : at + k + 1] for k in range(groups)], 1)
+    return rows, state
 
 
 def one_row(at, value):
@@ -106,7 +131,7 @@
     by_place(body)
 
 
-def first_kernel(mirror_v, own_v, v0, v1, v2, v3, own_p, other_p, state, *outs):
+def first_kernel(mirror_v, own_v, v0, v1, v2, v3, own_p, other_p, *outs):
     order = mirror_v.shape[1]
     vectors = (v0[...], v1[...], v2[...], v3[...])
     width = v0.shape[1] - order
@@ -117,9 +142,9 @@
             for step in range(2):
                 y = split_times(x, (own_p, other_p)[step ^ core])
                 x = jnp.concatenate([y[:PAD] + one_row(0, vectors[step ^ core][:, width:]), y[PAD:]], 0)
-            state[...] = x[:1]
-            at = PAD
-            for out in outs:
+            at = PAD + outs[0].shape[0] // (order // LANES) - 1
+            put_flat(outs[0], x[PAD:at], x[:1])
+            for out in outs[1:]:
                 out[...] = x[at : at + out.shape[0]]
                 at += out.shape[0]
 
@@ -153,13 +178,13 @@
     by_place(body)
 
 
-def state_rows_kernel(got, state, joint, joint_f, out):
+def state_rows_kernel(got, joint, joint_f, out):
     @pl.when(on_second_chip())
     def _():
-        x = jnp.concatenate([one_row(0, state[...]), got[...]], 0)
+        rows, state = take_flat(got, joint.shape[2])
+        x = jnp.concatenate([one_row(0, state), rows], 0)
         y = times(stacked(x), joint[0], joint[1])
-        out[:PAD] = y[:PAD] + one_row(0, joint_f[...])
-        out[PAD:] = y[PAD:]
+        put_flat(out, y[PAD:], y[:1] + joint_f[...])
 
 
 def rows_kernel(got, joint, out):
@@ -179,10 +204,11 @@
     *came, starts, directions, residual, jacobian, end = refs
     place = lax.axis_index("step") % WIN
     mine = place >= HALF
-    end[...] = came[0][:1]
-    whole = jnp.concatenate([came[0][PAD:]] + [piece[...] for piece in came[1:]], 0)
+    rows, came_end = take_flat(came[0], directions.shape[1])
+    end[...] = came_end
+    whole = jnp.concatenate([rows] + [piece[...] for piece in came[1:]], 0)
     jacobian[...] = jnp.where(mine, whole, 0.0) - directions[...]
-    residual[...] = jnp.where(mine, slice_of(came[0][:1], place, starts.shape[1]), 0.0) - starts[...]
+    residual[...] = jnp.where(mine, slice_of(came_end, place, starts.shape[1]), 0.0) - starts[...]
 
 
 def far_kernel(*refs):
@@ -232,8 +258,9 @@
     other_half = swapped(own_half, 1)
     heights = [rows // NEAR_PIECES] * NEAR_PIECES + [rows // FAR_PIECES] * FAR_PIECES
     pieces = [jax.ShapeDtypeStruct((height, order), jnp.float32) for height in heights]
-    state, *xs = call(first_kernel, 60, [row, *pieces], mirror_v, own_v, *vectors, own_p, other_p)
-    got_state = swapped(state, 2)
+    groups = order // LANES
+    pieces[0] = jax.ShapeDtypeStruct((groups * (heights[0] + 1), LANES), jnp.float32)
+    xs = call(first_kernel, 60, pieces, mirror_v, own_v, *vectors, own_p, other_p)
     got = [swapped(x, 2) for x in xs]
     joint, joint_f = call(
         joint_kernel, 1, [split(order), row], *vectors[:2], own_p, other_p, own_half, other_half, after=(xs[0],)
@@ -243,8 +270,7 @@
     done = []
     for k, x in enumerate(got):
         if k == 0:
-            tall = jax.ShapeDtypeStruct((PAD + heights[0], order), jnp.float32)
-            done.append(call(state_rows_kernel, 2, tall, x, got_state, joint, joint_f))
+            done.append(call(state_rows_kernel, 2, pieces[k], x, joint, joint_f))
         else:
             done.append(call(rows_kernel, 2, pieces[k], x, joint, after=done[-1:]))
     near = [lax.ppermute(y, "step", to_near) for y in done[:NEAR_PIECES]]

time: 39.2 us -> 38.5 us (0.982)
  starting transfers between devices: 18.7 us -> 16.9 us
  waiting for transfers between devices: 12.2 us -> 13.3 us
    ppermute x12 -> x11, starting transfers between devices: 14.3 us -> 12.5 us  [swapped(): return lax.ppermute(block, 'step', [(i, i ^ bit) for i in range(count)])]
    ppermute x12 -> x11, waiting for transfers between devices: 8.42 us -> 9.23 us  [swapped(): return lax.ppermute(block, 'step', [(i, i ^ bit) for i in range(count)])]
  transfers between devices with their start and end apart: 16 -> 15, of which waited for: 5 -> 5; matrix products, arithmetic and copies ran while one was open for 4% -> 4% of each run, Pallas kernels for 7% -> 7%
where the time goes in v6:
time: 38.5 us; the launch traced here: 38.3 us
  starting transfers between devices  16.9 us (44%)
  waiting for transfers between devices  13.3 us (35%)
  local copies, waits for them, and re-layouts  3.92 us (10%)
  Pallas kernels  3.46 us (9%)
  between operations  0.68 us (2%)
    ppermute x11, starting transfers between devices, swapped(): return lax.ppermute(block, 'step', [(i, i ^ bit) for i in range(count)])  12.5 us
    ppermute x11, waiting for transfers between devices, swapped(): return lax.ppermute(block, 'step', [(i, i ^ bit) for i in range(count)])  9.23 us
    ppermute x2, starting transfers between devices, local(): far = [lax.ppermute(y, 'step', to_far) for y in done[NEAR_PIECES:]]  4.4 us
    ppermute x2, waiting for transfers between devices, local(): far = [lax.ppermute(y, 'step', to_far) for y in done[NEAR_PIECES:]]  4.06 us
    pallas_call x10, Pallas kernels, call(): pl.pallas_call(run, out_shape=out_shape, in_specs=(specs or [VMEM] * coun...  3.46 us
    unnamed x9, local copies, waits for them, and re-layouts  3.23 us
  transfers between devices with their start and end apart: 15, of which 5 were waited for; matrix products, arithmetic and copies ran while one was open for 4% of the time, Pallas kernels for 7%

profile of v6, /device:TPU:0, one launch (start us, length us, event | category | flops | bytes accessed | tf_op | source)
XLA Modules:
  0.0 38.3 jit_solution(16702255913143647927)
XLA Ops:
  0.6 0.5 %collective-permute-start.4 = (f32[1024,1024]{1,0:T(8,128)}, f32[1024,1024]{1,0:T(8,128)S(1)}, u32[]{:S(2)}, u32[]{:S(2)}) collective-permute-start(f32[1024,1024]{1,0:T(8,128)} %bitcast.3), channel_id=1, source_target_pairs={{0,1},{1,0},{2,3},{3,2},{4,5},{5,4},{6,7},{7,6},{8,9},{9,8},{10,11... | collective-permute-start | bytes 12582920 | tf_op jit(solution)/shard_map/ppermute | solution.py:23
  1.1 2.6 %collective-permute-start = (f32[64,1024]{1,0:T(8,128)}, f32[64,1024]{1,0:T(8,128)S(1)}, u32[]{:S(2)}, u32[]{:S(2)}) collective-permute-start(f32[64,1024]{1,0:T(8,128)} %bitcast.8), channel_id=1, source_target_pairs={{0,2},{1,3},{2,0},{3,1},{4,6},{5,7},{6,4},{7,5},{8,10},{9,11},{10,... | collective-permute-start | bytes 786440 | tf_op jit(solution)/shard_map/ppermute | solution.py:23
  3.7 0.7 %constant_dynamic-update-slice_fusion.1 = f32[1,1280]{1,0:T(1,128)S(1)} fusion(f32[1,256]{1,0:T(1,128)} %refs_2_.1), kind=kLoop, calls=%fused_computation.1 | loop fusion | bytes 2048
  4.4 0.7 %constant_dynamic-update-slice_fusion.refs_2_.refs_0_ = f32[1,1280]{1,0:T(1,128)S(1)} fusion(f32[1,1280]{1,0:T(1,128)S(1)} %constant_dynamic-update-slice_fusion.1, f32[1,1024]{1,0:T(1,128)} %param.5), kind=kLoop, calls=%fused_computation | loop fusion | bytes 8192 | tf_op jit(solution)/shard_map/concatenate | solution.py:253
  5.1 0.2 collective-permute-start.1
  5.3 0.3 collective-permute-start.2
  5.5 1.4 %collective-permute-start.3 = (f32[1,1280]{1,0:T(1,128)S(1)}, f32[1,1280]{1,0:T(1,128)S(1)}, u32[]{:S(2)}, u32[]{:S(2)}) collective-permute-start(f32[1,1280]{1,0:T(1,128)S(1)} %constant_dynamic-update-slice_fusion.refs_2_.refs_0_), channel_id=1, source_target_pairs={{0,3},{1,2},{2,1},{3,0},{4,7},{5,6},{6,5},{7,4},{8,11},{9,10},{10,... | collective-permute-start | bytes 15368 | tf_op jit(solution)/shard_map/ppermute | solution.py:23
  7.0 2.2 %copy-done = f32[1,1024,1024]{2,1,0:T(8,128)S(1)} copy-done((f32[1,1024,1024]{2,1,0:T(8,128)S(1)}, f32[1,1024,1024]{2,1,0:T(8,128)}, u32[]{:S(2)}) %copy-start) | copy-done | bytes 4194328
  9.2 0.0 collective-permute-done.4.refs_7_.refs_2_.refs_3_
  9.2 0.5 %collective-permute-start.6 = (f32[512,1024]{1,0:T(8,128)S(1)}, f32[512,1024]{1,0:T(8,128)S(1)}, u32[]{:S(2)}, u32[]{:S(2)}) collective-permute-start(f32[512,1024]{1,0:T(8,128)S(1)} %shard_map.61.refs_4_), channel_id=1, source_target_pairs={{0,1},{1,0},{2,3},{3,2},{4,5},{5,4},{6,7},{7,6},{8,9},{9,8},{10,11... | collective-permute-start | bytes 6291464 | tf_op jit(solution)/shard_map/ppermute | solution.py:23
  9.7 0.0 collective-permute-done.1.refs_3_.refs_1_
  9.7 1.3 %collective-permute-done.2.refs_4_ = f32[1,1280]{1,0:T(1,128)S(1)} collective-permute-done((f32[1,1280]{1,0:T(1,128)S(1)}, f32[1,1280]{1,0:T(1,128)S(1)}, u32[]{:S(2)}, u32[]{:S(2)}) %collective-permute-start.2) | collective-permute-done | bytes 5152 | tf_op jit(solution)/shard_map/ppermute | solution.py:23
  11.0 0.3 copy-done.1
  11.4 0.0 copy-done.3
  11.4 2.6 %shard_map.59 = (f32[264,128]{1,0:T(8,128)S(1)}, f32[32,1024]{1,0:T(8,128)S(1)}, f32[32,1024]{1,0:T(8,128)S(1)}, f32[32,1024]{1,0:T(8,128)S(1)}) custom-call(f32[64,1024]{1,0:T(8,128)S(1)} %collective-permute-done.refs_0_, f32[64,1024]{1,0:T(8,128)S(1)} %bitcast.9, f32[1,1280]{1,0:T(1,128)S(1)} %constant_dynamic-update-slice_fusion.refs_2_.refs_0_, ...), custom_call_target="tpu_custom_call" | custom-call | flops 60000002048 | bytes 1 | tf_op jit(solution)/shard_map/pallas_call | solution.py:229
  14.0 0.9 %collective-permute-start.8 = (f32[264,128]{1,0:T(8,128)S(1)}, f32[264,128]{1,0:T(8,128)S(1)}, u32[]{:S(2)}, u32[]{:S(2)}) collective-permute-start(f32[264,128]{1,0:T(8,128)S(1)} %get-tuple-element.14.refs_6_), channel_id=1, source_target_pairs={{0,2},{1,3},{2,0},{3,1},{4,6},{5,7},{6,4},{7,5},{8,10},{9,11},{10,... | collective-permute-start | bytes 405512 | tf_op jit(solution)/shard_map/ppermute | solution.py:23
  14.9 1.2 %collective-permute-start.7 = (f32[32,1024]{1,0:T(8,128)S(1)}, f32[32,1024]{1,0:T(8,128)S(1)}, u32[]{:S(2)}, u32[]{:S(2)}) collective-permute-start(f32[32,1024]{1,0:T(8,128)S(1)} %get-tuple-element.16), channel_id=1, source_target_pairs={{0,2},{1,3},{2,0},{3,1},{4,6},{5,7},{6,4},{7,5},{8,10},{9,11},{10,... | collective-permute-start | bytes 393224 | tf_op jit(solution)/shard_map/ppermute | solution.py:23
  16.1 0.8 %collective-permute-start.5 = (f32[32,1024]{1,0:T(8,128)S(1)}, f32[32,1024]{1,0:T(8,128)S(1)}, u32[]{:S(2)}, u32[]{:S(2)}) collective-permute-start(f32[32,1024]{1,0:T(8,128)S(1)} %get-tuple-element.13), channel_id=1, source_target_pairs={{0,2},{1,3},{2,0},{3,1},{4,6},{5,7},{6,4},{7,5},{8,10},{9,11},{10,... | collective-permute-start | bytes 393224 | tf_op jit(solution)/shard_map/ppermute | solution.py:23
  16.9 1.2 %collective-permute-start.10 = (f32[32,1024]{1,0:T(8,128)S(1)}, f32[32,1024]{1,0:T(8,128)S(1)}, u32[]{:S(2)}, u32[]{:S(2)}) collective-permute-start(f32[32,1024]{1,0:T(8,128)S(1)} %get-tuple-element.18), channel_id=1, source_target_pairs={{0,2},{1,3},{2,0},{3,1},{4,6},{5,7},{6,4},{7,5},{8,10},{9,11},{10,... | collective-permute-start | bytes 393224 | tf_op jit(solution)/shard_map/ppermute | solution.py:23
  18.2 0.0 collective-permute-done.6.refs_5_
  18.2 2.3 %collective-permute-done.8.refs_0_ = f32[264,128]{1,0:T(8,128)S(1)} collective-permute-done((f32[264,128]{1,0:T(8,128)S(1)}, f32[264,128]{1,0:T(8,128)S(1)}, u32[]{:S(2)}, u32[]{:S(2)}) %collective-permute-start.8) | collective-permute-done | bytes 135200 | tf_op jit(solution)/shard_map/ppermute | solution.py:23
  20.5 0.0 collective-permute-start.12
  20.5 2.8 %collective-permute-done.7.refs_0_ = f32[32,1024]{1,0:T(8,128)S(1)} collective-permute-done((f32[32,1024]{1,0:T(8,128)S(1)}, f32[32,1024]{1,0:T(8,128)S(1)}, u32[]{:S(2)}, u32[]{:S(2)}) %collective-permute-start.7) | collective-permute-done | bytes 131104 | tf_op jit(solution)/shard_map/ppermute | solution.py:23
  23.3 2.8 %collective-permute-done.5.refs_0_ = f32[32,1024]{1,0:T(8,128)S(1)} collective-permute-done((f32[32,1024]{1,0:T(8,128)S(1)}, f32[32,1024]{1,0:T(8,128)S(1)}, u32[]{:S(2)}, u32[]{:S(2)}) %collective-permute-start.5) | collective-permute-done | bytes 131104 | tf_op jit(solution)/shard_map/ppermute | solution.py:23
  26.1 2.6 %collective-permute-start.9 = (f32[32,1024]{1,0:T(8,128)S(1)}, f32[32,1024]{1,0:T(8,128)S(1)}, u32[]{:S(2)}, u32[]{:S(2)}) collective-permute-start(f32[32,1024]{1,0:T(8,128)S(1)} %shard_map.65.refs_2_), channel_id=1, source_target_pairs={{0,2},{1,3},{2,4},{3,5},{4,6},{5,7},{6,8},{7,9},{8,10},{9,11},{10,... | collective-permute-start | bytes 393224 | tf_op jit(solution)/shard_map/ppermute | solution.py:277
  28.7 1.8 %collective-permute-start.11 = (f32[32,1024]{1,0:T(8,128)S(1)}, f32[32,1024]{1,0:T(8,128)S(1)}, u32[]{:S(2)}, u32[]{:S(2)}) collective-permute-start(f32[32,1024]{1,0:T(8,128)S(1)} %shard_map.66), channel_id=1, source_target_pairs={{0,2},{1,3},{2,4},{3,5},{4,6},{5,7},{6,8},{7,9},{8,10},{9,11},{10,... | collective-permute-start | bytes 393224 | tf_op jit(solution)/shard_map/ppermute | solution.py:277
  30.5 0.0 collective-permute-done.13.refs_1_
  30.5 0.0 collective-permute-done.12.refs_0_
  30.5 0.1 shard_map.67
  30.6 2.9 %collective-permute-start.14 = (f32[1,1024]{1,0:T(1,128)S(1)}, f32[1,1024]{1,0:T(1,128)S(1)}, u32[]{:S(2)}, u32[]{:S(2)}) collective-permute-start(f32[1,1024]{1,0:T(1,128)S(1)} %get-tuple-element.19), channel_id=1, source_target_pairs={{0,2},{1,3},{2,0},{3,1},{4,6},{5,7},{6,4},{7,5},{8,10},{9,11},{10,... | collective-permute-start | bytes 12296 | tf_op jit(solution)/shard_map/ppermute | solution.py:23
  33.5 4.1 %collective-permute-done.11.refs_1_ = f32[32,1024]{1,0:T(8,128)S(1)} collective-permute-done((f32[32,1024]{1,0:T(8,128)S(1)}, f32[32,1024]{1,0:T(8,128)S(1)}, u32[]{:S(2)}, u32[]{:S(2)}) %collective-permute-start.11) | collective-permute-done | bytes 131104 | tf_op jit(solution)/shard_map/ppermute | solution.py:277
  37.5 0.7 %shard_map.68 = (f32[1,256]{1,0:T(1,128)}, f32[64,1024]{1,0:T(8,128)}) custom-call(f32[32,1024]{1,0:T(8,128)S(1)} %collective-permute-done.9.refs_0_, f32[32,1024]{1,0:T(8,128)S(1)} %collective-permute-done.11.refs_1_, f32[1,1024]{1,0:T(1,128)S(1)} %collective-permute-done.14.refs_2_, f32[1,256]{1,0:T(1,128)S(1)} %get-tuple-element.20.refs_3_, ...), custom_call_target="tpu_custom_call" | custom-call | flops 1000000000 | bytes 1 | tf_op jit(solution)/shard_map/pallas_call | solution.py:229
  (18 shorter events, 0.1 us)
Async XLA Ops:
  0.6 8.5 %collective-permute-start.4 = (f32[1024,1024]{1,0:T(8,128)}, f32[1024,1024]{1,0:T(8,128)S(1)}, u32[]{:S(2)}, u32[]{:S(2)}) collective-permute-start(f32[1024,1024]{1,0:T(8,128)} %bitcast.3), channel_id=1, source_target_pairs={{0,1},{1,0},{2,3},{3,2},{4,5},{5,4},{6,7},{7,6},{8,9},{9,8},{10,11... | collective-permute-start | bytes 12582920 | tf_op jit(solution)/shard_map/ppermute | solution.py:23
  1.1 9.9 %collective-permute-start = (f32[64,1024]{1,0:T(8,128)}, f32[64,1024]{1,0:T(8,128)S(1)}, u32[]{:S(2)}, u32[]{:S(2)}) collective-permute-start(f32[64,1024]{1,0:T(8,128)} %bitcast.8), channel_id=1, source_target_pairs={{0,2},{1,3},{2,0},{3,1},{4,6},{5,7},{6,4},{7,5},{8,10},{9,11},{10,... | collective-permute-start | bytes 786440 | tf_op jit(solution)/shard_map/ppermute | solution.py:23
  5.1 4.6 %collective-permute-start.1 = (f32[1,1280]{1,0:T(1,128)S(1)}, f32[1,1280]{1,0:T(1,128)S(1)}, u32[]{:S(2)}, u32[]{:S(2)}) collective-permute-start(f32[1,1280]{1,0:T(1,128)S(1)} %constant_dynamic-update-slice_fusion.refs_2_.refs_0_), channel_id=1, source_target_pairs={{0,1},{1,0},{2,3},{3,2},{4,5},{5,4},{6,7},{7,6},{8,9},{9,8},{10,11... | collective-permute-start | bytes 15368 | tf_op jit(solution)/shard_map/ppermute | solution.py:23
  5.3 5.7 %collective-permute-start.2 = (f32[1,1280]{1,0:T(1,128)S(1)}, f32[1,1280]{1,0:T(1,128)S(1)}, u32[]{:S(2)}, u32[]{:S(2)}) collective-permute-start(f32[1,1280]{1,0:T(1,128)S(1)} %constant_dynamic-update-slice_fusion.refs_2_.refs_0_), channel_id=1, source_target_pairs={{0,2},{1,3},{2,0},{3,1},{4,6},{5,7},{6,4},{7,5},{8,10},{9,11},{10,... | collective-permute-start | bytes 15368 | tf_op jit(solution)/shard_map/ppermute | solution.py:23
  5.5 5.5 %collective-permute-start.3 = (f32[1,1280]{1,0:T(1,128)S(1)}, f32[1,1280]{1,0:T(1,128)S(1)}, u32[]{:S(2)}, u32[]{:S(2)}) collective-permute-start(f32[1,1280]{1,0:T(1,128)S(1)} %constant_dynamic-update-slice_fusion.refs_2_.refs_0_), channel_id=1, source_target_pairs={{0,3},{1,2},{2,1},{3,0},{4,7},{5,6},{6,5},{7,4},{8,11},{9,10},{10,... | collective-permute-start | bytes 15368 | tf_op jit(solution)/shard_map/ppermute | solution.py:23
  7.0 2.2 %copy-start = (f32[1,1024,1024]{2,1,0:T(8,128)S(1)}, f32[1,1024,1024]{2,1,0:T(8,128)}, u32[]{:S(2)}) copy-start(f32[1,1024,1024]{2,1,0:T(8,128)} %param.4) | copy-start | bytes 12582916
  9.2 2.2 %copy-start.1 = (f32[1,1024,1024]{2,1,0:T(8,128)S(1)}, f32[1,1024,1024]{2,1,0:T(8,128)}, u32[]{:S(2)}) copy-start(f32[1,1024,1024]{2,1,0:T(8,128)} %param.4) | copy-start | bytes 12582916
  9.2 2.2 %copy-start.3 = (f32[1,64,1024]{2,1,0:T(8,128)S(1)}, f32[1,64,1024]{2,1,0:T(8,128)}, u32[]{:S(2)}) copy-start(f32[1,64,1024]{2,1,0:T(8,128)} %param.7) | copy-start | bytes 786436
  9.2 8.9 %collective-permute-start.6 = (f32[512,1024]{1,0:T(8,128)S(1)}, f32[512,1024]{1,0:T(8,128)S(1)}, u32[]{:S(2)}, u32[]{:S(2)}) collective-permute-start(f32[512,1024]{1,0:T(8,128)S(1)} %shard_map.61.refs_4_), channel_id=1, source_target_pairs={{0,1},{1,0},{2,3},{3,2},{4,5},{5,4},{6,7},{7,6},{8,9},{9,8},{10,11... | collective-permute-start | bytes 6291464 | tf_op jit(solution)/shard_map/ppermute | solution.py:23
  14.0 6.5 %collective-permute-start.8 = (f32[264,128]{1,0:T(8,128)S(1)}, f32[264,128]{1,0:T(8,128)S(1)}, u32[]{:S(2)}, u32[]{:S(2)}) collective-permute-start(f32[264,128]{1,0:T(8,128)S(1)} %get-tuple-element.14.refs_6_), channel_id=1, source_target_pairs={{0,2},{1,3},{2,0},{3,1},{4,6},{5,7},{6,4},{7,5},{8,10},{9,11},{10,... | collective-permute-start | bytes 405512 | tf_op jit(solution)/shard_map/ppermute | solution.py:23
  14.9 8.4 %collective-permute-start.7 = (f32[32,1024]{1,0:T(8,128)S(1)}, f32[32,1024]{1,0:T(8,128)S(1)}, u32[]{:S(2)}, u32[]{:S(2)}) collective-permute-start(f32[32,1024]{1,0:T(8,128)S(1)} %get-tuple-element.16), channel_id=1, source_target_pairs={{0,2},{1,3},{2,0},{3,1},{4,6},{5,7},{6,4},{7,5},{8,10},{9,11},{10,... | collective-permute-start | bytes 393224 | tf_op jit(solution)/shard_map/ppermute | solution.py:23
  16.1 10.0 %collective-permute-start.5 = (f32[32,1024]{1,0:T(8,128)S(1)}, f32[32,1024]{1,0:T(8,128)S(1)}, u32[]{:S(2)}, u32[]{:S(2)}) collective-permute-start(f32[32,1024]{1,0:T(8,128)S(1)} %get-tuple-element.13), channel_id=1, source_target_pairs={{0,2},{1,3},{2,0},{3,1},{4,6},{5,7},{6,4},{7,5},{8,10},{9,11},{10,... | collective-permute-start | bytes 393224 | tf_op jit(solution)/shard_map/ppermute | solution.py:23
  16.9 11.7 %collective-permute-start.10 = (f32[32,1024]{1,0:T(8,128)S(1)}, f32[32,1024]{1,0:T(8,128)S(1)}, u32[]{:S(2)}, u32[]{:S(2)}) collective-permute-start(f32[32,1024]{1,0:T(8,128)S(1)} %get-tuple-element.18), channel_id=1, source_target_pairs={{0,2},{1,3},{2,0},{3,1},{4,6},{5,7},{6,4},{7,5},{8,10},{9,11},{10,... | collective-permute-start | bytes 393224 | tf_op jit(solution)/shard_map/ppermute | solution.py:23
  20.5 10.0 %collective-permute-start.12 = (f32[264,128]{1,0:T(8,128)S(1)}, f32[264,128]{1,0:T(8,128)S(1)}, u32[]{:S(2)}, u32[]{:S(2)}) collective-permute-start(f32[264,128]{1,0:T(8,128)S(1)} %shard_map.63.refs_2_), channel_id=1, source_target_pairs={{0,1},{1,0},{2,6},{3,7},{4,5},{5,4},{6,10},{7,11},{8,9},{9,8},{10,... | collective-permute-start | bytes 405512 | tf_op jit(solution)/shard_map/ppermute | solution.py:276
  23.3 7.2 %collective-permute-start.13 = (f32[32,1024]{1,0:T(8,128)S(1)}, f32[32,1024]{1,0:T(8,128)S(1)}, u32[]{:S(2)}, u32[]{:S(2)}) collective-permute-start(f32[32,1024]{1,0:T(8,128)S(1)} %shard_map.64.refs_2_), channel_id=1, source_target_pairs={{0,1},{1,0},{2,6},{3,7},{4,5},{5,4},{6,10},{7,11},{8,9},{9,8},{10,... | collective-permute-start | bytes 393224 | tf_op jit(solution)/shard_map/ppermute | solution.py:276
  26.1 4.4 %copy-start.2 = (f32[1,256]{1,0:T(1,128)S(1)}, f32[1,256]{1,0:T(1,128)}, u32[]{:S(2)}) copy-start(f32[1,256]{1,0:T(1,128)} %refs_2_.1) | copy-start | bytes 3076
  26.1 11.4 %collective-permute-start.9 = (f32[32,1024]{1,0:T(8,128)S(1)}, f32[32,1024]{1,0:T(8,128)S(1)}, u32[]{:S(2)}, u32[]{:S(2)}) collective-permute-start(f32[32,1024]{1,0:T(8,128)S(1)} %shard_map.65.refs_2_), channel_id=1, source_target_pairs={{0,2},{1,3},{2,4},{3,5},{4,6},{5,7},{6,8},{7,9},{8,10},{9,11},{10,... | collective-permute-start | bytes 393224 | tf_op jit(solution)/shard_map/ppermute | solution.py:277
  28.7 8.9 %collective-permute-start.11 = (f32[32,1024]{1,0:T(8,128)S(1)}, f32[32,1024]{1,0:T(8,128)S(1)}, u32[]{:S(2)}, u32[]{:S(2)}) collective-permute-start(f32[32,1024]{1,0:T(8,128)S(1)} %shard_map.66), channel_id=1, source_target_pairs={{0,2},{1,3},{2,4},{3,5},{4,6},{5,7},{6,8},{7,9},{8,10},{9,11},{10,... | collective-permute-start | bytes 393224 | tf_op jit(solution)/shard_map/ppermute | solution.py:277
  30.6 7.0 %collective-permute-start.14 = (f32[1,1024]{1,0:T(1,128)S(1)}, f32[1,1024]{1,0:T(1,128)S(1)}, u32[]{:S(2)}, u32[]{:S(2)}) collective-permute-start(f32[1,1024]{1,0:T(1,128)S(1)} %get-tuple-element.19), channel_id=1, source_target_pairs={{0,2},{1,3},{2,0},{3,1},{4,6},{5,7},{6,4},{7,5},{8,10},{9,11},{10,... | collective-permute-start | bytes 12296 | tf_op jit(solution)/shard_map/ppermute | solution.py:23

commit v7 on v6

--- a/solution.py
+++ b/solution.py
@@ -12,8 +12,6 @@
 PAD = 8
 PIECES = 4
 LANES = 128
-NEAR_PIECES = 2
-FAR_PIECES = 2
 VMEM = pl.BlockSpec(memory_space=pltpu.VMEM)
 ANY = pl.BlockSpec(memory_space=pl.ANY)
 
@@ -138,7 +136,9 @@
 
     def body(chip, core):
         if chip == 0:
-            x = jnp.concatenate([one_row(0, whole_start(vectors, width)), mirror_v[...], own_v[...]], 0)
+            half = mirror_v.shape[0] // 2
+            x = [one_row(0, whole_start(vectors, width)), mirror_v[:half], own_v[...], mirror_v[half:]]
+            x = jnp.concatenate(x, 0)
             for step in range(2):
                 y = split_times(x, (own_p, other_p)[step ^ core])
                 x = jnp.concatenate([y[:PAD] + one_row(0, vectors[step ^ core][:, width:]), y[PAD:]], 0)
@@ -200,24 +200,30 @@
     return mine
 
 
-def near_kernel(*refs):
-    *came, starts, directions, residual, jacobian, end = refs
+def end_kernel(came, end):
+    groups = end.shape[1] // LANES
+    at = came.shape[0] - groups
+    end[...] = jnp.concatenate([came[at + k : at + k + 1] for k in range(groups)], 1)
+
+
+def middle_kernel(near, far_0, far_1, starts, directions, residual, jacobian):
     place = lax.axis_index("step") % WIN
-    mine = place >= HALF
-    rows, came_end = take_flat(came[0], directions.shape[1])
-    end[...] = came_end
-    whole = jnp.concatenate([rows] + [piece[...] for piece in came[1:]], 0)
-    jacobian[...] = jnp.where(mine, whole, 0.0) - directions[...]
-    residual[...] = jnp.where(mine, slice_of(came_end, place, starts.shape[1]), 0.0) - starts[...]
-
-
-def far_kernel(*refs):
-    *came, end, residual_in, jacobian_in, residual, jacobian = refs
+    first = place < HALF
+    rows, end = take_flat(near, directions.shape[1])
+    count = rows.shape[0]
+    jacobian[:count] = jnp.where(first, far_0[...], rows) - directions[:count]
+    jacobian[count:] = jnp.where(first, far_1[...], 0.0) - directions[count:]
+    residual[...] = jnp.where(first, 0.0, slice_of(end, place, starts.shape[1])) - starts[...]
+
+
+def last_kernel(near, mirror_end, residual_in, jacobian_in, residual, jacobian):
     place = lax.axis_index("step") % WIN
-    mine = place < HALF
-    whole = jnp.concatenate([piece[...] for piece in came], 0)
-    jacobian[...] = jnp.where(mine, whole, 0.0) + jacobian_in[...]
-    residual[...] = jnp.where(mine, slice_of(end[...], place, residual.shape[1]), 0.0) + residual_in[...]
+    first = place < HALF
+    count = jacobian.shape[0] - near.shape[0]
+    jacobian[:count] = jacobian_in[:count]
+    jacobian[count:] = jnp.where(first, 0.0, near[...]) + jacobian_in[count:]
+    here = slice_of(mirror_end[...], place, residual.shape[1])
+    residual[...] = jnp.where(first, here, 0.0) + residual_in[...]
 
 
 def call(body, micros, out_shape, *args, specs=None, scratch=(), after=()):
@@ -256,7 +262,7 @@
     half_rows = jax.ShapeDtypeStruct((order // 2, order), jnp.float32)
     own_half = call(half_kernel, 0.01, half_rows, own, own_p, other_p)
     other_half = swapped(own_half, 1)
-    heights = [rows // NEAR_PIECES] * NEAR_PIECES + [rows // FAR_PIECES] * FAR_PIECES
+    heights = [rows // 2] * 4
     pieces = [jax.ShapeDtypeStruct((height, order), jnp.float32) for height in heights]
     groups = order // LANES
     pieces[0] = jax.ShapeDtypeStruct((groups * (heights[0] + 1), LANES), jnp.float32)
@@ -266,18 +272,19 @@
         joint_kernel, 1, [split(order), row], *vectors[:2], own_p, other_p, own_half, other_half, after=(xs[0],)
     )
     to_near = [(i, (i + WIN) % steps if i % WIN >= HALF else i ^ 1) for i in range(steps)]
-    to_far = [(i, (i + WIN - HALF) % steps if i % WIN >= HALF else i + HALF) for i in range(steps)]
+    to_far = [(i, (i + WIN - HALF) % steps) for i in range(steps) if i % WIN >= HALF]
     done = []
     for k, x in enumerate(got):
         if k == 0:
             done.append(call(state_rows_kernel, 2, pieces[k], x, joint, joint_f))
         else:
             done.append(call(rows_kernel, 2, pieces[k], x, joint, after=done[-1:]))
-    near = [lax.ppermute(y, "step", to_near) for y in done[:NEAR_PIECES]]
-    far = [lax.ppermute(y, "step", to_far) for y in done[NEAR_PIECES:]]
+    routes = to_near, to_far, to_far, to_near
+    near_0, far_0, far_1, near_1 = (lax.ppermute(y, "step", route) for y, route in zip(done, routes))
+    end = call(end_kernel, 0.01, row, near_0)
     results = [jax.ShapeDtypeStruct(starts.shape, jnp.float32), block]
-    *sums, end = call(near_kernel, 5, results + [row], *near, starts, own_v)
-    residual, jacobian = call(far_kernel, 1, results, *far, swapped(end, 2), *sums)
+    sums = call(middle_kernel, 5, results, near_0, far_0, far_1, starts, own_v)
+    residual, jacobian = call(last_kernel, 1, results, near_1, swapped(end, 2), *sums)
     return residual, jacobian[None]
 
 

time: 38.5 us -> 37.4 us (0.971)
  waiting for transfers between devices: 13.3 us -> 10.9 us
  starting transfers between devices: 16.9 us -> 18 us
    ppermute x11, starting transfers between devices: 12.5 us -> 15.4 us  [swapped(): return lax.ppermute(block, 'step', [(i, i ^ bit) for i in range(count)])]
    ppermute x4, waiting for transfers between devices: 4.07 us -> 2.05 us  [local(): lax.ppermute(y, 'step', route)]
    ppermute x4, starting transfers between devices: 4.4 us -> 2.7 us  [local(): lax.ppermute(y, 'step', route)]
    pallas_call x10 -> x11, Pallas kernels: 3.46 us -> 3.47 us  [call(): pl.pallas_call(run, out_shape=out_shape, in_specs=(specs or [VMEM] * coun...]
  transfers between devices with their start and end apart: 15 -> 15, of which waited for: 5 -> 6; matrix products, arithmetic and copies ran while one was open for 4% -> 4% of each run, Pallas kernels for 7% -> 7%
where the time goes in v7:
time: 37.4 us; the launch traced here: 37.1 us
  starting transfers between devices  18 us (48%)
  waiting for transfers between devices  10.9 us (29%)
  local copies, waits for them, and re-layouts  3.92 us (10%)
  Pallas kernels  3.47 us (9%)
  between operations  0.71 us (2%)
    ppermute x11, starting transfers between devices, swapped(): return lax.ppermute(block, 'step', [(i, i ^ bit) for i in range(count)])  15.4 us
    ppermute x11, waiting for transfers between devices, swapped(): return lax.ppermute(block, 'step', [(i, i ^ bit) for i in range(count)])  8.89 us
    pallas_call x11, Pallas kernels, call(): pl.pallas_call(run, out_shape=out_shape, in_specs=(specs or [VMEM] * coun...  3.47 us
    unnamed x9, local copies, waits for them, and re-layouts  3.23 us
    ppermute x4, starting transfers between devices, local(): lax.ppermute(y, 'step', route)  2.7 us
    ppermute x4, waiting for transfers between devices, local(): lax.ppermute(y, 'step', route)  2.05 us
  transfers between devices with their start and end apart: 15, of which 6 were waited for; matrix products, arithmetic and copies ran while one was open for 4% of the time, Pallas kernels for 7%

profile of v7, /device:TPU:0, one launch (start us, length us, event | category | flops | bytes accessed | tf_op | source)
XLA Modules:
  0.0 37.1 jit_solution(13580482760633958981)
XLA Ops:
  0.6 0.5 %collective-permute-start.4 = (f32[1024,1024]{1,0:T(8,128)}, f32[1024,1024]{1,0:T(8,128)S(1)}, u32[]{:S(2)}, u32[]{:S(2)}) collective-permute-start(f32[1024,1024]{1,0:T(8,128)} %bitcast.3), channel_id=1, source_target_pairs={{0,1},{1,0},{2,3},{3,2},{4,5},{5,4},{6,7},{7,6},{8,9},{9,8},{10,11... | collective-permute-start | bytes 12582920 | tf_op jit(solution)/shard_map/ppermute | solution.py:21
  1.1 2.6 %collective-permute-start = (f32[64,1024]{1,0:T(8,128)}, f32[64,1024]{1,0:T(8,128)S(1)}, u32[]{:S(2)}, u32[]{:S(2)}) collective-permute-start(f32[64,1024]{1,0:T(8,128)} %bitcast.8), channel_id=1, source_target_pairs={{0,2},{1,3},{2,0},{3,1},{4,6},{5,7},{6,4},{7,5},{8,10},{9,11},{10,... | collective-permute-start | bytes 786440 | tf_op jit(solution)/shard_map/ppermute | solution.py:21
  3.7 0.7 %constant_dynamic-update-slice_fusion.1 = f32[1,1280]{1,0:T(1,128)S(1)} fusion(f32[1,256]{1,0:T(1,128)} %refs_3_.1), kind=kLoop, calls=%fused_computation.1 | loop fusion | bytes 2048
  4.4 0.7 %constant_dynamic-update-slice_fusion.refs_2_.refs_0_ = f32[1,1280]{1,0:T(1,128)S(1)} fusion(f32[1,1280]{1,0:T(1,128)S(1)} %constant_dynamic-update-slice_fusion.1, f32[1,1024]{1,0:T(1,128)} %param.5), kind=kLoop, calls=%fused_computation | loop fusion | bytes 8192 | tf_op jit(solution)/shard_map/concatenate | solution.py:259
  5.1 0.2 collective-permute-start.1
  5.3 0.3 collective-permute-start.2
  5.5 1.4 %collective-permute-start.3 = (f32[1,1280]{1,0:T(1,128)S(1)}, f32[1,1280]{1,0:T(1,128)S(1)}, u32[]{:S(2)}, u32[]{:S(2)}) collective-permute-start(f32[1,1280]{1,0:T(1,128)S(1)} %constant_dynamic-update-slice_fusion.refs_2_.refs_0_), channel_id=1, source_target_pairs={{0,3},{1,2},{2,1},{3,0},{4,7},{5,6},{6,5},{7,4},{8,11},{9,10},{10,... | collective-permute-start | bytes 15368 | tf_op jit(solution)/shard_map/ppermute | solution.py:21
  7.0 2.2 %copy-done = f32[1,1024,1024]{2,1,0:T(8,128)S(1)} copy-done((f32[1,1024,1024]{2,1,0:T(8,128)S(1)}, f32[1,1024,1024]{2,1,0:T(8,128)}, u32[]{:S(2)}) %copy-start) | copy-done | bytes 4194328
  9.2 0.5 %collective-permute-start.6 = (f32[512,1024]{1,0:T(8,128)S(1)}, f32[512,1024]{1,0:T(8,128)S(1)}, u32[]{:S(2)}, u32[]{:S(2)}) collective-permute-start(f32[512,1024]{1,0:T(8,128)S(1)} %shard_map.61.refs_4_), channel_id=1, source_target_pairs={{0,1},{1,0},{2,3},{3,2},{4,5},{5,4},{6,7},{7,6},{8,9},{9,8},{10,11... | collective-permute-start | bytes 6291464 | tf_op jit(solution)/shard_map/ppermute | solution.py:21
  9.7 0.0 collective-permute-done.1.refs_3_.refs_1_
  9.7 1.3 %collective-permute-done.2.refs_4_ = f32[1,1280]{1,0:T(1,128)S(1)} collective-permute-done((f32[1,1280]{1,0:T(1,128)S(1)}, f32[1,1280]{1,0:T(1,128)S(1)}, u32[]{:S(2)}, u32[]{:S(2)}) %collective-permute-start.2) | collective-permute-done | bytes 5152 | tf_op jit(solution)/shard_map/ppermute | solution.py:21
  11.0 0.0 collective-permute-done.refs_0_
  11.0 0.3 copy-done.1
  11.4 0.0 copy-done.3
  11.4 2.6 %shard_map.59 = (f32[264,128]{1,0:T(8,128)S(1)}, f32[32,1024]{1,0:T(8,128)S(1)}, f32[32,1024]{1,0:T(8,128)S(1)}, f32[32,1024]{1,0:T(8,128)S(1)}) custom-call(f32[64,1024]{1,0:T(8,128)S(1)} %collective-permute-done.refs_0_, f32[64,1024]{1,0:T(8,128)S(1)} %bitcast.9, f32[1,1280]{1,0:T(1,128)S(1)} %constant_dynamic-update-slice_fusion.refs_2_.refs_0_, ...), custom_call_target="tpu_custom_call" | custom-call | flops 60000002048 | bytes 1 | tf_op jit(solution)/shard_map/pallas_call | solution.py:235
  14.0 0.9 %collective-permute-start.9 = (f32[264,128]{1,0:T(8,128)S(1)}, f32[264,128]{1,0:T(8,128)S(1)}, u32[]{:S(2)}, u32[]{:S(2)}) collective-permute-start(f32[264,128]{1,0:T(8,128)S(1)} %get-tuple-element.13.refs_6_), channel_id=1, source_target_pairs={{0,2},{1,3},{2,0},{3,1},{4,6},{5,7},{6,4},{7,5},{8,10},{9,11},{10,... | collective-permute-start | bytes 405512 | tf_op jit(solution)/shard_map/ppermute | solution.py:21
  14.9 1.2 %collective-permute-start.8 = (f32[32,1024]{1,0:T(8,128)S(1)}, f32[32,1024]{1,0:T(8,128)S(1)}, u32[]{:S(2)}, u32[]{:S(2)}) collective-permute-start(f32[32,1024]{1,0:T(8,128)S(1)} %get-tuple-element.16), channel_id=1, source_target_pairs={{0,2},{1,3},{2,0},{3,1},{4,6},{5,7},{6,4},{7,5},{8,10},{9,11},{10,... | collective-permute-start | bytes 393224 | tf_op jit(solution)/shard_map/ppermute | solution.py:21
  16.1 0.8 %collective-permute-start.7 = (f32[32,1024]{1,0:T(8,128)S(1)}, f32[32,1024]{1,0:T(8,128)S(1)}, u32[]{:S(2)}, u32[]{:S(2)}) collective-permute-start(f32[32,1024]{1,0:T(8,128)S(1)} %get-tuple-element.15), channel_id=1, source_target_pairs={{0,2},{1,3},{2,0},{3,1},{4,6},{5,7},{6,4},{7,5},{8,10},{9,11},{10,... | collective-permute-start | bytes 393224 | tf_op jit(solution)/shard_map/ppermute | solution.py:21
  16.9 1.2 %collective-permute-start.5 = (f32[32,1024]{1,0:T(8,128)S(1)}, f32[32,1024]{1,0:T(8,128)S(1)}, u32[]{:S(2)}, u32[]{:S(2)}) collective-permute-start(f32[32,1024]{1,0:T(8,128)S(1)} %get-tuple-element.12), channel_id=1, source_target_pairs={{0,2},{1,3},{2,0},{3,1},{4,6},{5,7},{6,4},{7,5},{8,10},{9,11},{10,... | collective-permute-start | bytes 393224 | tf_op jit(solution)/shard_map/ppermute | solution.py:21
  18.2 0.0 collective-permute-done.6.refs_5_
  18.2 2.3 %collective-permute-done.9.refs_0_ = f32[264,128]{1,0:T(8,128)S(1)} collective-permute-done((f32[264,128]{1,0:T(8,128)S(1)}, f32[264,128]{1,0:T(8,128)S(1)}, u32[]{:S(2)}, u32[]{:S(2)}) %collective-permute-start.9) | collective-permute-done | bytes 135200 | tf_op jit(solution)/shard_map/ppermute | solution.py:21
  20.5 2.8 %collective-permute-done.8.refs_0_ = f32[32,1024]{1,0:T(8,128)S(1)} collective-permute-done((f32[32,1024]{1,0:T(8,128)S(1)}, f32[32,1024]{1,0:T(8,128)S(1)}, u32[]{:S(2)}, u32[]{:S(2)}) %collective-permute-start.8) | collective-permute-done | bytes 131104 | tf_op jit(solution)/shard_map/ppermute | solution.py:21
  23.3 1.3 %collective-permute-start.13 = (f32[32,1024]{1,0:T(8,128)S(1)}, f32[32,1024]{1,0:T(8,128)S(1)}, u32[]{:S(2)}, u32[]{:S(2)}) collective-permute-start(f32[32,1024]{1,0:T(8,128)S(1)} %shard_map.64.refs_2_), channel_id=1, source_target_pairs={{2,4},{3,5},{6,8},{7,9},{10,12},{11,13},{14,0},{15,1},{18,20},{19,... | collective-permute-start | bytes 393224 | tf_op jit(solution)/shard_map/ppermute | solution.py:283
  24.6 1.5 %collective-permute-done.7.refs_0_ = f32[32,1024]{1,0:T(8,128)S(1)} collective-permute-done((f32[32,1024]{1,0:T(8,128)S(1)}, f32[32,1024]{1,0:T(8,128)S(1)}, u32[]{:S(2)}, u32[]{:S(2)}) %collective-permute-start.7) | collective-permute-done | bytes 131104 | tf_op jit(solution)/shard_map/ppermute | solution.py:21
  26.1 1.4 %collective-permute-start.14 = (f32[32,1024]{1,0:T(8,128)S(1)}, f32[32,1024]{1,0:T(8,128)S(1)}, u32[]{:S(2)}, u32[]{:S(2)}) collective-permute-start(f32[32,1024]{1,0:T(8,128)S(1)} %shard_map.65.refs_2_), channel_id=1, source_target_pairs={{2,4},{3,5},{6,8},{7,9},{10,12},{11,13},{14,0},{15,1},{18,20},{19,... | collective-permute-start | bytes 393224 | tf_op jit(solution)/shard_map/ppermute | solution.py:283
  27.5 0.9 %collective-permute-done.5.refs_0_ = f32[32,1024]{1,0:T(8,128)S(1)} collective-permute-done((f32[32,1024]{1,0:T(8,128)S(1)}, f32[32,1024]{1,0:T(8,128)S(1)}, u32[]{:S(2)}, u32[]{:S(2)}) %collective-permute-start.5) | collective-permute-done | bytes 131104 | tf_op jit(solution)/shard_map/ppermute | solution.py:21
  28.5 5.7 %collective-permute-start.12 = (f32[1,1024]{1,0:T(1,128)S(1)}, f32[1,1024]{1,0:T(1,128)S(1)}, u32[]{:S(2)}, u32[]{:S(2)}) collective-permute-start(f32[1,1024]{1,0:T(1,128)S(1)} %shard_map.67), channel_id=1, source_target_pairs={{0,2},{1,3},{2,0},{3,1},{4,6},{5,7},{6,4},{7,5},{8,10},{9,11},{10,... | collective-permute-start | bytes 12296 | tf_op jit(solution)/shard_map/ppermute | solution.py:21
  34.2 2.0 %collective-permute-done.14.refs_2_ = f32[32,1024]{1,0:T(8,128)S(1)} collective-permute-done((f32[32,1024]{1,0:T(8,128)S(1)}, f32[32,1024]{1,0:T(8,128)S(1)}, u32[]{:S(2)}, u32[]{:S(2)}) %collective-permute-start.14) | collective-permute-done | bytes 131104 | tf_op jit(solution)/shard_map/ppermute | solution.py:283
  36.3 0.0 collective-permute-done.13.refs_1_
  36.3 0.1 shard_map.68
  36.4 0.0 collective-permute-done.12.refs_1_
  36.4 0.7 %shard_map.69 = (f32[1,256]{1,0:T(1,128)}, f32[64,1024]{1,0:T(8,128)}) custom-call(f32[32,1024]{1,0:T(8,128)S(1)} %collective-permute-done.10.refs_0_, f32[1,1024]{1,0:T(1,128)S(1)} %collective-permute-done.12.refs_1_, f32[1,256]{1,0:T(1,128)S(1)} %get-tuple-element.18.refs_2_, f32[64,1024]{1,0:T(8,128)S(1)} %get-tuple-element.19.refs_3_), custom_call_target="tpu_custom_call" | custom-call | flops 1000000000 | bytes 1 | tf_op jit(solution)/shard_map/pallas_call | solution.py:235
  (19 shorter events, 0.1 us)
Async XLA Ops:
  0.6 8.5 %collective-permute-start.4 = (f32[1024,1024]{1,0:T(8,128)}, f32[1024,1024]{1,0:T(8,128)S(1)}, u32[]{:S(2)}, u32[]{:S(2)}) collective-permute-start(f32[1024,1024]{1,0:T(8,128)} %bitcast.3), channel_id=1, source_target_pairs={{0,1},{1,0},{2,3},{3,2},{4,5},{5,4},{6,7},{7,6},{8,9},{9,8},{10,11... | collective-permute-start | bytes 12582920 | tf_op jit(solution)/shard_map/ppermute | solution.py:21
  1.1 9.9 %collective-permute-start = (f32[64,1024]{1,0:T(8,128)}, f32[64,1024]{1,0:T(8,128)S(1)}, u32[]{:S(2)}, u32[]{:S(2)}) collective-permute-start(f32[64,1024]{1,0:T(8,128)} %bitcast.8), channel_id=1, source_target_pairs={{0,2},{1,3},{2,0},{3,1},{4,6},{5,7},{6,4},{7,5},{8,10},{9,11},{10,... | collective-permute-start | bytes 786440 | tf_op jit(solution)/shard_map/ppermute | solution.py:21
  5.1 4.6 %collective-permute-start.1 = (f32[1,1280]{1,0:T(1,128)S(1)}, f32[1,1280]{1,0:T(1,128)S(1)}, u32[]{:S(2)}, u32[]{:S(2)}) collective-permute-start(f32[1,1280]{1,0:T(1,128)S(1)} %constant_dynamic-update-slice_fusion.refs_2_.refs_0_), channel_id=1, source_target_pairs={{0,1},{1,0},{2,3},{3,2},{4,5},{5,4},{6,7},{7,6},{8,9},{9,8},{10,11... | collective-permute-start | bytes 15368 | tf_op jit(solution)/shard_map/ppermute | solution.py:21
  5.3 5.7 %collective-permute-start.2 = (f32[1,1280]{1,0:T(1,128)S(1)}, f32[1,1280]{1,0:T(1,128)S(1)}, u32[]{:S(2)}, u32[]{:S(2)}) collective-permute-start(f32[1,1280]{1,0:T(1,128)S(1)} %constant_dynamic-update-slice_fusion.refs_2_.refs_0_), channel_id=1, source_target_pairs={{0,2},{1,3},{2,0},{3,1},{4,6},{5,7},{6,4},{7,5},{8,10},{9,11},{10,... | collective-permute-start | bytes 15368 | tf_op jit(solution)/shard_map/ppermute | solution.py:21
  5.5 5.5 %collective-permute-start.3 = (f32[1,1280]{1,0:T(1,128)S(1)}, f32[1,1280]{1,0:T(1,128)S(1)}, u32[]{:S(2)}, u32[]{:S(2)}) collective-permute-start(f32[1,1280]{1,0:T(1,128)S(1)} %constant_dynamic-update-slice_fusion.refs_2_.refs_0_), channel_id=1, source_target_pairs={{0,3},{1,2},{2,1},{3,0},{4,7},{5,6},{6,5},{7,4},{8,11},{9,10},{10,... | collective-permute-start | bytes 15368 | tf_op jit(solution)/shard_map/ppermute | solution.py:21
  7.0 2.2 %copy-start = (f32[1,1024,1024]{2,1,0:T(8,128)S(1)}, f32[1,1024,1024]{2,1,0:T(8,128)}, u32[]{:S(2)}) copy-start(f32[1,1024,1024]{2,1,0:T(8,128)} %param.4) | copy-start | bytes 12582916
  9.2 2.2 %copy-start.1 = (f32[1,1024,1024]{2,1,0:T(8,128)S(1)}, f32[1,1024,1024]{2,1,0:T(8,128)}, u32[]{:S(2)}) copy-start(f32[1,1024,1024]{2,1,0:T(8,128)} %param.4) | copy-start | bytes 12582916
  9.2 2.2 %copy-start.3 = (f32[1,64,1024]{2,1,0:T(8,128)S(1)}, f32[1,64,1024]{2,1,0:T(8,128)}, u32[]{:S(2)}) copy-start(f32[1,64,1024]{2,1,0:T(8,128)} %param.7) | copy-start | bytes 786436
  9.2 8.9 %collective-permute-start.6 = (f32[512,1024]{1,0:T(8,128)S(1)}, f32[512,1024]{1,0:T(8,128)S(1)}, u32[]{:S(2)}, u32[]{:S(2)}) collective-permute-start(f32[512,1024]{1,0:T(8,128)S(1)} %shard_map.61.refs_4_), channel_id=1, source_target_pairs={{0,1},{1,0},{2,3},{3,2},{4,5},{5,4},{6,7},{7,6},{8,9},{9,8},{10,11... | collective-permute-start | bytes 6291464 | tf_op jit(solution)/shard_map/ppermute | solution.py:21
  14.0 6.5 %collective-permute-start.9 = (f32[264,128]{1,0:T(8,128)S(1)}, f32[264,128]{1,0:T(8,128)S(1)}, u32[]{:S(2)}, u32[]{:S(2)}) collective-permute-start(f32[264,128]{1,0:T(8,128)S(1)} %get-tuple-element.13.refs_6_), channel_id=1, source_target_pairs={{0,2},{1,3},{2,0},{3,1},{4,6},{5,7},{6,4},{7,5},{8,10},{9,11},{10,... | collective-permute-start | bytes 405512 | tf_op jit(solution)/shard_map/ppermute | solution.py:21
  14.9 8.4 %collective-permute-start.8 = (f32[32,1024]{1,0:T(8,128)S(1)}, f32[32,1024]{1,0:T(8,128)S(1)}, u32[]{:S(2)}, u32[]{:S(2)}) collective-permute-start(f32[32,1024]{1,0:T(8,128)S(1)} %get-tuple-element.16), channel_id=1, source_target_pairs={{0,2},{1,3},{2,0},{3,1},{4,6},{5,7},{6,4},{7,5},{8,10},{9,11},{10,... | collective-permute-start | bytes 393224 | tf_op jit(solution)/shard_map/ppermute | solution.py:21
  16.1 10.0 %collective-permute-start.7 = (f32[32,1024]{1,0:T(8,128)S(1)}, f32[32,1024]{1,0:T(8,128)S(1)}, u32[]{:S(2)}, u32[]{:S(2)}) collective-permute-start(f32[32,1024]{1,0:T(8,128)S(1)} %get-tuple-element.15), channel_id=1, source_target_pairs={{0,2},{1,3},{2,0},{3,1},{4,6},{5,7},{6,4},{7,5},{8,10},{9,11},{10,... | collective-permute-start | bytes 393224 | tf_op jit(solution)/shard_map/ppermute | solution.py:21
  16.9 11.5 %collective-permute-start.5 = (f32[32,1024]{1,0:T(8,128)S(1)}, f32[32,1024]{1,0:T(8,128)S(1)}, u32[]{:S(2)}, u32[]{:S(2)}) collective-permute-start(f32[32,1024]{1,0:T(8,128)S(1)} %get-tuple-element.12), channel_id=1, source_target_pairs={{0,2},{1,3},{2,0},{3,1},{4,6},{5,7},{6,4},{7,5},{8,10},{9,11},{10,... | collective-permute-start | bytes 393224 | tf_op jit(solution)/shard_map/ppermute | solution.py:21
  20.5 8.0 %collective-permute-start.11 = (f32[264,128]{1,0:T(8,128)S(1)}, f32[264,128]{1,0:T(8,128)S(1)}, u32[]{:S(2)}, u32[]{:S(2)}) collective-permute-start(f32[264,128]{1,0:T(8,128)S(1)} %shard_map.63.refs_2_), channel_id=1, source_target_pairs={{0,1},{1,0},{2,6},{3,7},{4,5},{5,4},{6,10},{7,11},{8,9},{9,8},{10,... | collective-permute-start | bytes 405512 | tf_op jit(solution)/shard_map/ppermute | solution.py:283
  23.3 13.0 %collective-permute-start.13 = (f32[32,1024]{1,0:T(8,128)S(1)}, f32[32,1024]{1,0:T(8,128)S(1)}, u32[]{:S(2)}, u32[]{:S(2)}) collective-permute-start(f32[32,1024]{1,0:T(8,128)S(1)} %shard_map.64.refs_2_), channel_id=1, source_target_pairs={{2,4},{3,5},{6,8},{7,9},{10,12},{11,13},{14,0},{15,1},{18,20},{19,... | collective-permute-start | bytes 393224 | tf_op jit(solution)/shard_map/ppermute | solution.py:283
  26.1 10.2 %copy-start.2 = (f32[1,256]{1,0:T(1,128)S(1)}, f32[1,256]{1,0:T(1,128)}, u32[]{:S(2)}) copy-start(f32[1,256]{1,0:T(1,128)} %refs_3_.1) | copy-start | bytes 3076
  26.1 10.2 %collective-permute-start.14 = (f32[32,1024]{1,0:T(8,128)S(1)}, f32[32,1024]{1,0:T(8,128)S(1)}, u32[]{:S(2)}, u32[]{:S(2)}) collective-permute-start(f32[32,1024]{1,0:T(8,128)S(1)} %shard_map.65.refs_2_), channel_id=1, source_target_pairs={{2,4},{3,5},{6,8},{7,9},{10,12},{11,13},{14,0},{15,1},{18,20},{19,... | collective-permute-start | bytes 393224 | tf_op jit(solution)/shard_map/ppermute | solution.py:283
  28.5 7.9 %collective-permute-start.10 = (f32[32,1024]{1,0:T(8,128)S(1)}, f32[32,1024]{1,0:T(8,128)S(1)}, u32[]{:S(2)}, u32[]{:S(2)}) collective-permute-start(f32[32,1024]{1,0:T(8,128)S(1)} %shard_map.66), channel_id=1, source_target_pairs={{0,1},{1,0},{2,6},{3,7},{4,5},{5,4},{6,10},{7,11},{8,9},{9,8},{10,... | collective-permute-start | bytes 393224 | tf_op jit(solution)/shard_map/ppermute | solution.py:283
  28.5 7.9 %collective-permute-start.12 = (f32[1,1024]{1,0:T(1,128)S(1)}, f32[1,1024]{1,0:T(1,128)S(1)}, u32[]{:S(2)}, u32[]{:S(2)}) collective-permute-start(f32[1,1024]{1,0:T(1,128)S(1)} %shard_map.67), channel_id=1, source_target_pairs={{0,2},{1,3},{2,0},{3,1},{4,6},{5,7},{6,4},{7,5},{8,10},{9,11},{10,... | collective-permute-start | bytes 12296 | tf_op jit(solution)/shard_map/ppermute | solution.py:21

commit v8 on v7

--- a/solution.py
+++ b/solution.py
@@ -267,7 +267,8 @@
     groups = order // LANES
     pieces[0] = jax.ShapeDtypeStruct((groups * (heights[0] + 1), LANES), jnp.float32)
     xs = call(first_kernel, 60, pieces, mirror_v, own_v, *vectors, own_p, other_p)
-    got = [swapped(x, 2) for x in xs]
+    to_second = [(i, i + HALF) for i in range(steps) if i % WIN < HALF]
+    got = [swapped(x, 2) for x in xs[:3]] + [lax.ppermute(x, "step", to_second) for x in xs[3:]]
     joint, joint_f = call(
         joint_kernel, 1, [split(order), row], *vectors[:2], own_p, other_p, own_half, other_half, after=(xs[0],)
     )

time: 37.4 us -> 37.2 us (level)
  waiting for transfers between devices: 10.9 us -> 7.34 us
  starting transfers between devices: 18 us -> 21.1 us
    ppermute x11 -> x10, waiting for transfers between devices: 8.89 us -> 5.38 us  [swapped(): return lax.ppermute(block, 'step', [(i, i ^ bit) for i in range(count)])]
    ppermute x0 -> x1, starting transfers between devices: none -> 3.12 us  [local(): lax.ppermute(x, 'step', to_second)]
    ppermute x11 -> x10, starting transfers between devices: 15.4 us -> 15.3 us  [swapped(): return lax.ppermute(block, 'step', [(i, i ^ bit) for i in range(count)])]
  transfers between devices with their start and end apart: 15 -> 15, of which waited for: 6 -> 5; matrix products, arithmetic and copies ran while one was open for 4% -> 4% of each run, Pallas kernels for 7% -> 8%
where the time goes in v8:
time: 37.2 us; the launch traced here: 36.9 us
  starting transfers between devices  21.1 us (57%)
  waiting for transfers between devices  7.34 us (20%)
  local copies, waits for them, and re-layouts  3.92 us (11%)
  Pallas kernels  3.69 us (10%)
  between operations  0.76 us (2%)
    ppermute x10, starting transfers between devices, swapped(): return lax.ppermute(block, 'step', [(i, i ^ bit) for i in range(count)])  15.3 us
    ppermute x10, waiting for transfers between devices, swapped(): return lax.ppermute(block, 'step', [(i, i ^ bit) for i in range(count)])  5.38 us
    pallas_call x11, Pallas kernels, call(): pl.pallas_call(run, out_shape=out_shape, in_specs=(specs or [VMEM] * coun...  3.69 us
    unnamed x9, local copies, waits for them, and re-layouts  3.23 us
    ppermute x1, starting transfers between devices, local(): lax.ppermute(x, 'step', to_second)  3.12 us
    ppermute x4, starting transfers between devices, local(): lax.ppermute(y, 'step', route)  2.75 us
    ppermute x4, waiting for transfers between devices, local(): lax.ppermute(y, 'step', route)  1.96 us
  transfers between devices with their start and end apart: 15, of which 5 were waited for; matrix products, arithmetic and copies ran while one was open for 4% of the time, Pallas kernels for 8%

profile of v8, /device:TPU:0, one launch (start us, length us, event | category | flops | bytes accessed | tf_op | source)
XLA Modules:
  0.0 36.9 jit_solution(15933219396261915650)
XLA Ops:
  0.6 0.5 %collective-permute-start.4 = (f32[1024,1024]{1,0:T(8,128)}, f32[1024,1024]{1,0:T(8,128)S(1)}, u32[]{:S(2)}, u32[]{:S(2)}) collective-permute-start(f32[1024,1024]{1,0:T(8,128)} %bitcast.3), channel_id=1, source_target_pairs={{0,1},{1,0},{2,3},{3,2},{4,5},{5,4},{6,7},{7,6},{8,9},{9,8},{10,11... | collective-permute-start | bytes 12582920 | tf_op jit(solution)/shard_map/ppermute | solution.py:21
  1.1 2.6 %collective-permute-start = (f32[64,1024]{1,0:T(8,128)}, f32[64,1024]{1,0:T(8,128)S(1)}, u32[]{:S(2)}, u32[]{:S(2)}) collective-permute-start(f32[64,1024]{1,0:T(8,128)} %bitcast.8), channel_id=1, source_target_pairs={{0,2},{1,3},{2,0},{3,1},{4,6},{5,7},{6,4},{7,5},{8,10},{9,11},{10,... | collective-permute-start | bytes 786440 | tf_op jit(solution)/shard_map/ppermute | solution.py:21
  3.7 0.7 %constant_dynamic-update-slice_fusion.1 = f32[1,1280]{1,0:T(1,128)S(1)} fusion(f32[1,256]{1,0:T(1,128)} %refs_3_.1), kind=kLoop, calls=%fused_computation.1 | loop fusion | bytes 2048
  4.4 0.7 %constant_dynamic-update-slice_fusion.refs_2_.refs_0_ = f32[1,1280]{1,0:T(1,128)S(1)} fusion(f32[1,1280]{1,0:T(1,128)S(1)} %constant_dynamic-update-slice_fusion.1, f32[1,1024]{1,0:T(1,128)} %param.5), kind=kLoop, calls=%fused_computation | loop fusion | bytes 8192 | tf_op jit(solution)/shard_map/concatenate | solution.py:259
  5.1 0.2 collective-permute-start.1
  5.3 0.3 collective-permute-start.2
  5.5 1.4 %collective-permute-start.3 = (f32[1,1280]{1,0:T(1,128)S(1)}, f32[1,1280]{1,0:T(1,128)S(1)}, u32[]{:S(2)}, u32[]{:S(2)}) collective-permute-start(f32[1,1280]{1,0:T(1,128)S(1)} %constant_dynamic-update-slice_fusion.refs_2_.refs_0_), channel_id=1, source_target_pairs={{0,3},{1,2},{2,1},{3,0},{4,7},{5,6},{6,5},{7,4},{8,11},{9,10},{10,... | collective-permute-start | bytes 15368 | tf_op jit(solution)/shard_map/ppermute | solution.py:21
  7.0 2.2 %copy-done = f32[1,1024,1024]{2,1,0:T(8,128)S(1)} copy-done((f32[1,1024,1024]{2,1,0:T(8,128)S(1)}, f32[1,1024,1024]{2,1,0:T(8,128)}, u32[]{:S(2)}) %copy-start) | copy-done | bytes 4194328
  9.2 0.5 %collective-permute-start.6 = (f32[512,1024]{1,0:T(8,128)S(1)}, f32[512,1024]{1,0:T(8,128)S(1)}, u32[]{:S(2)}, u32[]{:S(2)}) collective-permute-start(f32[512,1024]{1,0:T(8,128)S(1)} %shard_map.61.refs_4_), channel_id=1, source_target_pairs={{0,1},{1,0},{2,3},{3,2},{4,5},{5,4},{6,7},{7,6},{8,9},{9,8},{10,11... | collective-permute-start | bytes 6291464 | tf_op jit(solution)/shard_map/ppermute | solution.py:21
  9.7 0.0 collective-permute-done.1.refs_3_.refs_1_
  9.7 1.3 %collective-permute-done.2.refs_4_ = f32[1,1280]{1,0:T(1,128)S(1)} collective-permute-done((f32[1,1280]{1,0:T(1,128)S(1)}, f32[1,1280]{1,0:T(1,128)S(1)}, u32[]{:S(2)}, u32[]{:S(2)}) %collective-permute-start.2) | collective-permute-done | bytes 5152 | tf_op jit(solution)/shard_map/ppermute | solution.py:21
  11.0 0.3 copy-done.1
  11.4 0.0 copy-done.3
  11.4 2.6 %shard_map.59 = (f32[264,128]{1,0:T(8,128)S(1)}, f32[32,1024]{1,0:T(8,128)S(1)}, f32[32,1024]{1,0:T(8,128)S(1)}, f32[32,1024]{1,0:T(8,128)S(1)}) custom-call(f32[64,1024]{1,0:T(8,128)S(1)} %collective-permute-done.refs_0_, f32[64,1024]{1,0:T(8,128)S(1)} %bitcast.9, f32[1,1280]{1,0:T(1,128)S(1)} %constant_dynamic-update-slice_fusion.refs_2_.refs_0_, ...), custom_call_target="tpu_custom_call" | custom-call | flops 60000002048 | bytes 1 | tf_op jit(solution)/shard_map/pallas_call | solution.py:235
  14.0 0.9 %collective-permute-start.9 = (f32[264,128]{1,0:T(8,128)S(1)}, f32[264,128]{1,0:T(8,128)S(1)}, u32[]{:S(2)}, u32[]{:S(2)}) collective-permute-start(f32[264,128]{1,0:T(8,128)S(1)} %get-tuple-element.13.refs_6_), channel_id=1, source_target_pairs={{0,2},{1,3},{2,0},{3,1},{4,6},{5,7},{6,4},{7,5},{8,10},{9,11},{10,... | collective-permute-start | bytes 405512 | tf_op jit(solution)/shard_map/ppermute | solution.py:21
  14.9 1.2 %collective-permute-start.8 = (f32[32,1024]{1,0:T(8,128)S(1)}, f32[32,1024]{1,0:T(8,128)S(1)}, u32[]{:S(2)}, u32[]{:S(2)}) collective-permute-start(f32[32,1024]{1,0:T(8,128)S(1)} %get-tuple-element.16), channel_id=1, source_target_pairs={{0,2},{1,3},{2,0},{3,1},{4,6},{5,7},{6,4},{7,5},{8,10},{9,11},{10,... | collective-permute-start | bytes 393224 | tf_op jit(solution)/shard_map/ppermute | solution.py:21
  16.1 0.8 %collective-permute-start.7 = (f32[32,1024]{1,0:T(8,128)S(1)}, f32[32,1024]{1,0:T(8,128)S(1)}, u32[]{:S(2)}, u32[]{:S(2)}) collective-permute-start(f32[32,1024]{1,0:T(8,128)S(1)} %get-tuple-element.15), channel_id=1, source_target_pairs={{0,2},{1,3},{2,0},{3,1},{4,6},{5,7},{6,4},{7,5},{8,10},{9,11},{10,... | collective-permute-start | bytes 393224 | tf_op jit(solution)/shard_map/ppermute | solution.py:21
  16.9 3.1 %collective-permute-start.5 = (f32[32,1024]{1,0:T(8,128)S(1)}, f32[32,1024]{1,0:T(8,128)S(1)}, u32[]{:S(2)}, u32[]{:S(2)}) collective-permute-start(f32[32,1024]{1,0:T(8,128)S(1)} %get-tuple-element.12), channel_id=1, source_target_pairs={{0,2},{1,3},{4,6},{5,7},{8,10},{9,11},{12,14},{13,15},{16,18},{17,... | collective-permute-start | bytes 393224 | tf_op jit(solution)/shard_map/ppermute | solution.py:271
  20.1 0.0 collective-permute-done.6.refs_5_
  20.1 0.2 shard_map.62
  20.3 0.2 collective-permute-done.9.refs_0_
  20.5 0.0 collective-permute-start.11
  20.5 2.8 %collective-permute-done.8.refs_0_ = f32[32,1024]{1,0:T(8,128)S(1)} collective-permute-done((f32[32,1024]{1,0:T(8,128)S(1)}, f32[32,1024]{1,0:T(8,128)S(1)}, u32[]{:S(2)}, u32[]{:S(2)}) %collective-permute-start.8) | collective-permute-done | bytes 131104 | tf_op jit(solution)/shard_map/ppermute | solution.py:21
  23.3 1.3 %collective-permute-start.13 = (f32[32,1024]{1,0:T(8,128)S(1)}, f32[32,1024]{1,0:T(8,128)S(1)}, u32[]{:S(2)}, u32[]{:S(2)}) collective-permute-start(f32[32,1024]{1,0:T(8,128)S(1)} %shard_map.64.refs_2_), channel_id=1, source_target_pairs={{2,4},{3,5},{6,8},{7,9},{10,12},{11,13},{14,0},{15,1},{18,20},{19,... | collective-permute-start | bytes 393224 | tf_op jit(solution)/shard_map/ppermute | solution.py:284
  24.6 1.1 %collective-permute-done.7.refs_0_ = f32[32,1024]{1,0:T(8,128)S(1)} collective-permute-done((f32[32,1024]{1,0:T(8,128)S(1)}, f32[32,1024]{1,0:T(8,128)S(1)}, u32[]{:S(2)}, u32[]{:S(2)}) %collective-permute-start.7) | collective-permute-done | bytes 131104 | tf_op jit(solution)/shard_map/ppermute | solution.py:21
  25.7 1.4 %collective-permute-start.14 = (f32[32,1024]{1,0:T(8,128)S(1)}, f32[32,1024]{1,0:T(8,128)S(1)}, u32[]{:S(2)}, u32[]{:S(2)}) collective-permute-start(f32[32,1024]{1,0:T(8,128)S(1)} %shard_map.65.refs_2_), channel_id=1, source_target_pairs={{2,4},{3,5},{6,8},{7,9},{10,12},{11,13},{14,0},{15,1},{18,20},{19,... | collective-permute-start | bytes 393224 | tf_op jit(solution)/shard_map/ppermute | solution.py:284
  27.1 0.1 collective-permute-start.10
  27.2 0.0 collective-permute-done.11.refs_0_
  27.2 6.9 %collective-permute-start.12 = (f32[1,1024]{1,0:T(1,128)S(1)}, f32[1,1024]{1,0:T(1,128)S(1)}, u32[]{:S(2)}, u32[]{:S(2)}) collective-permute-start(f32[1,1024]{1,0:T(1,128)S(1)} %shard_map.67), channel_id=1, source_target_pairs={{0,2},{1,3},{2,0},{3,1},{4,6},{5,7},{6,4},{7,5},{8,10},{9,11},{10,... | collective-permute-start | bytes 12296 | tf_op jit(solution)/shard_map/ppermute | solution.py:21
  34.1 1.9 %collective-permute-done.14.refs_2_ = f32[32,1024]{1,0:T(8,128)S(1)} collective-permute-done((f32[32,1024]{1,0:T(8,128)S(1)}, f32[32,1024]{1,0:T(8,128)S(1)}, u32[]{:S(2)}, u32[]{:S(2)}) %collective-permute-start.14) | collective-permute-done | bytes 131104 | tf_op jit(solution)/shard_map/ppermute | solution.py:284
  36.0 0.1 shard_map.68
  36.1 0.7 %shard_map.69 = (f32[1,256]{1,0:T(1,128)}, f32[64,1024]{1,0:T(8,128)}) custom-call(f32[32,1024]{1,0:T(8,128)S(1)} %collective-permute-done.10.refs_0_, f32[1,1024]{1,0:T(1,128)S(1)} %collective-permute-done.12.refs_1_, f32[1,256]{1,0:T(1,128)S(1)} %get-tuple-element.18.refs_2_, f32[64,1024]{1,0:T(8,128)S(1)} %get-tuple-element.19.refs_3_), custom_call_target="tpu_custom_call" | custom-call | flops 1000000000 | bytes 1 | tf_op jit(solution)/shard_map/pallas_call | solution.py:235
  (19 shorter events, 0.1 us)
Async XLA Ops:
  0.6 8.5 %collective-permute-start.4 = (f32[1024,1024]{1,0:T(8,128)}, f32[1024,1024]{1,0:T(8,128)S(1)}, u32[]{:S(2)}, u32[]{:S(2)}) collective-permute-start(f32[1024,1024]{1,0:T(8,128)} %bitcast.3), channel_id=1, source_target_pairs={{0,1},{1,0},{2,3},{3,2},{4,5},{5,4},{6,7},{7,6},{8,9},{9,8},{10,11... | collective-permute-start | bytes 12582920 | tf_op jit(solution)/shard_map/ppermute | solution.py:21
  1.1 9.9 %collective-permute-start = (f32[64,1024]{1,0:T(8,128)}, f32[64,1024]{1,0:T(8,128)S(1)}, u32[]{:S(2)}, u32[]{:S(2)}) collective-permute-start(f32[64,1024]{1,0:T(8,128)} %bitcast.8), channel_id=1, source_target_pairs={{0,2},{1,3},{2,0},{3,1},{4,6},{5,7},{6,4},{7,5},{8,10},{9,11},{10,... | collective-permute-start | bytes 786440 | tf_op jit(solution)/shard_map/ppermute | solution.py:21
  5.1 4.6 %collective-permute-start.1 = (f32[1,1280]{1,0:T(1,128)S(1)}, f32[1,1280]{1,0:T(1,128)S(1)}, u32[]{:S(2)}, u32[]{:S(2)}) collective-permute-start(f32[1,1280]{1,0:T(1,128)S(1)} %constant_dynamic-update-slice_fusion.refs_2_.refs_0_), channel_id=1, source_target_pairs={{0,1},{1,0},{2,3},{3,2},{4,5},{5,4},{6,7},{7,6},{8,9},{9,8},{10,11... | collective-permute-start | bytes 15368 | tf_op jit(solution)/shard_map/ppermute | solution.py:21
  5.3 5.7 %collective-permute-start.2 = (f32[1,1280]{1,0:T(1,128)S(1)}, f32[1,1280]{1,0:T(1,128)S(1)}, u32[]{:S(2)}, u32[]{:S(2)}) collective-permute-start(f32[1,1280]{1,0:T(1,128)S(1)} %constant_dynamic-update-slice_fusion.refs_2_.refs_0_), channel_id=1, source_target_pairs={{0,2},{1,3},{2,0},{3,1},{4,6},{5,7},{6,4},{7,5},{8,10},{9,11},{10,... | collective-permute-start | bytes 15368 | tf_op jit(solution)/shard_map/ppermute | solution.py:21
  5.5 5.5 %collective-permute-start.3 = (f32[1,1280]{1,0:T(1,128)S(1)}, f32[1,1280]{1,0:T(1,128)S(1)}, u32[]{:S(2)}, u32[]{:S(2)}) collective-permute-start(f32[1,1280]{1,0:T(1,128)S(1)} %constant_dynamic-update-slice_fusion.refs_2_.refs_0_), channel_id=1, source_target_pairs={{0,3},{1,2},{2,1},{3,0},{4,7},{5,6},{6,5},{7,4},{8,11},{9,10},{10,... | collective-permute-start | bytes 15368 | tf_op jit(solution)/shard_map/ppermute | solution.py:21
  7.0 2.2 %copy-start = (f32[1,1024,1024]{2,1,0:T(8,128)S(1)}, f32[1,1024,1024]{2,1,0:T(8,128)}, u32[]{:S(2)}) copy-start(f32[1,1024,1024]{2,1,0:T(8,128)} %param.4) | copy-start | bytes 12582916
  9.2 2.2 %copy-start.1 = (f32[1,1024,1024]{2,1,0:T(8,128)S(1)}, f32[1,1024,1024]{2,1,0:T(8,128)}, u32[]{:S(2)}) copy-start(f32[1,1024,1024]{2,1,0:T(8,128)} %param.4) | copy-start | bytes 12582916
  9.2 2.2 %copy-start.3 = (f32[1,64,1024]{2,1,0:T(8,128)S(1)}, f32[1,64,1024]{2,1,0:T(8,128)}, u32[]{:S(2)}) copy-start(f32[1,64,1024]{2,1,0:T(8,128)} %param.7) | copy-start | bytes 786436
  9.2 10.9 %collective-permute-start.6 = (f32[512,1024]{1,0:T(8,128)S(1)}, f32[512,1024]{1,0:T(8,128)S(1)}, u32[]{:S(2)}, u32[]{:S(2)}) collective-permute-start(f32[512,1024]{1,0:T(8,128)S(1)} %shard_map.61.refs_4_), channel_id=1, source_target_pairs={{0,1},{1,0},{2,3},{3,2},{4,5},{5,4},{6,7},{7,6},{8,9},{9,8},{10,11... | collective-permute-start | bytes 6291464 | tf_op jit(solution)/shard_map/ppermute | solution.py:21
  14.0 6.5 %collective-permute-start.9 = (f32[264,128]{1,0:T(8,128)S(1)}, f32[264,128]{1,0:T(8,128)S(1)}, u32[]{:S(2)}, u32[]{:S(2)}) collective-permute-start(f32[264,128]{1,0:T(8,128)S(1)} %get-tuple-element.13.refs_6_), channel_id=1, source_target_pairs={{0,2},{1,3},{2,0},{3,1},{4,6},{5,7},{6,4},{7,5},{8,10},{9,11},{10,... | collective-permute-start | bytes 405512 | tf_op jit(solution)/shard_map/ppermute | solution.py:21
  14.9 8.4 %collective-permute-start.8 = (f32[32,1024]{1,0:T(8,128)S(1)}, f32[32,1024]{1,0:T(8,128)S(1)}, u32[]{:S(2)}, u32[]{:S(2)}) collective-permute-start(f32[32,1024]{1,0:T(8,128)S(1)} %get-tuple-element.16), channel_id=1, source_target_pairs={{0,2},{1,3},{2,0},{3,1},{4,6},{5,7},{6,4},{7,5},{8,10},{9,11},{10,... | collective-permute-start | bytes 393224 | tf_op jit(solution)/shard_map/ppermute | solution.py:21
  16.1 9.5 %collective-permute-start.7 = (f32[32,1024]{1,0:T(8,128)S(1)}, f32[32,1024]{1,0:T(8,128)S(1)}, u32[]{:S(2)}, u32[]{:S(2)}) collective-permute-start(f32[32,1024]{1,0:T(8,128)S(1)} %get-tuple-element.15), channel_id=1, source_target_pairs={{0,2},{1,3},{2,0},{3,1},{4,6},{5,7},{6,4},{7,5},{8,10},{9,11},{10,... | collective-permute-start | bytes 393224 | tf_op jit(solution)/shard_map/ppermute | solution.py:21
  16.9 10.2 %collective-permute-start.5 = (f32[32,1024]{1,0:T(8,128)S(1)}, f32[32,1024]{1,0:T(8,128)S(1)}, u32[]{:S(2)}, u32[]{:S(2)}) collective-permute-start(f32[32,1024]{1,0:T(8,128)S(1)} %get-tuple-element.12), channel_id=1, source_target_pairs={{0,2},{1,3},{4,6},{5,7},{8,10},{9,11},{12,14},{13,15},{16,18},{17,... | collective-permute-start | bytes 393224 | tf_op jit(solution)/shard_map/ppermute | solution.py:271
  20.5 6.7 %collective-permute-start.11 = (f32[264,128]{1,0:T(8,128)S(1)}, f32[264,128]{1,0:T(8,128)S(1)}, u32[]{:S(2)}, u32[]{:S(2)}) collective-permute-start(f32[264,128]{1,0:T(8,128)S(1)} %shard_map.63.refs_2_), channel_id=1, source_target_pairs={{0,1},{1,0},{2,6},{3,7},{4,5},{5,4},{6,10},{7,11},{8,9},{9,8},{10,... | collective-permute-start | bytes 405512 | tf_op jit(solution)/shard_map/ppermute | solution.py:284
  23.3 12.8 %collective-permute-start.13 = (f32[32,1024]{1,0:T(8,128)S(1)}, f32[32,1024]{1,0:T(8,128)S(1)}, u32[]{:S(2)}, u32[]{:S(2)}) collective-permute-start(f32[32,1024]{1,0:T(8,128)S(1)} %shard_map.64.refs_2_), channel_id=1, source_target_pairs={{2,4},{3,5},{6,8},{7,9},{10,12},{11,13},{14,0},{15,1},{18,20},{19,... | collective-permute-start | bytes 393224 | tf_op jit(solution)/shard_map/ppermute | solution.py:284
  25.7 10.4 %copy-start.2 = (f32[1,256]{1,0:T(1,128)S(1)}, f32[1,256]{1,0:T(1,128)}, u32[]{:S(2)}) copy-start(f32[1,256]{1,0:T(1,128)} %refs_3_.1) | copy-start | bytes 3076
  25.7 10.4 %collective-permute-start.14 = (f32[32,1024]{1,0:T(8,128)S(1)}, f32[32,1024]{1,0:T(8,128)S(1)}, u32[]{:S(2)}, u32[]{:S(2)}) collective-permute-start(f32[32,1024]{1,0:T(8,128)S(1)} %shard_map.65.refs_2_), channel_id=1, source_target_pairs={{2,4},{3,5},{6,8},{7,9},{10,12},{11,13},{14,0},{15,1},{18,20},{19,... | collective-permute-start | bytes 393224 | tf_op jit(solution)/shard_map/ppermute | solution.py:284
  27.1 9.0 %collective-permute-start.10 = (f32[32,1024]{1,0:T(8,128)S(1)}, f32[32,1024]{1,0:T(8,128)S(1)}, u32[]{:S(2)}, u32[]{:S(2)}) collective-permute-start(f32[32,1024]{1,0:T(8,128)S(1)} %shard_map.66), channel_id=1, source_target_pairs={{0,1},{1,0},{2,6},{3,7},{4,5},{5,4},{6,10},{7,11},{8,9},{9,8},{10,... | collective-permute-start | bytes 393224 | tf_op jit(solution)/shard_map/ppermute | solution.py:284
  27.2 8.9 %collective-permute-start.12 = (f32[1,1024]{1,0:T(1,128)S(1)}, f32[1,1024]{1,0:T(1,128)S(1)}, u32[]{:S(2)}, u32[]{:S(2)}) collective-permute-start(f32[1,1024]{1,0:T(1,128)S(1)} %shard_map.67), channel_id=1, source_target_pairs={{0,2},{1,3},{2,0},{3,1},{4,6},{5,7},{6,4},{7,5},{8,10},{9,11},{10,... | collective-permute-start | bytes 12296 | tf_op jit(solution)/shard_map/ppermute | solution.py:21
